TPU v7x, 512 devices: a whole 4x8x8 slice. The times are simulated.
512 devices in a mesh: row: 16 (over z_lo, y), col: 32 (over z_hi, x, core).
Axes of the slice: x: 4, y: 8, z: 8 (z_hi: 4, z_lo: 2; z = z_hi * 2 + z_lo), core: 2. Of those that a mesh axis runs over, the one named last changes fastest.
Arguments:
- inputs: bfloat16 [2560, 6144], P('row', 'col'), may hold values from -48 to 48
- gain: bfloat16 [6144], P('col'), may hold values from 0.5 to 2
- w_in: bfloat16 [6144, 12288], P('row', 'col'), may hold values from -0.15625 to 0.15625
- w_out: bfloat16 [12288, 6144], P('col', 'row'), may hold values from -0.109375 to 0.109375
- grad_out: bfloat16 [2560, 6144], P('row', 'col'), may hold values from -6 to 6
Outputs:
- branch_out: bfloat16 [2560, 6144], P('row', 'col')
- grad_in: bfloat16 [2560, 6144], P('row', 'col')
All inputs are finite; a program needn't handle non-finite values.
Results may differ from a plain program's by a relative error of at most 0.02.
Values may be sent and summed in bfloat16 or wider, within the bound.
No kernel may reach another device: no remote copies, remote signals or barrier semaphores. Data moves between devices by JAX's collectives and lax.ppermute only.
A program may use at most 64 MiB of HBM per device.

v0:
```python
import jax
import jax.numpy as jnp
from jax import lax
from jax.sharding import PartitionSpec as P

root_half = 0.7071067811865476
inv_root_tau = 0.3989422804014327
epsilon = 1e-06


def gelu_value(preact):
    return preact * 0.5 * (1.0 + jax.scipy.special.erf(preact * root_half))


def gelu_slope(preact):
    return (
        0.5 * (1.0 + jax.scipy.special.erf(preact * root_half))
        + preact * jnp.exp(-0.5 * preact * preact) * inv_root_tau
    )


def transposed_product(left, right):
    return lax.dot_general(
        left, right, (((1,), (1,)), ((), ())), preferred_element_type=jnp.float32
    )


def on_device(inputs, gain, w_in, w_out, grad_out):
    features = inputs.shape[1] * lax.axis_size("col")
    values = inputs.astype(jnp.float32)
    row_total = lax.psum(jnp.sum(values, axis=1), "col")
    center = row_total / features
    shifted = values - center[:, None]
    spread = lax.psum(jnp.sum(shifted * shifted, axis=1), "col") / features
    inverse = lax.rsqrt(spread + epsilon)[:, None]
    standard = shifted * inverse
    gain_value = gain.astype(jnp.float32)[None, :]
    normed = (standard * gain_value).astype(jnp.bfloat16)
    gathered = lax.all_gather(normed, "col", axis=1, tiled=True)
    weight_panel = lax.all_gather(w_in, "row", axis=0, tiled=True)
    preact = jnp.dot(gathered, weight_panel, preferred_element_type=jnp.float32)
    activation = gelu_value(preact).astype(jnp.bfloat16)
    grads_all = lax.all_gather(grad_out, "col", axis=1, tiled=True)
    block_piece = lax.all_gather(w_out, "row", axis=1, tiled=True)
    partial_out = jnp.dot(activation, block_piece, preferred_element_type=jnp.float32)
    act_grad = transposed_product(grads_all, block_piece)
    partial_out, act_grad = (partial_out, act_grad)
    branch_out = lax.psum_scatter(
        partial_out.astype(jnp.bfloat16), "col", scatter_dimension=1, tiled=True
    )
    d_pre = (act_grad * gelu_slope(preact)).astype(jnp.bfloat16)
    partial_in = transposed_product(d_pre, weight_panel)
    d_normed = lax.psum_scatter(
        partial_in.astype(jnp.bfloat16), "col", scatter_dimension=1, tiled=True
    ).astype(jnp.float32)
    scaled = d_normed * gain_value
    sum_grad, sum_cross = lax.psum(
        (jnp.sum(scaled, axis=1), jnp.sum(scaled * standard, axis=1)), "col"
    )
    grad_in = inverse * (
        scaled - (sum_grad / features)[:, None] - standard * (sum_cross / features)[:, None]
    )
    return (branch_out, grad_in.astype(jnp.bfloat16))


def solution(mesh):
    in_specs = (P("row", "col"), P("col"), P("row", "col"), P("col", "row"), P("row", "col"))
    out_specs = (P("row", "col"), P("row", "col"))
    return jax.shard_map(
        on_device, mesh=mesh, in_specs=in_specs, out_specs=out_specs, check_vma=False
    )
```

profile of v0, /device:TPU:16, one launch (start us, length us, event | category | flops | bytes accessed | tf_op | source)
XLA Modules:
  0.0 742.1 jit_solution(15506074448089987860)
XLA Ops:
  7.2 0.0 all-gather.11.cloned.1.call-start
  7.2 1.0 convert_reduce_fusion
  8.2 80.5 %psum.28 = f32[160]{0:T(256)S(1)} all-reduce(f32[160]{0:T(256)S(1)} %convert_reduce_fusion), channel_id=1, replica_groups=mesh['row'=16,'col'=32] {'col'}, use_global_device_ids=true, to_apply=%region_1.0 | all-reduce | flops 160 | bytes 1280 | tf_op jit(solution)/shard_map/psum | solution.py:31
  88.7 1.1 fusion.17
  89.8 69.9 %psum.29 = f32[160]{0:T(256)S(1)} all-reduce(f32[160]{0:T(256)S(1)} %fusion.17), channel_id=1, replica_groups=mesh['row'=16,'col'=32] {'col'}, use_global_device_ids=true, to_apply=%region_3.0 | all-reduce | flops 160 | bytes 1280 | tf_op jit(solution)/shard_map/psum | solution.py:34
  159.7 0.7 convert_element_type.28
  160.3 1.6 fusion.23
  162.0 0.0 all-gather.11.cloned.1.call-update
  162.0 0.0 all-gather.13.cloned.1.call-start
  162.1 0.7 all-gather.13.cloned.1.call-update
  162.8 0.0 all-gather.7.cloned.1.call-start
  162.8 0.7 all-gather.7.cloned.1.call-update
  163.5 0.0 all-gather.9.cloned.1.call-start
  163.5 0.5 all-gather.9.cloned.1.call-update
  164.1 0.0 reduce-scatter.9.cloned.1.call-start
  164.1 54.4 %all-gather.11.cloned.1.call-done = bf16[32,192,160]{1,2,0:T(8,128)(2,1)} async-done(((bf16[1,192,160]{1,2,0:T(8,128)(2,1)}), bf16[32,192,160]{1,2,0:T(8,128)(2,1)}) %all-gather.11.cloned.1.call-update) | async-done | bytes 1966096 | tf_op jit(solution)/shard_map/all_gather | solution.py:39
  218.5 3.2 copy.9
  221.7 3.8 reshape.10
  225.5 55.1 %all-gather.13.cloned.1.call-done = bf16[32,192,160]{1,2,0:T(8,128)(2,1)} async-done(((bf16[1,192,160]{1,2,0:T(8,128)(2,1)}), bf16[32,192,160]{1,2,0:T(8,128)(2,1)}) %all-gather.13.cloned.1.call-update) | async-done | bytes 1966096 | tf_op jit(solution)/shard_map/all_gather | solution.py:43
  280.6 3.2 copy.10
  283.8 3.8 reshape.12
  287.6 0.0 copy-start
  287.6 70.3 %all-gather.7.cloned.1.call-done = bf16[6144,384]{1,0:T(8,128)(2,1)} async-done(((bf16[384,384]{1,0:T(8,128)(2,1)}), bf16[6144,384]{1,0:T(8,128)(2,1)}) %all-gather.7.cloned.1.call-update) | async-done | bytes 4718608 | tf_op jit(solution)/shard_map/all_gather | solution.py:40
  357.9 4.1 fusion.28
  362.0 75.9 %all-gather.9.cloned.1.call-done = bf16[384,6144]{1,0:T(8,128)(2,1)} async-done(((bf16[384,384]{1,0:T(8,128)(2,1)}), bf16[384,6144]{1,0:T(8,128)(2,1)}) %all-gather.9.cloned.1.call-update) | async-done | bytes 4718608 | tf_op jit(solution)/shard_map/all_gather | solution.py:44
  437.9 0.0 copy-done
  438.0 8.8 %convolution_convert_fusion = bf16[160,6144]{1,0:T(8,128)(2,1)} fusion(bf16[6144,384]{1,0:T(8,128)(2,1)} %all-gather.7.cloned.1.call-done, bf16[6144,160]{0,1:T(8,128)(2,1)S(1)} %copy-done, bf16[384,6144]{1,0:T(8,128)(2,1)} %all-gather.9.cloned.1.call-done, f32[160,384]{1,0:T(8,128)S(1)} %fusion.28), kind=kOutput, calls=%fused_computation | convolution fusion | flops 1511546880 | bytes 13615104 | tf_op jit(solution)/shard_map/dot_general | solution.py:23
  446.7 4.4 copy.13
  451.1 0.0 reduce-scatter.9.cloned.1.call-update
  451.1 0.0 reduce-scatter.7.cloned.1.call-start
  451.2 3.5 convolution_convert_fusion.1
  454.7 0.0 copy-start.1
  454.7 2.8 copy.11
  457.5 0.0 reduce-scatter.7.cloned.1.call-update
  457.5 98.0 %reduce-scatter.9.cloned.1.call-done = bf16[192,160]{1,0:T(8,128)(2,1)} async-done(((bf16[6144,160]{1,0:T(8,128)(2,1)}), bf16[192,160]{1,0:T(8,128)(2,1)}) %reduce-scatter.9.cloned.1.call-update) | async-done | bytes 61456
  555.5 1.0 copy.14
  556.5 0.0 copy-done.1
  556.5 0.2 fusion.18
  556.7 105.1 %reduce-scatter.7.cloned.1.call-done = bf16[192,160]{1,0:T(8,128)(2,1)} async-done(((bf16[6144,160]{1,0:T(8,128)(2,1)}), bf16[192,160]{1,0:T(8,128)(2,1)}) %reduce-scatter.7.cloned.1.call-update) | async-done | bytes 61456
  661.8 1.6 copy.12
  663.4 71.1 %all-reduce = (f32[160]{0:T(256)S(1)}, f32[160]{0:T(256)S(1)}) all-reduce(f32[160]{0:T(256)S(1)} %get-tuple-element.3, f32[160]{0:T(256)S(1)} %get-tuple-element.2), channel_id=1, replica_groups=mesh['row'=16,'col'=32] {'col'}, use_global_device_ids=true, to_apply=%region_9.0 | all-reduce | flops 320 | bytes 2560 | tf_op jit(solution)/shard_map/psum | solution.py:57
  734.5 0.8 fusion.16
  (3 shorter events, 0.0 us)
Async XLA Ops:
  7.2 211.3 %all-gather.11.cloned.1.call-start = ((), (), s32[]{:S(2)}) async-start(), calls=%async_computation.4 | async-start | bytes 2703360 | tf_op jit(solution)/shard_map/all_gather | solution.py:39
  162.0 118.6 %all-gather.13.cloned.1.call-start = ((), (), s32[]{:S(2)}) async-start(), calls=%async_computation.5 | async-start | bytes 2703360 | tf_op jit(solution)/shard_map/all_gather | solution.py:43
  162.8 195.1 %all-gather.7.cloned.1.call-start = ((), (), s32[]{:S(2)}) async-start(), calls=%async_computation.2 | async-start | bytes 5013504 | tf_op jit(solution)/shard_map/all_gather | solution.py:40
  163.5 274.5 %all-gather.9.cloned.1.call-start = ((), (), s32[]{:S(2)}) async-start(), calls=%async_computation.3 | async-start | bytes 5013504 | tf_op jit(solution)/shard_map/all_gather | solution.py:44
  164.1 391.4 %reduce-scatter.9.cloned.1.call-start = ((), (), s32[]{:S(2)}) async-start(), calls=%async_computation.7 | async-start | bytes 3244032
  287.6 150.4 %copy-start = (bf16[6144,160]{0,1:T(8,128)(2,1)S(1)}, bf16[6144,160]{0,1:T(8,128)(2,1)}, u32[]{:S(2)}) copy-start(bf16[6144,160]{0,1:T(8,128)(2,1)} %reshape.12) | copy-start | bytes 5898244
  451.1 210.7 %reduce-scatter.7.cloned.1.call-start = ((), (), s32[]{:S(2)}) async-start(), calls=%async_computation.6 | async-start | bytes 3244032
  454.7 101.7 %copy-start.1 = (bf16[160,192]{1,0:T(8,128)(2,1)S(1)}, bf16[160,192]{1,0:T(8,128)(2,1)}, u32[]{:S(2)}) copy-start(bf16[160,192]{1,0:T(8,128)(2,1)} %param.5) | copy-start | bytes 184324
Sparse Core Ops, SparseCore 0:
  162.1 56.3 all-gather.10
  221.6 58.9 all-gather.12
  282.7 75.1 all-gather.6
  359.8 78.0 all-gather.8
  451.3 104.1 reduce-scatter.8
  560.5 101.2 reduce-scatter.6
where the time goes:
time: 743 us; the launch traced here: 742 us
  waiting for transfers between devices  461 us (62%)
  blocking collectives  221 us (30%)
  local copies, waits for them, and re-layouts  23.8 us (3%)
  matrix products  16.4 us (2%)
  between operations  14.2 us (2%)
    unnamed x8, waiting for transfers between devices  205 us
    psum x1, blocking collectives, on_device(): row_total = lax.psum(jnp.sum(values, axis=1), 'col')  80.5 us
    all_gather x1, waiting for transfers between devices, on_device(): block_piece = lax.all_gather(w_out, 'row', axis=1, tiled=True)  75.9 us
    psum x1, blocking collectives, on_device(): lax.psum((jnp.sum(scaled, axis=1), jnp.sum(scaled * standard, axis=1)), '...  71.1 us
    all_gather x1, waiting for transfers between devices, on_device(): weight_panel = lax.all_gather(w_in, 'row', axis=0, tiled=True)  70.3 us
    psum x1, blocking collectives, on_device(): spread = lax.psum(jnp.sum(shifted * shifted, axis=1), 'col') / features  69.9 us
    all_gather x1, waiting for transfers between devices, on_device(): grads_all = lax.all_gather(grad_out, 'col', axis=1, tiled=True)  55.1 us
    all_gather x1, waiting for transfers between devices, on_device(): gathered = lax.all_gather(normed, 'col', axis=1, tiled=True)  54.4 us
  transfers between devices with their start and end apart: 6, of which 6 were waited for; matrix products, arithmetic and copies ran while one was open for 3% of the time, Pallas kernels for 0%

commit v1 on v0

v1 whole, which is shorter than its diff:
```python
import functools

import jax
import jax.numpy as jnp
from jax import lax
from jax.experimental import pallas as pl
from jax.experimental.pallas import tpu as pltpu
from jax.sharding import Mesh
from jax.sharding import PartitionSpec as P

root_half = 0.7071067811865476
inv_root_tau = 0.3989422804014327
epsilon = 1e-06
narrow = jnp.bfloat16
wide = jnp.float32
vmem_bytes = 44 * 2**20


def swap_pairs():
    pairs = []
    for l in range(2):
        for h in range(4):
            pairs.append((l * 4 + h, (h // 2) * 4 + l * 2 + h % 2))
    return pairs


def merge_kernel(core_ref, own0, own1, far0, far1, x_ref, g_ref, gain_ref, stat_ref, mean_s, spread_s):
    step = pl.program_id(0)
    rows = x_ref.shape[1] // 2
    half = x_ref.shape[2] // 2
    block = x_ref.shape[2]
    first = core_ref[0] == 0

    def sides(own, far):
        own, far = own.astype(wide), far.astype(wide)
        a = jnp.where(first, own, far)
        b = jnp.where(first, far, own)
        left = jnp.concatenate([a[:, :half], b[:, :half]], axis=1)
        right = jnp.concatenate([a[:, half:], b[:, half:]], axis=1)
        return left, right

    x0, g0 = sides(own0[0, 0, :rows], far0[0, 0, :rows])
    x1, g1 = sides(own1[0, 0, :rows], far1[0, 0, :rows])
    gain, _ = sides(own0[0, 0, rows:], far0[0, 0, rows:])
    gain_ref[0] = gain
    x_ref[0, :rows] = x0.astype(narrow)
    x_ref[0, rows:] = x1.astype(narrow)
    g_ref[0, :rows] = g0.astype(narrow)
    g_ref[0, rows:] = g1.astype(narrow)

    @pl.when(step == 0)
    def _():
        mean_s[...] = jnp.zeros_like(mean_s)
        spread_s[...] = jnp.zeros_like(spread_s)

    seen = step.astype(wide)
    for index, values in enumerate((x0, x1)):
        at = pl.ds(index * rows, rows)
        center = jnp.sum(values, axis=1, keepdims=True) * (1.0 / block)
        shifted = values - center
        spread = jnp.sum(shifted * shifted, axis=1, keepdims=True)
        gap = center - mean_s[at]
        mean_s[at] = mean_s[at] + gap / (seen + 1.0)
        spread_s[at] = spread_s[at] + spread + gap * gap * (block * seen / (seen + 1.0))

    @pl.when(step == pl.num_programs(0) - 1)
    def _():
        lane = lax.broadcasted_iota(jnp.int32, stat_ref.shape, 1)
        stat_ref[...] = jnp.where(lane < 64, mean_s[...], spread_s[...])


def first_kernel(x_ref, g_ref, gain_ref, stat_ref, panel_ref, sums_ref, pre_s, act_s, gain_s):
    step = pl.program_id(0)
    tokens = x_ref.shape[1]
    block = x_ref.shape[2]

    @pl.when(step == 0)
    def _():
        pre_s[...] = jnp.zeros_like(pre_s)
        act_s[...] = jnp.zeros_like(act_s)
        gain_s[...] = jnp.zeros_like(gain_s)

    w_in = panel_ref[0, :block]
    w_out = panel_ref[0, block:]
    gain = gain_ref[0]
    shifted = ((x_ref[0].astype(wide) - stat_ref[:, :1]) * gain[:1]).astype(narrow)
    pre_s[...] += jnp.dot(shifted, w_in, preferred_element_type=wide)
    act_s[...] += lax.dot_general(
        g_ref[0], w_out, (((1,), (1,)), ((), ())), preferred_element_type=wide
    )
    gain_s[...] += jnp.dot(gain.astype(narrow), w_in, preferred_element_type=wide)

    @pl.when(step == pl.num_programs(0) - 1)
    def _():
        sums_ref[:tokens] = pre_s[...].astype(narrow)
        sums_ref[tokens : 2 * tokens] = act_s[...].astype(narrow)
        high = gain_s[...].astype(narrow).astype(wide)
        sums_ref[2 * tokens :] = jnp.concatenate([high, gain_s[...] - high], axis=0).astype(narrow)


def second_kernel(
    features, core_ref, own_ref, far_ref, stat_ref, far_stat_ref, x_ref, gain_ref, panel_ref,
    keep_ref, send_ref, act_s, pre_s, mean_s, inv_s, flat_s, cross_s,
):
    step = pl.program_id(0)
    tokens = x_ref.shape[1]
    block = x_ref.shape[2]
    rows = tokens // 2
    half = block // 2

    @pl.when(step == 0)
    def _():
        mean_a, mean_b = stat_ref[:, :1], far_stat_ref[:, :1]
        gap = mean_a - mean_b
        mean = 0.5 * (mean_a + mean_b)
        spread = stat_ref[:, 64:65] + far_stat_ref[:, 64:65] + gap * gap * (features / 4)
        inverse = lax.rsqrt(spread / features + epsilon)

        def gain_sum(ref):
            lines = ref[2 * tokens :].astype(wide)
            return lines[:1] + lines[8:9]

        gain_a, gain_b = gain_sum(own_ref), gain_sum(far_ref)
        total = own_ref[:tokens].astype(wide) + far_ref[:tokens].astype(wide)
        total = total + (mean_a - mean) * gain_a + (mean_b - mean) * gain_b
        preact = total * inverse
        act_grad = own_ref[tokens : 2 * tokens].astype(wide) + far_ref[tokens : 2 * tokens].astype(wide)
        bulk = 0.5 * (1.0 + lax.erf(preact * root_half))
        slope = bulk + preact * jnp.exp(-0.5 * preact * preact) * inv_root_tau
        act_s[...] = (preact * bulk).astype(narrow)
        d_pre = (act_grad * slope).astype(narrow)
        pre_s[...] = d_pre
        d_pre = d_pre.astype(wide)
        mean_s[...] = mean
        inv_s[...] = inverse
        flat_s[...] = jnp.sum(d_pre * (gain_a + gain_b), axis=1, keepdims=True) / features
        cross_s[...] = jnp.sum(d_pre * preact, axis=1, keepdims=True) / features

    w_in = panel_ref[0, :block]
    w_out = panel_ref[0, block:]
    out = jnp.dot(act_s[...], w_out, preferred_element_type=wide)
    d_normed = lax.dot_general(
        pre_s[...], w_in, (((1,), (1,)), ((), ())), preferred_element_type=wide
    )
    standard = (x_ref[0].astype(wide) - mean_s[...]) * inv_s[...]
    grad = inv_s[...] * (d_normed * gain_ref[0][:1] - flat_s[...] - standard * cross_s[...])
    side0 = jnp.concatenate([out[:, :half], grad[:, :half]], axis=1)
    side1 = jnp.concatenate([out[:, half:], grad[:, half:]], axis=1)
    first = core_ref[0] == 0
    keep = jnp.where(first, side0, side1).astype(narrow)
    send = jnp.where(first, side1, side0).astype(narrow)
    for index in range(2):
        keep_ref[0, index, 0] = keep[index * rows : (index + 1) * rows]
        send_ref[0, index, 0] = send[index * rows : (index + 1) * rows]


def whole(shape):
    return pl.BlockSpec(shape, lambda j: (0,) * len(shape))


def params():
    return pltpu.CompilerParams(
        dimension_semantics=("arbitrary",), vmem_limit_bytes=vmem_bytes
    )


def on_device(inputs, gain, w_in, w_out, grad_out):
    rows, piece = inputs.shape
    block = 2 * piece
    tokens = 2 * rows
    hidden = w_in.shape[1]
    features = piece * lax.axis_size(("h", "x", "k"))
    steps = features // 2 // block
    other_core = [(0, 1), (1, 0)]
    core = lax.axis_index("k").astype(jnp.int32).reshape(1)

    panels = lax.all_gather(jnp.concatenate([w_in, w_out], axis=0), "y", axis=0)

    gain_rows = jnp.broadcast_to(jnp.concatenate([gain, gain])[None, :], (8, block))
    pack = jnp.concatenate([jnp.concatenate([inputs, grad_out], axis=1), gain_rows], axis=0)
    pack = lax.ppermute(pack, ("l", "h"), swap_pairs())
    pack = lax.all_gather(pack, "h", axis=0)
    own0 = lax.all_gather(pack[:2], "x", axis=0)
    far0 = lax.ppermute(own0, "k", other_core)
    own1 = lax.all_gather(pack[2:], "x", axis=0)
    far1 = lax.ppermute(own1, "k", other_core)

    tile = pl.BlockSpec((1, 1, rows + 8, block), lambda j: (j % 4, j // 4, 0, 0))
    step_block = pl.BlockSpec((1, tokens, block), lambda j: (j, 0, 0))
    gain_block = pl.BlockSpec((1, 8, block), lambda j: (j, 0, 0))
    panel_block = pl.BlockSpec((1,) + panels.shape[1:], lambda j: (j, 0, 0))
    scalar = pl.BlockSpec(memory_space=pltpu.SMEM)
    stat_shape = (tokens, 128)
    column = pltpu.VMEM((tokens, 1), wide)

    values, grads, gains, stats = pl.pallas_call(
        merge_kernel,
        grid=(steps,),
        in_specs=[scalar] + [tile] * 4,
        out_specs=[step_block, step_block, gain_block, whole(stat_shape)],
        out_shape=[
            jax.ShapeDtypeStruct((steps, tokens, block), narrow),
            jax.ShapeDtypeStruct((steps, tokens, block), narrow),
            jax.ShapeDtypeStruct((steps, 8, block), wide),
            jax.ShapeDtypeStruct(stat_shape, wide),
        ],
        scratch_shapes=[column, column],
        compiler_params=params(),
        name="merge",
    )(core, own0, own1, far0, far1)

    sums_shape = (2 * tokens + 16, hidden)
    sums = pl.pallas_call(
        first_kernel,
        grid=(steps,),
        in_specs=[step_block, step_block, gain_block, whole(stat_shape), panel_block],
        out_specs=whole(sums_shape),
        out_shape=jax.ShapeDtypeStruct(sums_shape, narrow),
        scratch_shapes=[
            pltpu.VMEM((tokens, hidden), wide),
            pltpu.VMEM((tokens, hidden), wide),
            pltpu.VMEM((8, hidden), wide),
        ],
        compiler_params=params(),
        name="first",
    )(values, grads, gains, stats, panels)

    far_stats = lax.ppermute(stats, "l", other_core)
    far_sums = lax.ppermute(sums, "l", other_core)

    part_shape = (4, 2, 2, rows, block)
    part_block = pl.BlockSpec((1, 2, 1, rows, block), lambda j: (j % 4, 0, j // 4, 0, 0))
    part = jax.ShapeDtypeStruct(part_shape, narrow)
    keep, send = pl.pallas_call(
        functools.partial(second_kernel, features),
        grid=(steps,),
        in_specs=[
            scalar, whole(sums_shape), whole(sums_shape), whole(stat_shape), whole(stat_shape),
            step_block, gain_block, panel_block,
        ],
        out_specs=[part_block, part_block],
        out_shape=[part, part],
        scratch_shapes=[
            pltpu.VMEM((tokens, hidden), narrow),
            pltpu.VMEM((tokens, hidden), narrow),
            column, column, column, column,
        ],
        compiler_params=params(),
        name="second",
    )(core, sums, far_sums, stats, far_stats, values, gains, panels)

    got = lax.ppermute(send, "k", other_core)
    total = (keep.astype(wide) + got.astype(wide)).astype(narrow)
    total = lax.all_to_all(total, "x", 0, 0)
    total = jnp.sum(total.astype(wide), axis=0).astype(narrow).reshape(4, rows, block)
    total = lax.all_to_all(total, "h", 0, 0)
    total = jnp.sum(total.astype(wide), axis=0).astype(narrow)
    total = lax.ppermute(total, ("l", "h"), swap_pairs())
    return (total[:, :piece], total[:, piece:])


def solution(mesh):
    fine = Mesh(mesh.devices.reshape(2, 8, 4, 4, 2), ("l", "y", "h", "x", "k"))
    row, col = ("l", "y"), ("h", "x", "k")
    in_specs = (P(row, col), P(col), P(row, col), P(col, row), P(row, col))
    out_specs = (P(row, col), P(row, col))
    return jax.shard_map(
        on_device, mesh=fine, in_specs=in_specs, out_specs=out_specs, check_vma=False
    )
```

time: 743 us -> 197 us (0.27)
  the two profiles are of different devices: /device:TPU:16 before, /device:TPU:80 now
where the time goes in v1:
time: 197 us; the launch traced here: 196 us
  blocking collectives  93.1 us (47%)
  waiting for transfers between devices  30.7 us (16%)
  starting transfers between devices  25.1 us (13%)
  Pallas kernels  19.6 us (10%)
  between operations  14.2 us (7%)
  local copies, waits for them, and re-layouts  8.2 us (4%)
  other arithmetic  4.96 us (3%)
    all_to_all x1, blocking collectives, on_device(): total = lax.all_to_all(total, 'x', 0, 0)  29.2 us
    all_to_all x1, blocking collectives, on_device(): total = lax.all_to_all(total, 'h', 0, 0)  17.5 us
    all_gather x1, blocking collectives, on_device(): own0 = lax.all_gather(pack[:2], 'x', axis=0)  15.5 us
    all_gather x1, blocking collectives, on_device(): own1 = lax.all_gather(pack[2:], 'x', axis=0)  15.4 us
    all_gather x1, blocking collectives, on_device(): pack = lax.all_gather(pack, 'h', axis=0)  15.4 us
    ppermute x1, waiting for transfers between devices, on_device(): far_stats = lax.ppermute(stats, 'l', other_core)  13.4 us
    ppermute x1, starting transfers between devices, on_device(): pack = lax.ppermute(pack, ('l', 'h'), swap_pairs())  9.11 us
    pallas_call x1, Pallas kernels, on_device(): pl.pallas_call(functools.partial(second_kernel, features), grid=(steps,),...  8.7 us
  transfers between devices with their start and end apart: 8, of which 5 were waited for; matrix products, arithmetic and copies ran while one was open for 1% of the time, Pallas kernels for 3%

profile of v1, /device:TPU:80, one launch (start us, length us, event | category | flops | bytes accessed | tf_op | source)
XLA Modules:
  0.0 195.8 jit_solution(16210882693945253519)
XLA Ops:
  7.2 0.0 all-gather.6.cloned.1.call-start
  7.2 2.0 %pad_maximum_fusion = bf16[768,384]{1,0:T(8,128)(2,1)} fusion(bf16[384,384]{1,0:T(8,128)(2,1)} %param.8, bf16[384,384]{1,0:T(8,128)(2,1)} %param.7), kind=kLoop, calls=%fused_computation.1 | loop fusion | flops 1179648 | bytes 1179648 | tf_op jit(solution)/shard_map/concatenate | solution.py:177
  9.2 0.0 all-gather.6.cloned.1.call-update
  9.2 0.8 pad_maximum_fusion.2
  10.0 1.0 pad_maximum_fusion.1
  11.0 9.1 %collective-permute-start = (bf16[168,384]{1,0:T(8,128)(2,1)S(1)}, bf16[168,384]{1,0:T(8,128)(2,1)S(1)}, u32[]{:S(2)}, u32[]{:S(2)}) collective-permute-start(bf16[168,384]{1,0:T(8,128)(2,1)S(1)} %pad_maximum_fusion.1), channel_id=1, source_target_pairs={{0,0},{8,8},{16,256},{24,264},{256,16},{264,24},{272,272},{280,280... | collective-permute-start | bytes 387080 | tf_op jit(solution)/shard_map/ppermute | solution.py:181
  20.2 6.2 %collective-permute-done = bf16[168,384]{1,0:T(8,128)(2,1)S(1)} collective-permute-done((bf16[168,384]{1,0:T(8,128)(2,1)S(1)}, bf16[168,384]{1,0:T(8,128)(2,1)S(1)}, u32[]{:S(2)}, u32[]{:S(2)}) %collective-permute-start) | collective-permute-done | bytes 129056 | tf_op jit(solution)/shard_map/ppermute | solution.py:181
  26.4 15.4 %all-gather = bf16[672,384]{1,0:T(8,128)(2,1)S(1)} all-gather(bf16[168,384]{1,0:T(8,128)(2,1)S(1)} %collective-permute-done), channel_id=2, replica_groups=mesh['l'=2,'y'=8,'h'=4,'x'=4,'k'=2] {'h'}, dimensions={0}, use_global_device_ids=true | all-gather | bytes 645120 | tf_op jit(solution)/shard_map/all_gather | solution.py:182
  41.8 0.1 fusion
  41.8 15.5 %all-gather.1 = bf16[8,168,384]{2,1,0:T(8,128)(2,1)S(1)} all-gather(bf16[2,168,384]{2,1,0:T(8,128)(2,1)S(1)} %bitcast.15), channel_id=3, replica_groups=mesh['l'=2,'y'=8,'h'=4,'x'=4,'k'=2] {'x'}, dimensions={0}, use_global_device_ids=true | all-gather | bytes 1290240 | tf_op jit(solution)/shard_map/all_gather | solution.py:183
  57.4 1.9 collective-permute-start.1
  59.3 15.4 %all-gather.2 = bf16[8,168,384]{2,1,0:T(8,128)(2,1)S(1)} all-gather(bf16[2,168,384]{2,1,0:T(8,128)(2,1)S(1)} %bitcast.14), channel_id=4, replica_groups=mesh['l'=2,'y'=8,'h'=4,'x'=4,'k'=2] {'x'}, dimensions={0}, use_global_device_ids=true | all-gather | bytes 1290240 | tf_op jit(solution)/shard_map/all_gather | solution.py:185
  74.7 1.9 collective-permute-start.2
  76.7 0.0 copy-start.1
  76.7 1.0 copy-done.1
  77.6 0.0 collective-permute-done.1.far0
  77.6 1.7 collective-permute-done.2.far1
  79.4 0.0 copy-start.2
  79.4 1.2 copy-done.2
  80.6 6.4 %merge.1 = (bf16[8,320,384]{2,1,0:T(8,128)(2,1)S(1)}, bf16[8,320,384]{2,1,0:T(8,128)(2,1)S(1)}, f32[8,8,384]{2,1,0:T(8,128)S(1)}, f32[320,128]{1,0:T(8,128)S(1)}) custom-call(s32[1]{0:T(128)} %bitcast.core_ref, bf16[4,2,168,384]{3,2,1,0:T(8,128)(2,1)S(1)} %bitcast.10, bf16[4,2,168,384]{3,2,1,0:T(8,128)(2,1)S(1)} %bitcast.12, ...), custom_call_target="tpu_custom_call" | custom-call | tf_op jit(solution)/shard_map/merge/pallas_call | solution.py:196
  87.0 0.0 copy-start.3
  87.0 1.3 copy-done.3
  88.3 0.0 all-gather.6.cloned.1.call-done
  88.3 0.0 copy-start
  88.3 2.3 %copy-done = bf16[6144,384]{1,0:T(8,128)(2,1)S(1)} copy-done((bf16[6144,384]{1,0:T(8,128)(2,1)S(1)}, bf16[6144,384]{1,0:T(8,128)(2,1)}, u32[]{:S(2)}) %copy-start) | copy-done | bytes 4718616
  90.7 0.0 copy-start.4
  90.7 1.5 copy-done.4
  92.2 4.6 %first.1.own_ref = bf16[656,384]{1,0:T(8,128)(2,1)S(1)} custom-call(bf16[8,320,384]{2,1,0:T(8,128)(2,1)S(1)} %get-tuple-element.8.x_ref, bf16[8,320,384]{2,1,0:T(8,128)(2,1)S(1)} %copy-done.4, f32[8,8,384]{2,1,0:T(8,128)S(1)} %get-tuple-element.10.gain_ref, f32[320,128]{1,0:T(8,128)S(1)} %get-tuple-element.11.stat_ref, bf16[8,768,384]{2,1,0:T(8,128)(2,1)S(1)} %bitcast.8), custom_call_target="tpu_custom_call" | custom-call | tf_op jit(solution)/shard_map/first/pallas_call | solution.py:213
  96.8 4.0 %collective-permute-start.3 = (bf16[656,384]{1,0:T(8,128)(2,1)S(1)}, bf16[656,384]{1,0:T(8,128)(2,1)S(1)}, u32[]{:S(2)}, u32[]{:S(2)}) collective-permute-start(bf16[656,384]{1,0:T(8,128)(2,1)S(1)} %first.1.own_ref), channel_id=1, source_target_pairs={{0,256},{256,0},{1,257},{257,1},{2,258},{258,2},{3,259},{259,3},{4... | collective-permute-start | bytes 1511432 | tf_op jit(solution)/shard_map/ppermute | solution.py:229
  100.8 1.9 collective-permute-start.4
  102.7 13.4 %collective-permute-done.4.far_stat_ref = f32[320,128]{1,0:T(8,128)S(1)} collective-permute-done((f32[320,128]{1,0:T(8,128)S(1)}, f32[320,128]{1,0:T(8,128)S(1)}, u32[]{:S(2)}, u32[]{:S(2)}) %collective-permute-start.4) | collective-permute-done | bytes 163872 | tf_op jit(solution)/shard_map/ppermute | solution.py:228
  116.1 0.0 collective-permute-done.3.far_ref
  116.1 8.7 %second.1 = (bf16[4,2,2,160,384]{4,3,2,1,0:T(8,128)(2,1)S(1)}, bf16[4,2,2,160,384]{4,3,2,1,0:T(8,128)(2,1)S(1)}) custom-call(s32[1]{0:T(128)} %bitcast.core_ref, bf16[656,384]{1,0:T(8,128)(2,1)S(1)} %first.1.own_ref, bf16[656,384]{1,0:T(8,128)(2,1)S(1)} %collective-permute-done.3.far_ref, f32[320,128]{1,0:T(8,128)S(1)} %get-tuple-element.11.stat_ref, ...), custom_call_target="tpu_custom_call" | custom-call | tf_op jit(solution)/shard_map/second/pallas_call | solution.py:234
  124.8 1.9 collective-permute-start.5
  126.7 3.9 %collective-permute-done.5 = bf16[4,2,2,160,384]{4,3,2,1,0:T(8,128)(2,1)S(1)} collective-permute-done((bf16[4,2,2,160,384]{4,3,2,1,0:T(8,128)(2,1)S(1)}, bf16[4,2,2,160,384]{4,3,2,1,0:T(8,128)(2,1)S(1)}, u32[]{:S(2)}, u32[]{:S(2)}) %collective-permute-start.5) | collective-permute-done | bytes 1966112 | tf_op jit(solution)/shard_map/ppermute | solution.py:252
  130.6 0.5 add_convert_fusion
  131.2 29.2 %all_to_all.10 = bf16[4,2,2,160,384]{4,3,2,1,0:T(8,128)(2,1)S(1)} all-to-all(bf16[4,2,2,160,384]{4,3,2,1,0:T(8,128)(2,1)S(1)} %add_convert_fusion), channel_id=1, replica_groups=mesh['l'=2,'y'=8,'h'=4,'x'=4,'k'=2] {'x'}, dimensions={0} | all-to-all | bytes 3932160 | tf_op jit(solution)/shard_map/all_to_all | solution.py:254
  160.4 0.5 reduce_sum.24
  160.9 17.5 %all_to_all.11 = bf16[4,160,384]{2,1,0:T(8,128)(2,1)S(1)} all-to-all(bf16[4,160,384]{2,1,0:T(8,128)(2,1)S(1)} %bitcast.13), channel_id=1, replica_groups=mesh['l'=2,'y'=8,'h'=4,'x'=4,'k'=2] {'h'}, dimensions={0} | all-to-all | bytes 983040 | tf_op jit(solution)/shard_map/all_to_all | solution.py:256
  178.4 0.1 reduce_sum.25
  178.5 4.4 %collective-permute-start.6 = (bf16[160,384]{1,0:T(8,128)(2,1)S(1)}, bf16[160,384]{1,0:T(8,128)(2,1)S(1)}, u32[]{:S(2)}, u32[]{:S(2)}) collective-permute-start(bf16[160,384]{1,0:T(8,128)(2,1)S(1)} %reduce_sum.25), channel_id=1, source_target_pairs={{0,0},{8,8},{16,256},{24,264},{256,16},{264,24},{272,272},{280,280... | collective-permute-start | bytes 368648 | tf_op jit(solution)/shard_map/ppermute | solution.py:258
  182.8 5.4 %collective-permute-done.6 = bf16[160,384]{1,0:T(8,128)(2,1)S(1)} collective-permute-done((bf16[160,384]{1,0:T(8,128)(2,1)S(1)}, bf16[160,384]{1,0:T(8,128)(2,1)S(1)}, u32[]{:S(2)}, u32[]{:S(2)}) %collective-permute-start.6) | collective-permute-done | bytes 122912 | tf_op jit(solution)/shard_map/ppermute | solution.py:258
  188.3 0.7 fusion.1
  (1 shorter events, 0.0 us)
Async XLA Ops:
  7.2 81.2 %all-gather.6.cloned.1.call-start = ((), (), s32[]{:S(2)}) async-start(), calls=%async_computation.2 | async-start | bytes 5308416 | tf_op jit(solution)/shard_map/all_gather | solution.py:177
  11.0 15.3 %collective-permute-start = (bf16[168,384]{1,0:T(8,128)(2,1)S(1)}, bf16[168,384]{1,0:T(8,128)(2,1)S(1)}, u32[]{:S(2)}, u32[]{:S(2)}) collective-permute-start(bf16[168,384]{1,0:T(8,128)(2,1)S(1)} %pad_maximum_fusion.1), channel_id=1, source_target_pairs={{0,0},{8,8},{16,256},{24,264},{256,16},{264,24},{272,272},{280,280... | collective-permute-start | bytes 387080 | tf_op jit(solution)/shard_map/ppermute | solution.py:181
  57.4 20.3 %collective-permute-start.1 = (bf16[4,2,168,384]{3,2,1,0:T(8,128)(2,1)S(1)}, bf16[4,2,168,384]{3,2,1,0:T(8,128)(2,1)}, u32[]{:S(2)}, u32[]{:S(2)}) collective-permute-start(bf16[4,2,168,384]{3,2,1,0:T(8,128)(2,1)S(1)} %bitcast.9), channel_id=1, source_target_pairs={{0,1},{1,0},{2,3},{3,2},{4,5},{5,4},{6,7},{7,6},{8,9},{9,8},{10,11... | collective-permute-start | bytes 3096584 | tf_op jit(solution)/shard_map/ppermute | solution.py:184
  74.7 4.7 %collective-permute-start.2 = (bf16[4,2,168,384]{3,2,1,0:T(8,128)(2,1)S(1)}, bf16[4,2,168,384]{3,2,1,0:T(8,128)(2,1)}, u32[]{:S(2)}, u32[]{:S(2)}) collective-permute-start(bf16[4,2,168,384]{3,2,1,0:T(8,128)(2,1)S(1)} %bitcast.11), channel_id=1, source_target_pairs={{0,1},{1,0},{2,3},{3,2},{4,5},{5,4},{6,7},{7,6},{8,9},{9,8},{10,11... | collective-permute-start | bytes 3096584 | tf_op jit(solution)/shard_map/ppermute | solution.py:186
  76.7 1.0 copy-start.1
  79.4 1.2 copy-start.2
  87.0 1.3 copy-start.3
  88.3 2.3 %copy-start = (bf16[6144,384]{1,0:T(8,128)(2,1)S(1)}, bf16[6144,384]{1,0:T(8,128)(2,1)}, u32[]{:S(2)}) copy-start(bf16[6144,384]{1,0:T(8,128)(2,1)} %all-gather.6.cloned.1.call-done) | copy-start | bytes 14155780
  90.7 1.5 copy-start.4
  96.8 19.3 %collective-permute-start.3 = (bf16[656,384]{1,0:T(8,128)(2,1)S(1)}, bf16[656,384]{1,0:T(8,128)(2,1)S(1)}, u32[]{:S(2)}, u32[]{:S(2)}) collective-permute-start(bf16[656,384]{1,0:T(8,128)(2,1)S(1)} %first.1.own_ref), channel_id=1, source_target_pairs={{0,256},{256,0},{1,257},{257,1},{2,258},{258,2},{3,259},{259,3},{4... | collective-permute-start | bytes 1511432 | tf_op jit(solution)/shard_map/ppermute | solution.py:229
  100.8 15.3 %collective-permute-start.4 = (f32[320,128]{1,0:T(8,128)S(1)}, f32[320,128]{1,0:T(8,128)S(1)}, u32[]{:S(2)}, u32[]{:S(2)}) collective-permute-start(f32[320,128]{1,0:T(8,128)S(1)} %get-tuple-element.11.stat_ref), channel_id=1, source_target_pairs={{0,256},{256,0},{1,257},{257,1},{2,258},{258,2},{3,259},{259,3},{4... | collective-permute-start | bytes 491528 | tf_op jit(solution)/shard_map/ppermute | solution.py:228
  124.8 5.9 %collective-permute-start.5 = (bf16[4,2,2,160,384]{4,3,2,1,0:T(8,128)(2,1)S(1)}, bf16[4,2,2,160,384]{4,3,2,1,0:T(8,128)(2,1)S(1)}, u32[]{:S(2)}, u32[]{:S(2)}) collective-permute-start(bf16[4,2,2,160,384]{4,3,2,1,0:T(8,128)(2,1)S(1)} %get-tuple-element.13), channel_id=1, source_target_pairs={{0,1},{1,0},{2,3},{3,2},{4,5},{5,4},{6,7},{7,6},{8,9},{9,8},{10,11... | collective-permute-start | bytes 5898248 | tf_op jit(solution)/shard_map/ppermute | solution.py:252
  178.5 9.8 %collective-permute-start.6 = (bf16[160,384]{1,0:T(8,128)(2,1)S(1)}, bf16[160,384]{1,0:T(8,128)(2,1)S(1)}, u32[]{:S(2)}, u32[]{:S(2)}) collective-permute-start(bf16[160,384]{1,0:T(8,128)(2,1)S(1)} %reduce_sum.25), channel_id=1, source_target_pairs={{0,0},{8,8},{16,256},{24,264},{256,16},{264,24},{272,272},{280,280... | collective-permute-start | bytes 368648 | tf_op jit(solution)/shard_map/ppermute | solution.py:258
Sparse Core Ops, SparseCore 0:
  10.1 64.4 all-gather.5

commit v2 on v1

v2 whole, which is shorter than its diff:
```python
import functools

import jax
import jax.numpy as jnp
from jax import lax
from jax.experimental import pallas as pl
from jax.experimental.pallas import tpu as pltpu
from jax.sharding import Mesh
from jax.sharding import PartitionSpec as P

root_half = 0.7071067811865476
inv_root_tau = 0.3989422804014327
epsilon = 1e-06
narrow = jnp.bfloat16
wide = jnp.float32


def pairs_of(target):
    pairs = []
    for l in range(2):
        for h in range(4):
            new_l, new_high, new_low = target(l, h // 2, h % 2)
            pairs.append((l * 4 + h, new_l * 4 + new_high * 2 + new_low))
    return pairs


def gather_pairs(i, j):
    return pairs_of(lambda l, high, low: (high, l ^ i, low ^ j))


def scatter_pairs(i, j):
    return pairs_of(lambda l, high, low: (high ^ i, l, low ^ j))


def split3(value):
    high = value.astype(narrow).astype(wide)
    middle = (value - high).astype(narrow).astype(wide)
    return high, middle, value - high - middle


def ones_diagonal(rows, columns):
    row = lax.broadcasted_iota(jnp.int32, (rows, columns), 0)
    column = lax.broadcasted_iota(jnp.int32, (rows, columns), 1)
    return jnp.where(row == column, 1.0, 0.0).astype(narrow)


def merge_kernel(place_ref, own0, own1, far0, far1, x_ref, g_ref, gain_ref, stat_ref, mean_s, spread_s):
    step = pl.program_id(0)
    rows = x_ref.shape[1] // 2
    half = x_ref.shape[2] // 2
    block = x_ref.shape[2]
    first = place_ref[0] == 0

    def sides(own, far):
        own, far = own.astype(wide), far.astype(wide)
        a = jnp.where(first, own, far)
        b = jnp.where(first, far, own)
        left = jnp.concatenate([a[:, :half], b[:, :half]], axis=1)
        right = jnp.concatenate([a[:, half:], b[:, half:]], axis=1)
        return left, right

    x0, g0 = sides(own0[0, 0, :rows], far0[0, 0, :rows])
    x1, g1 = sides(own1[0, 0, :rows], far1[0, 0, :rows])
    gain, _ = sides(own0[0, 0, rows:], far0[0, 0, rows:])
    gain_ref[0] = gain
    x_ref[0, :rows] = x0.astype(narrow)
    x_ref[0, rows:] = x1.astype(narrow)
    g_ref[0, :rows] = g0.astype(narrow)
    g_ref[0, rows:] = g1.astype(narrow)

    @pl.when(step == 0)
    def _():
        mean_s[...] = jnp.zeros_like(mean_s)
        spread_s[...] = jnp.zeros_like(spread_s)

    seen = step.astype(wide)
    for index, values in enumerate((x0, x1)):
        at = pl.ds(index * rows, rows)
        center = jnp.sum(values, axis=1, keepdims=True) * (1.0 / block)
        shifted = values - center
        spread = jnp.sum(shifted * shifted, axis=1, keepdims=True)
        gap = center - mean_s[at]
        mean_s[at] = mean_s[at] + gap / (seen + 1.0)
        spread_s[at] = spread_s[at] + spread + gap * gap * (block * seen / (seen + 1.0))

    @pl.when(step == pl.num_programs(0) - 1)
    def _():
        lane = lax.broadcasted_iota(jnp.int32, stat_ref.shape, 1)
        stat_ref[...] = jnp.where(lane < 64, mean_s[...], spread_s[...])


def first_kernel(place_ref, x_ref, g_ref, gain_ref, stat_ref, panel_ref, sums_ref, pre_s, act_s, gain_s, table_s):
    step = pl.program_id(0)
    tokens = x_ref.shape[1]
    block = x_ref.shape[2]

    @pl.when(step == 0)
    def _():
        pre_s[...] = jnp.zeros_like(pre_s)
        act_s[...] = jnp.zeros_like(act_s)
        gain_s[...] = jnp.zeros_like(gain_s)

    w_in = panel_ref[0, :block]
    w_out = panel_ref[0, block:]
    gain = gain_ref[0]
    shifted = ((x_ref[0].astype(wide) - stat_ref[:, :1]) * gain[:1]).astype(narrow)
    pre_s[...] += jnp.dot(shifted, w_in, preferred_element_type=wide)
    act_s[...] += lax.dot_general(
        g_ref[0], w_out, (((1,), (1,)), ((), ())), preferred_element_type=wide
    )
    gain_s[...] += jnp.dot(gain.astype(narrow), w_in, preferred_element_type=wide)

    @pl.when(step == pl.num_programs(0) - 1)
    def _():
        sums_ref[:tokens] = pre_s[...].astype(narrow)
        sums_ref[tokens : 2 * tokens] = act_s[...].astype(narrow)
        columns = split3(stat_ref[:, :1]) + split3(stat_ref[:, 64:65])
        lane = lax.broadcasted_iota(jnp.int32, (tokens, 128), 1)
        table = jnp.zeros((tokens, 128), wide)
        for index, column in enumerate(columns):
            table = jnp.where(lane == index, column, table)
        table_s[...] = jnp.zeros_like(table_s)
        table_s[:tokens] = table.astype(narrow)
        lines = lax.dot_general(
            ones_diagonal(16, 128), table_s[...], (((1,), (1,)), ((), ())), preferred_element_type=wide
        )
        high = gain_s[:1].astype(narrow).astype(wide)
        row = lax.broadcasted_iota(jnp.int32, lines.shape, 0)
        lines = jnp.where(row == 6, high, jnp.where(row == 7, gain_s[:1] - high, lines))
        sums_ref[2 * tokens :] = lines.astype(narrow)


def second_kernel(
    features, place_ref, own_ref, far_ref, x_ref, gain_ref, panel_ref,
    keep_ref, send_ref, act_s, pre_s, mean_s, inv_s, flat_s, cross_s,
):
    step = pl.program_id(0)
    tokens = x_ref.shape[1]
    block = x_ref.shape[2]
    rows = tokens // 2
    half = block // 2

    @pl.when(step == 0)
    def _():
        def extras(ref):
            lines = ref[2 * tokens :]
            table = lax.dot_general(
                lines, ones_diagonal(16, 128), (((0,), (0,)), ((), ())), preferred_element_type=wide
            )[:tokens]
            center = table[:, 0:1] + table[:, 1:2] + table[:, 2:3]
            spread = table[:, 3:4] + table[:, 4:5] + table[:, 5:6]
            lines = lines.astype(wide)
            return center, spread, lines[6:7] + lines[7:8]

        mean_a, spread_a, gain_a = extras(own_ref)
        mean_b, spread_b, gain_b = extras(far_ref)
        gap = mean_a - mean_b
        mean = 0.5 * (mean_a + mean_b)
        spread = spread_a + spread_b + gap * gap * (features / 4)
        inverse = lax.rsqrt(spread / features + epsilon)

        total = own_ref[:tokens].astype(wide) + far_ref[:tokens].astype(wide)
        total = total + (mean_a - mean) * gain_a + (mean_b - mean) * gain_b
        preact = total * inverse
        act_grad = own_ref[tokens : 2 * tokens].astype(wide) + far_ref[tokens : 2 * tokens].astype(wide)
        bulk = 0.5 * (1.0 + lax.erf(preact * root_half))
        slope = bulk + preact * jnp.exp(-0.5 * preact * preact) * inv_root_tau
        act_s[...] = (preact * bulk).astype(narrow)
        d_pre = (act_grad * slope).astype(narrow)
        pre_s[...] = d_pre
        d_pre = d_pre.astype(wide)
        mean_s[...] = mean
        inv_s[...] = inverse
        flat_s[...] = jnp.sum(d_pre * (gain_a + gain_b), axis=1, keepdims=True) / features
        cross_s[...] = jnp.sum(d_pre * preact, axis=1, keepdims=True) / features

    w_in = panel_ref[0, :block]
    w_out = panel_ref[0, block:]
    out = jnp.dot(act_s[...], w_out, preferred_element_type=wide)
    d_normed = lax.dot_general(
        pre_s[...], w_in, (((1,), (1,)), ((), ())), preferred_element_type=wide
    )
    standard = (x_ref[0].astype(wide) - mean_s[...]) * inv_s[...]
    grad = inv_s[...] * (d_normed * gain_ref[0][:1] - flat_s[...] - standard * cross_s[...])
    out, grad = out.astype(narrow), grad.astype(narrow)
    side0 = jnp.concatenate([out[:, :half], grad[:, :half]], axis=1)
    side1 = jnp.concatenate([out[:, half:], grad[:, half:]], axis=1)
    first = place_ref[0] == 0
    keep = jnp.where(first, side0, side1)
    send = jnp.where(first, side1, side0)
    for index in range(2):
        keep_ref[0, index, 0] = keep[index * rows : (index + 1) * rows]
        send_ref[0, index, 0] = send[index * rows : (index + 1) * rows]


def whole(shape):
    return pl.BlockSpec(shape, lambda j, place: (0,) * len(shape))


def call(kernel, steps, in_specs, out_specs, out_shape, scratch_shapes, vmem, name):
    return pl.pallas_call(
        kernel,
        grid_spec=pltpu.PrefetchScalarGridSpec(
            num_scalar_prefetch=1,
            grid=(steps,),
            in_specs=in_specs,
            out_specs=out_specs,
            scratch_shapes=scratch_shapes,
        ),
        out_shape=out_shape,
        compiler_params=pltpu.CompilerParams(
            dimension_semantics=("arbitrary",), vmem_limit_bytes=vmem * 2**20
        ),
        name=name,
    )


def on_device(inputs, gain, w_in, w_out, grad_out):
    rows, piece = inputs.shape
    block = 2 * piece
    tokens = 2 * rows
    hidden = w_in.shape[1]
    features = piece * lax.axis_size(("h", "x", "k"))
    steps = features // 2 // block
    other_core = [(0, 1), (1, 0)]
    place = jnp.stack([lax.axis_index("k"), lax.axis_index("h") % 2]).astype(jnp.int32)

    panels = lax.all_gather(jnp.concatenate([w_in, w_out], axis=0), "y", axis=0)

    gain_rows = jnp.broadcast_to(jnp.concatenate([gain, gain])[None, :], (8, block))
    pack = jnp.concatenate([jnp.concatenate([inputs, grad_out], axis=1), gain_rows], axis=0)
    near = [
        [lax.ppermute(pack, ("l", "h"), gather_pairs(i, j)) for j in range(2)] for i in range(2)
    ]
    own0 = lax.all_gather(jnp.stack(near[0]), "x", axis=0)
    far0 = lax.ppermute(own0, "k", other_core)
    own1 = lax.all_gather(jnp.stack(near[1]), "x", axis=0)
    far1 = lax.ppermute(own1, "k", other_core)

    tile = pl.BlockSpec((1, 1, rows + 8, block), lambda j, place: (j % 4, j // 4, 0, 0))
    step_block = pl.BlockSpec((1, tokens, block), lambda j, place: (j, 0, 0))
    gain_block = pl.BlockSpec((1, 8, block), lambda j, place: (j, 0, 0))
    panel_block = pl.BlockSpec(
        (1,) + panels.shape[1:], lambda j, place: (((j // 4) ^ place[1]) * 4 + j % 4, 0, 0)
    )
    stat_shape = (tokens, 128)
    column = pltpu.VMEM((tokens, 1), wide)

    values, grads, gains, stats = call(
        merge_kernel,
        steps,
        [tile] * 4,
        [step_block, step_block, gain_block, whole(stat_shape)],
        [
            jax.ShapeDtypeStruct((steps, tokens, block), narrow),
            jax.ShapeDtypeStruct((steps, tokens, block), narrow),
            jax.ShapeDtypeStruct((steps, 8, block), wide),
            jax.ShapeDtypeStruct(stat_shape, wide),
        ],
        [column, column],
        8,
        "merge",
    )(place, own0, own1, far0, far1)

    sums_shape = (2 * tokens + 16, hidden)
    sums = call(
        first_kernel,
        steps,
        [step_block, step_block, gain_block, whole(stat_shape), panel_block],
        whole(sums_shape),
        jax.ShapeDtypeStruct(sums_shape, narrow),
        [
            pltpu.VMEM((tokens, hidden), wide),
            pltpu.VMEM((tokens, hidden), wide),
            pltpu.VMEM((8, hidden), wide),
            pltpu.VMEM((hidden, 128), narrow),
        ],
        12,
        "first",
    )(place, values, grads, gains, stats, panels)

    far_sums = lax.ppermute(sums, "l", other_core)

    part_shape = (4, 2, 2, rows, block)
    part_block = pl.BlockSpec((1, 2, 1, rows, block), lambda j, place: (j % 4, 0, j // 4, 0, 0))
    part = jax.ShapeDtypeStruct(part_shape, narrow)
    keep, send = call(
        functools.partial(second_kernel, features),
        steps,
        [whole(sums_shape), whole(sums_shape), step_block, gain_block, panel_block],
        [part_block, part_block],
        [part, part],
        [
            pltpu.VMEM((tokens, hidden), narrow),
            pltpu.VMEM((tokens, hidden), narrow),
            column, column, column, column,
        ],
        14,
        "second",
    )(place, sums, far_sums, values, gains, panels)

    got = lax.ppermute(send, "k", other_core)
    total = (keep.astype(wide) + got.astype(wide)).astype(narrow)
    total = lax.all_to_all(total, "x", 0, 0)
    total = jnp.sum(total.astype(wide), axis=0).astype(narrow)
    shares = [
        lax.ppermute(total[i, j], ("l", "h"), scatter_pairs(i, j)).astype(wide)
        for i in range(2)
        for j in range(2)
    ]
    total = (shares[0] + shares[1] + shares[2] + shares[3]).astype(narrow)
    return (total[:, :piece], total[:, piece:])


def solution(mesh):
    fine = Mesh(mesh.devices.reshape(2, 8, 4, 4, 2), ("l", "y", "h", "x", "k"))
    row, col = ("l", "y"), ("h", "x", "k")
    in_specs = (P(row, col), P(col), P(row, col), P(col, row), P(row, col))
    out_specs = (P(row, col), P(row, col))
    return jax.shard_map(
        on_device, mesh=fine, in_specs=in_specs, out_specs=out_specs, check_vma=False
    )
```

time: 197 us -> 177 us (0.90)
  the two profiles are of different devices: /device:TPU:80 before, /device:TPU:96 now
where the time goes in v2:
time: 177 us; the launch traced here: 176 us
  blocking collectives  59.6 us (34%)
  starting transfers between devices  44.9 us (25%)
  waiting for transfers between devices  24.5 us (14%)
  Pallas kernels  19.8 us (11%)
  between operations  14.3 us (8%)
  local copies, waits for them, and re-layouts  8.19 us (5%)
  other arithmetic  5.09 us (3%)
    all_to_all x1, blocking collectives, on_device(): total = lax.all_to_all(total, 'x', 0, 0)  29.2 us
    ppermute x4, starting transfers between devices, on_device(): lax.ppermute(pack, ('l', 'h'), gather_pairs(i, j))  22.2 us
    all_gather x1, blocking collectives, on_device(): own0 = lax.all_gather(jnp.stack(near[0]), 'x', axis=0)  15.9 us
    ppermute x4, starting transfers between devices, on_device(): lax.ppermute(total[i, j], ('l', 'h'), scatter_pairs(i, j)).astype(wide)  15 us
    all_gather x1, blocking collectives, on_device(): own1 = lax.all_gather(jnp.stack(near[1]), 'x', axis=0)  14.5 us
    ppermute x1, waiting for transfers between devices, on_device(): far_sums = lax.ppermute(sums, 'l', other_core)  13.5 us
    unnamed x12, local copies, waits for them, and re-layouts  7.4 us
    pallas_call x1, Pallas kernels, on_device(): call(functools.partial(second_kernel, features), steps, [whole(sums_shape...  7.34 us
  transfers between devices with their start and end apart: 13, of which 5 were waited for; matrix products, arithmetic and copies ran while one was open for 1% of the time, Pallas kernels for 4%

profile of v2, /device:TPU:96, one launch (start us, length us, event | category | flops | bytes accessed | tf_op | source)
XLA Modules:
  0.0 176.4 jit_solution(18192060906980745048)
XLA Ops:
  7.2 0.0 all-gather.5.cloned.1.call-start
  7.2 2.0 %pad_maximum_fusion = bf16[768,384]{1,0:T(8,128)(2,1)} fusion(bf16[384,384]{1,0:T(8,128)(2,1)} %param.8, bf16[384,384]{1,0:T(8,128)(2,1)} %param.7), kind=kLoop, calls=%fused_computation.1 | loop fusion | flops 1179648 | bytes 1179648 | tf_op jit(solution)/shard_map/concatenate | solution.py:228
  9.2 0.0 all-gather.5.cloned.1.call-update
  9.2 0.8 pad_maximum_fusion.4
  10.0 1.0 pad_maximum_fusion.3
  11.1 1.9 %collective-permute-start.2 = (bf16[168,384]{1,0:T(8,128)(2,1)S(1)}, bf16[168,384]{1,0:T(8,128)(2,1)S(1)}, u32[]{:S(2)}, u32[]{:S(2)}) collective-permute-start(bf16[168,384]{1,0:T(8,128)(2,1)S(1)} %pad_maximum_fusion.3), channel_id=1, source_target_pairs={{0,16},{8,24},{16,272},{24,280},{256,0},{264,8},{272,256},{280,264... | collective-permute-start | bytes 387080 | tf_op jit(solution)/shard_map/ppermute | solution.py:233
  13.0 11.5 %collective-permute-start.3 = (bf16[168,384]{1,0:T(8,128)(2,1)S(1)}, bf16[168,384]{1,0:T(8,128)(2,1)S(1)}, u32[]{:S(2)}, u32[]{:S(2)}) collective-permute-start(bf16[168,384]{1,0:T(8,128)(2,1)S(1)} %pad_maximum_fusion.3), channel_id=1, source_target_pairs={{0,24},{8,16},{16,280},{24,272},{256,8},{264,0},{272,264},{280,256... | collective-permute-start | bytes 387080 | tf_op jit(solution)/shard_map/ppermute | solution.py:233
  24.5 2.8 %collective-permute-start = (bf16[168,384]{1,0:T(8,128)(2,1)S(1)}, bf16[168,384]{1,0:T(8,128)(2,1)S(1)}, u32[]{:S(2)}, u32[]{:S(2)}) collective-permute-start(bf16[168,384]{1,0:T(8,128)(2,1)S(1)} %pad_maximum_fusion.3), channel_id=1, source_target_pairs={{0,0},{8,8},{16,256},{24,264},{256,16},{264,24},{272,272},{280,280... | collective-permute-start | bytes 387080 | tf_op jit(solution)/shard_map/ppermute | solution.py:233
  27.3 6.0 %collective-permute-start.1 = (bf16[168,384]{1,0:T(8,128)(2,1)S(1)}, bf16[168,384]{1,0:T(8,128)(2,1)S(1)}, u32[]{:S(2)}, u32[]{:S(2)}) collective-permute-start(bf16[168,384]{1,0:T(8,128)(2,1)S(1)} %pad_maximum_fusion.3), channel_id=1, source_target_pairs={{0,8},{8,0},{16,264},{24,256},{256,24},{264,16},{272,280},{280,272... | collective-permute-start | bytes 387080 | tf_op jit(solution)/shard_map/ppermute | solution.py:233
  33.3 0.0 collective-permute-done.2
  33.3 0.0 collective-permute-done.3
  33.4 14.5 %all-gather.1 = bf16[8,168,384]{2,1,0:T(8,128)(2,1)S(1)} all-gather(bf16[2,168,384]{2,1,0:T(8,128)(2,1)S(1)} %pad_maximum_fusion.2), channel_id=3, replica_groups=mesh['l'=2,'y'=8,'h'=4,'x'=4,'k'=2] {'x'}, dimensions={0}, use_global_device_ids=true | all-gather | bytes 1290240 | tf_op jit(solution)/shard_map/all_gather | solution.py:237
  47.8 1.9 %collective-permute-start.5 = (bf16[4,2,168,384]{3,2,1,0:T(8,128)(2,1)S(1)}, bf16[4,2,168,384]{3,2,1,0:T(8,128)(2,1)}, u32[]{:S(2)}, u32[]{:S(2)}) collective-permute-start(bf16[4,2,168,384]{3,2,1,0:T(8,128)(2,1)S(1)} %bitcast.19), channel_id=1, source_target_pairs={{0,1},{1,0},{2,3},{3,2},{4,5},{5,4},{6,7},{7,6},{8,9},{9,8},{10,11... | collective-permute-start | bytes 3096584 | tf_op jit(solution)/shard_map/ppermute | solution.py:238
  49.7 0.0 collective-permute-done
  49.8 0.0 collective-permute-done.1
  49.8 15.9 %all-gather = bf16[8,168,384]{2,1,0:T(8,128)(2,1)S(1)} all-gather(bf16[2,168,384]{2,1,0:T(8,128)(2,1)S(1)} %pad_maximum_fusion.1), channel_id=2, replica_groups=mesh['l'=2,'y'=8,'h'=4,'x'=4,'k'=2] {'x'}, dimensions={0}, use_global_device_ids=true | all-gather | bytes 1290240 | tf_op jit(solution)/shard_map/all_gather | solution.py:235
  65.7 1.9 %collective-permute-start.4 = (bf16[4,2,168,384]{3,2,1,0:T(8,128)(2,1)S(1)}, bf16[4,2,168,384]{3,2,1,0:T(8,128)(2,1)}, u32[]{:S(2)}, u32[]{:S(2)}) collective-permute-start(bf16[4,2,168,384]{3,2,1,0:T(8,128)(2,1)S(1)} %bitcast.21), channel_id=1, source_target_pairs={{0,1},{1,0},{2,3},{3,2},{4,5},{5,4},{6,7},{7,6},{8,9},{9,8},{10,11... | collective-permute-start | bytes 3096584 | tf_op jit(solution)/shard_map/ppermute | solution.py:236
  67.6 0.0 copy-start.2
  67.6 1.0 copy-done.2
  68.6 0.1 pad_add_fusion.place_ref
  68.7 0.0 collective-permute-done.5.far1
  68.7 1.7 collective-permute-done.4.far0
  70.4 0.0 copy-start.3
  70.4 1.2 copy-done.3
  71.6 6.9 %merge.1 = (bf16[8,320,384]{2,1,0:T(8,128)(2,1)S(1)}, bf16[8,320,384]{2,1,0:T(8,128)(2,1)S(1)}, f32[8,8,384]{2,1,0:T(8,128)S(1)}, f32[320,128]{1,0:T(8,128)S(1)}) custom-call(s32[2]{0:T(128)S(1)} %pad_add_fusion.place_ref, bf16[4,2,168,384]{3,2,1,0:T(8,128)(2,1)S(1)} %bitcast.22, bf16[4,2,168,384]{3,2,1,0:T(8,128)(2,1)S(1)} %bitcast.20, ...), custom_call_target="tpu_custom_call" | custom-call | tf_op jit(solution)/shard_map/merge/pallas_call | solution.py:249
  78.5 0.0 copy-start.4
  78.5 1.3 copy-done.4
  79.8 0.0 all-gather.5.cloned.1.call-done
  79.8 0.0 copy-start
  79.8 2.3 %copy-done = bf16[6144,384]{1,0:T(8,128)(2,1)S(1)} copy-done((bf16[6144,384]{1,0:T(8,128)(2,1)S(1)}, bf16[6144,384]{1,0:T(8,128)(2,1)}, u32[]{:S(2)}) %copy-start) | copy-done | bytes 4718616
  82.2 0.0 copy-start.5
  82.2 1.5 copy-done.5
  83.7 0.0 copy-start.1
  83.7 5.6 %first.1.own_ref = bf16[656,384]{1,0:T(8,128)(2,1)S(1)} custom-call(s32[2]{0:T(128)S(1)} %pad_add_fusion.place_ref, bf16[8,320,384]{2,1,0:T(8,128)(2,1)S(1)} %get-tuple-element.8.x_ref, bf16[8,320,384]{2,1,0:T(8,128)(2,1)S(1)} %copy-done.5, f32[8,8,384]{2,1,0:T(8,128)S(1)} %get-tuple-element.10.gain_ref, f32[320,128]{1,0:T(8,128)S(1)} %get-tuple-element.11.stat_ref, ...), custom_call_target="tpu_custom_call" | custom-call | tf_op jit(solution)/shard_map/first/pallas_call | solution.py:266
  89.3 1.9 %collective-permute-start.6 = (bf16[656,384]{1,0:T(8,128)(2,1)S(1)}, bf16[656,384]{1,0:T(8,128)(2,1)S(1)}, u32[]{:S(2)}, u32[]{:S(2)}) collective-permute-start(bf16[656,384]{1,0:T(8,128)(2,1)S(1)} %first.1.own_ref), channel_id=1, source_target_pairs={{0,256},{256,0},{1,257},{257,1},{2,258},{258,2},{3,259},{259,3},{4... | collective-permute-start | bytes 1511432 | tf_op jit(solution)/shard_map/ppermute | solution.py:282
  91.2 13.5 %collective-permute-done.6.far_ref = bf16[656,384]{1,0:T(8,128)(2,1)S(1)} collective-permute-done((bf16[656,384]{1,0:T(8,128)(2,1)S(1)}, bf16[656,384]{1,0:T(8,128)(2,1)S(1)}, u32[]{:S(2)}, u32[]{:S(2)}) %collective-permute-start.6) | collective-permute-done | bytes 503840 | tf_op jit(solution)/shard_map/ppermute | solution.py:282
  104.7 0.0 copy-done.1
  104.7 7.3 %second.1 = (bf16[4,2,2,160,384]{4,3,2,1,0:T(8,128)(2,1)S(1)}, bf16[4,2,2,160,384]{4,3,2,1,0:T(8,128)(2,1)S(1)}) custom-call(s32[2]{0:T(128)S(1)} %pad_add_fusion.place_ref, bf16[656,384]{1,0:T(8,128)(2,1)S(1)} %first.1.own_ref, bf16[656,384]{1,0:T(8,128)(2,1)S(1)} %collective-permute-done.6.far_ref, bf16[8,320,384]{2,1,0:T(8,128)(2,1)S(1)} %get-tuple-element.8.x_ref, ...), custom_call_target="tpu_custom_call" | custom-call | tf_op jit(solution)/shard_map/second/pallas_call | solution.py:287
  112.1 1.9 %collective-permute-start.7 = (bf16[4,2,2,160,384]{4,3,2,1,0:T(8,128)(2,1)S(1)}, bf16[4,2,2,160,384]{4,3,2,1,0:T(8,128)(2,1)S(1)}, u32[]{:S(2)}, u32[]{:S(2)}) collective-permute-start(bf16[4,2,2,160,384]{4,3,2,1,0:T(8,128)(2,1)S(1)} %get-tuple-element.13), channel_id=1, source_target_pairs={{0,1},{1,0},{2,3},{3,2},{4,5},{5,4},{6,7},{7,6},{8,9},{9,8},{10,11... | collective-permute-start | bytes 5898248 | tf_op jit(solution)/shard_map/ppermute | solution.py:302
  114.0 3.9 %collective-permute-done.7 = bf16[4,2,2,160,384]{4,3,2,1,0:T(8,128)(2,1)S(1)} collective-permute-done((bf16[4,2,2,160,384]{4,3,2,1,0:T(8,128)(2,1)S(1)}, bf16[4,2,2,160,384]{4,3,2,1,0:T(8,128)(2,1)S(1)}, u32[]{:S(2)}, u32[]{:S(2)}) %collective-permute-start.7) | collective-permute-done | bytes 1966112 | tf_op jit(solution)/shard_map/ppermute | solution.py:302
  117.9 0.5 add_convert_fusion
  118.5 29.2 %all_to_all.5 = bf16[4,2,2,160,384]{4,3,2,1,0:T(8,128)(2,1)S(1)} all-to-all(bf16[4,2,2,160,384]{4,3,2,1,0:T(8,128)(2,1)S(1)} %add_convert_fusion), channel_id=1, replica_groups=mesh['l'=2,'y'=8,'h'=4,'x'=4,'k'=2] {'x'}, dimensions={0} | all-to-all | bytes 3932160 | tf_op jit(solution)/shard_map/all_to_all | solution.py:304
  147.7 0.5 reduce_sum.12
  148.2 0.1 slice_bitcast_fusion.3
  148.3 3.4 %collective-permute-start.10 = (bf16[160,384]{1,0:T(8,128)(2,1)S(1)}, bf16[160,384]{1,0:T(8,128)(2,1)S(1)}, u32[]{:S(2)}, u32[]{:S(2)}) collective-permute-start(bf16[160,384]{1,0:T(8,128)(2,1)S(1)} %get-tuple-element.16), channel_id=1, source_target_pairs={{0,256},{8,264},{16,0},{24,8},{256,272},{264,280},{272,16},{280,24... | collective-permute-start | bytes 368648 | tf_op jit(solution)/shard_map/ppermute | solution.py:307
  151.7 2.1 %collective-permute-start.11 = (bf16[160,384]{1,0:T(8,128)(2,1)S(1)}, bf16[160,384]{1,0:T(8,128)(2,1)S(1)}, u32[]{:S(2)}, u32[]{:S(2)}) collective-permute-start(bf16[160,384]{1,0:T(8,128)(2,1)S(1)} %get-tuple-element.15), channel_id=1, source_target_pairs={{0,264},{8,256},{16,8},{24,0},{256,280},{264,272},{272,24},{280,16... | collective-permute-start | bytes 368648 | tf_op jit(solution)/shard_map/ppermute | solution.py:307
  153.7 5.1 %collective-permute-start.8 = (bf16[160,384]{1,0:T(8,128)(2,1)S(1)}, bf16[160,384]{1,0:T(8,128)(2,1)S(1)}, u32[]{:S(2)}, u32[]{:S(2)}) collective-permute-start(bf16[160,384]{1,0:T(8,128)(2,1)S(1)} %get-tuple-element.14), channel_id=1, source_target_pairs={{0,0},{8,8},{16,256},{24,264},{256,16},{264,24},{272,272},{280,280... | collective-permute-start | bytes 368648 | tf_op jit(solution)/shard_map/ppermute | solution.py:307
  158.8 4.5 %collective-permute-start.9 = (bf16[160,384]{1,0:T(8,128)(2,1)S(1)}, bf16[160,384]{1,0:T(8,128)(2,1)S(1)}, u32[]{:S(2)}, u32[]{:S(2)}) collective-permute-start(bf16[160,384]{1,0:T(8,128)(2,1)S(1)} %get-tuple-element.17), channel_id=1, source_target_pairs={{0,8},{8,0},{16,264},{24,256},{256,24},{264,16},{272,280},{280,272... | collective-permute-start | bytes 368648 | tf_op jit(solution)/shard_map/ppermute | solution.py:307
  163.3 0.0 collective-permute-done.10
  163.3 0.0 collective-permute-done.11
  163.3 1.3 collective-permute-done.8
  164.6 4.1 %collective-permute-done.9 = bf16[160,384]{1,0:T(8,128)(2,1)S(1)} collective-permute-done((bf16[160,384]{1,0:T(8,128)(2,1)S(1)}, bf16[160,384]{1,0:T(8,128)(2,1)S(1)}, u32[]{:S(2)}, u32[]{:S(2)}) %collective-permute-start.9) | collective-permute-done | bytes 122912 | tf_op jit(solution)/shard_map/ppermute | solution.py:307
  168.7 0.1 add_convert_fusion.1
  168.8 0.7 fusion
  (3 shorter events, 0.1 us)
Async XLA Ops:
  7.2 72.7 %all-gather.5.cloned.1.call-start = ((), (), s32[]{:S(2)}) async-start(), calls=%async_computation.1 | async-start | bytes 5308416 | tf_op jit(solution)/shard_map/all_gather | solution.py:228
  11.1 22.3 %collective-permute-start.2 = (bf16[168,384]{1,0:T(8,128)(2,1)S(1)}, bf16[168,384]{1,0:T(8,128)(2,1)S(1)}, u32[]{:S(2)}, u32[]{:S(2)}) collective-permute-start(bf16[168,384]{1,0:T(8,128)(2,1)S(1)} %pad_maximum_fusion.3), channel_id=1, source_target_pairs={{0,16},{8,24},{16,272},{24,280},{256,0},{264,8},{272,256},{280,264... | collective-permute-start | bytes 387080 | tf_op jit(solution)/shard_map/ppermute | solution.py:233
  13.0 20.3 %collective-permute-start.3 = (bf16[168,384]{1,0:T(8,128)(2,1)S(1)}, bf16[168,384]{1,0:T(8,128)(2,1)S(1)}, u32[]{:S(2)}, u32[]{:S(2)}) collective-permute-start(bf16[168,384]{1,0:T(8,128)(2,1)S(1)} %pad_maximum_fusion.3), channel_id=1, source_target_pairs={{0,24},{8,16},{16,280},{24,272},{256,8},{264,0},{272,264},{280,256... | collective-permute-start | bytes 387080 | tf_op jit(solution)/shard_map/ppermute | solution.py:233
  24.5 25.3 %collective-permute-start = (bf16[168,384]{1,0:T(8,128)(2,1)S(1)}, bf16[168,384]{1,0:T(8,128)(2,1)S(1)}, u32[]{:S(2)}, u32[]{:S(2)}) collective-permute-start(bf16[168,384]{1,0:T(8,128)(2,1)S(1)} %pad_maximum_fusion.3), channel_id=1, source_target_pairs={{0,0},{8,8},{16,256},{24,264},{256,16},{264,24},{272,272},{280,280... | collective-permute-start | bytes 387080 | tf_op jit(solution)/shard_map/ppermute | solution.py:233
  27.3 22.5 %collective-permute-start.1 = (bf16[168,384]{1,0:T(8,128)(2,1)S(1)}, bf16[168,384]{1,0:T(8,128)(2,1)S(1)}, u32[]{:S(2)}, u32[]{:S(2)}) collective-permute-start(bf16[168,384]{1,0:T(8,128)(2,1)S(1)} %pad_maximum_fusion.3), channel_id=1, source_target_pairs={{0,8},{8,0},{16,264},{24,256},{256,24},{264,16},{272,280},{280,272... | collective-permute-start | bytes 387080 | tf_op jit(solution)/shard_map/ppermute | solution.py:233
  47.8 20.9 %collective-permute-start.5 = (bf16[4,2,168,384]{3,2,1,0:T(8,128)(2,1)S(1)}, bf16[4,2,168,384]{3,2,1,0:T(8,128)(2,1)}, u32[]{:S(2)}, u32[]{:S(2)}) collective-permute-start(bf16[4,2,168,384]{3,2,1,0:T(8,128)(2,1)S(1)} %bitcast.19), channel_id=1, source_target_pairs={{0,1},{1,0},{2,3},{3,2},{4,5},{5,4},{6,7},{7,6},{8,9},{9,8},{10,11... | collective-permute-start | bytes 3096584 | tf_op jit(solution)/shard_map/ppermute | solution.py:238
  65.7 4.7 %collective-permute-start.4 = (bf16[4,2,168,384]{3,2,1,0:T(8,128)(2,1)S(1)}, bf16[4,2,168,384]{3,2,1,0:T(8,128)(2,1)}, u32[]{:S(2)}, u32[]{:S(2)}) collective-permute-start(bf16[4,2,168,384]{3,2,1,0:T(8,128)(2,1)S(1)} %bitcast.21), channel_id=1, source_target_pairs={{0,1},{1,0},{2,3},{3,2},{4,5},{5,4},{6,7},{7,6},{8,9},{9,8},{10,11... | collective-permute-start | bytes 3096584 | tf_op jit(solution)/shard_map/ppermute | solution.py:236
  67.6 1.0 copy-start.2
  70.4 1.2 copy-start.3
  78.5 1.3 copy-start.4
  79.8 2.3 %copy-start = (bf16[6144,384]{1,0:T(8,128)(2,1)S(1)}, bf16[6144,384]{1,0:T(8,128)(2,1)}, u32[]{:S(2)}) copy-start(bf16[6144,384]{1,0:T(8,128)(2,1)} %all-gather.5.cloned.1.call-done) | copy-start | bytes 14155780
  82.2 1.5 copy-start.5
  83.7 21.0 %copy-start.1 = (bf16[6144,384]{1,0:T(8,128)(2,1)S(1)}, bf16[6144,384]{1,0:T(8,128)(2,1)}, u32[]{:S(2)}) copy-start(bf16[6144,384]{1,0:T(8,128)(2,1)} %all-gather.5.cloned.1.call-done) | copy-start | bytes 14155780
  89.3 15.4 %collective-permute-start.6 = (bf16[656,384]{1,0:T(8,128)(2,1)S(1)}, bf16[656,384]{1,0:T(8,128)(2,1)S(1)}, u32[]{:S(2)}, u32[]{:S(2)}) collective-permute-start(bf16[656,384]{1,0:T(8,128)(2,1)S(1)} %first.1.own_ref), channel_id=1, source_target_pairs={{0,256},{256,0},{1,257},{257,1},{2,258},{258,2},{3,259},{259,3},{4... | collective-permute-start | bytes 1511432 | tf_op jit(solution)/shard_map/ppermute | solution.py:282
  112.1 5.9 %collective-permute-start.7 = (bf16[4,2,2,160,384]{4,3,2,1,0:T(8,128)(2,1)S(1)}, bf16[4,2,2,160,384]{4,3,2,1,0:T(8,128)(2,1)S(1)}, u32[]{:S(2)}, u32[]{:S(2)}) collective-permute-start(bf16[4,2,2,160,384]{4,3,2,1,0:T(8,128)(2,1)S(1)} %get-tuple-element.13), channel_id=1, source_target_pairs={{0,1},{1,0},{2,3},{3,2},{4,5},{5,4},{6,7},{7,6},{8,9},{9,8},{10,11... | collective-permute-start | bytes 5898248 | tf_op jit(solution)/shard_map/ppermute | solution.py:302
  148.3 15.0 %collective-permute-start.10 = (bf16[160,384]{1,0:T(8,128)(2,1)S(1)}, bf16[160,384]{1,0:T(8,128)(2,1)S(1)}, u32[]{:S(2)}, u32[]{:S(2)}) collective-permute-start(bf16[160,384]{1,0:T(8,128)(2,1)S(1)} %get-tuple-element.16), channel_id=1, source_target_pairs={{0,256},{8,264},{16,0},{24,8},{256,272},{264,280},{272,16},{280,24... | collective-permute-start | bytes 368648 | tf_op jit(solution)/shard_map/ppermute | solution.py:307
  151.7 11.6 %collective-permute-start.11 = (bf16[160,384]{1,0:T(8,128)(2,1)S(1)}, bf16[160,384]{1,0:T(8,128)(2,1)S(1)}, u32[]{:S(2)}, u32[]{:S(2)}) collective-permute-start(bf16[160,384]{1,0:T(8,128)(2,1)S(1)} %get-tuple-element.15), channel_id=1, source_target_pairs={{0,264},{8,256},{16,8},{24,0},{256,280},{264,272},{272,24},{280,16... | collective-permute-start | bytes 368648 | tf_op jit(solution)/shard_map/ppermute | solution.py:307
  153.7 10.9 %collective-permute-start.8 = (bf16[160,384]{1,0:T(8,128)(2,1)S(1)}, bf16[160,384]{1,0:T(8,128)(2,1)S(1)}, u32[]{:S(2)}, u32[]{:S(2)}) collective-permute-start(bf16[160,384]{1,0:T(8,128)(2,1)S(1)} %get-tuple-element.14), channel_id=1, source_target_pairs={{0,0},{8,8},{16,256},{24,264},{256,16},{264,24},{272,272},{280,280... | collective-permute-start | bytes 368648 | tf_op jit(solution)/shard_map/ppermute | solution.py:307
  158.8 9.9 %collective-permute-start.9 = (bf16[160,384]{1,0:T(8,128)(2,1)S(1)}, bf16[160,384]{1,0:T(8,128)(2,1)S(1)}, u32[]{:S(2)}, u32[]{:S(2)}) collective-permute-start(bf16[160,384]{1,0:T(8,128)(2,1)S(1)} %get-tuple-element.17), channel_id=1, source_target_pairs={{0,8},{8,0},{16,264},{24,256},{256,24},{264,16},{272,280},{280,272... | collective-permute-start | bytes 368648 | tf_op jit(solution)/shard_map/ppermute | solution.py:307
Sparse Core Ops, SparseCore 0:
  10.1 63.3 all-gather.4

commit v3 on v2

--- a/solution.py
+++ b/solution.py
@@ -44,55 +44,71 @@
     return jnp.where(row == column, 1.0, 0.0).astype(narrow)
 
 
-def merge_kernel(place_ref, own0, own1, far0, far1, x_ref, g_ref, gain_ref, stat_ref, mean_s, spread_s):
+def stack_kernel(upper, lower, out, sems):
+    rows = upper.shape[0]
+    copies = [
+        pltpu.make_async_copy(upper, out.at[:rows], sems.at[0]),
+        pltpu.make_async_copy(lower, out.at[rows:], sems.at[1]),
+    ]
+    for copy in copies:
+        copy.start()
+    for copy in copies:
+        copy.wait()
+
+
+def merge_kernel(
+    place_ref, own0, own1, far0, far1, x_ref, g_ref, gain_ref, stat_ref, mean_s, gap_s, spread_s
+):
     step = pl.program_id(0)
-    rows = x_ref.shape[1] // 2
-    half = x_ref.shape[2] // 2
-    block = x_ref.shape[2]
+    per_step, tokens, block = x_ref.shape
+    rows = tokens // 2
+    half = block // 2
     first = place_ref[0] == 0
+    ones = jnp.ones((block, 128), narrow)
 
     def sides(own, far):
-        own, far = own.astype(wide), far.astype(wide)
         a = jnp.where(first, own, far)
         b = jnp.where(first, far, own)
         left = jnp.concatenate([a[:, :half], b[:, :half]], axis=1)
         right = jnp.concatenate([a[:, half:], b[:, half:]], axis=1)
         return left, right
 
-    x0, g0 = sides(own0[0, 0, :rows], far0[0, 0, :rows])
-    x1, g1 = sides(own1[0, 0, :rows], far1[0, 0, :rows])
-    gain, _ = sides(own0[0, 0, rows:], far0[0, 0, rows:])
-    gain_ref[0] = gain
-    x_ref[0, :rows] = x0.astype(narrow)
-    x_ref[0, rows:] = x1.astype(narrow)
-    g_ref[0, :rows] = g0.astype(narrow)
-    g_ref[0, rows:] = g1.astype(narrow)
-
     @pl.when(step == 0)
     def _():
         mean_s[...] = jnp.zeros_like(mean_s)
+        gap_s[...] = jnp.zeros_like(gap_s)
         spread_s[...] = jnp.zeros_like(spread_s)
 
-    seen = step.astype(wide)
-    for index, values in enumerate((x0, x1)):
-        at = pl.ds(index * rows, rows)
-        center = jnp.sum(values, axis=1, keepdims=True) * (1.0 / block)
-        shifted = values - center
-        spread = jnp.sum(shifted * shifted, axis=1, keepdims=True)
-        gap = center - mean_s[at]
-        mean_s[at] = mean_s[at] + gap / (seen + 1.0)
-        spread_s[at] = spread_s[at] + spread + gap * gap * (block * seen / (seen + 1.0))
+    for index in range(per_step):
+        seen = (step * per_step + index).astype(wide)
+        share = 1.0 / (seen + 1.0)
+        gain, _ = sides(own0[index, 0, rows:].astype(wide), far0[index, 0, rows:].astype(wide))
+        gain_ref[index] = gain
+        for part, (own, far) in enumerate(((own0, far0), (own1, far1))):
+            at = pl.ds(part * rows, rows)
+            values, grads = sides(own[index, 0, :rows], far[index, 0, :rows])
+            x_ref[index, at] = values
+            g_ref[index, at] = grads
+            center = jnp.dot(values, ones, preferred_element_type=wide) * (1.0 / block)
+            gap = center - mean_s[at]
+            mean_s[at] = mean_s[at] + gap * share
+            gap_s[at] = gap_s[at] + gap * gap * (block * seen * share)
+            spread = spread_s[at]
+            for lane in range(0, block, 128):
+                shifted = values[:, lane : lane + 128].astype(wide) - center
+                spread = spread + shifted * shifted
+            spread_s[at] = spread
 
     @pl.when(step == pl.num_programs(0) - 1)
     def _():
         lane = lax.broadcasted_iota(jnp.int32, stat_ref.shape, 1)
-        stat_ref[...] = jnp.where(lane < 64, mean_s[...], spread_s[...])
+        spread = jnp.sum(spread_s[...], axis=1, keepdims=True) + gap_s[...]
+        stat_ref[...] = jnp.where(lane < 64, mean_s[...], spread)
 
 
 def first_kernel(place_ref, x_ref, g_ref, gain_ref, stat_ref, panel_ref, sums_ref, pre_s, act_s, gain_s, table_s):
     step = pl.program_id(0)
-    tokens = x_ref.shape[1]
-    block = x_ref.shape[2]
+    per_step, tokens, block = x_ref.shape
 
     @pl.when(step == 0)
     def _():
@@ -100,15 +116,16 @@
         act_s[...] = jnp.zeros_like(act_s)
         gain_s[...] = jnp.zeros_like(gain_s)
 
-    w_in = panel_ref[0, :block]
-    w_out = panel_ref[0, block:]
-    gain = gain_ref[0]
-    shifted = ((x_ref[0].astype(wide) - stat_ref[:, :1]) * gain[:1]).astype(narrow)
-    pre_s[...] += jnp.dot(shifted, w_in, preferred_element_type=wide)
-    act_s[...] += lax.dot_general(
-        g_ref[0], w_out, (((1,), (1,)), ((), ())), preferred_element_type=wide
-    )
-    gain_s[...] += jnp.dot(gain.astype(narrow), w_in, preferred_element_type=wide)
+    for index in range(per_step):
+        w_in = panel_ref[index, :block]
+        w_out = panel_ref[index, block:]
+        gain = gain_ref[index]
+        shifted = ((x_ref[index].astype(wide) - stat_ref[:, :1]) * gain[:1]).astype(narrow)
+        pre_s[...] += jnp.dot(shifted, w_in, preferred_element_type=wide)
+        act_s[...] += lax.dot_general(
+            g_ref[index], w_out, (((1,), (1,)), ((), ())), preferred_element_type=wide
+        )
+        gain_s[...] += jnp.dot(gain.astype(narrow), w_in, preferred_element_type=wide)
 
     @pl.when(step == pl.num_programs(0) - 1)
     def _():
@@ -135,8 +152,7 @@
     keep_ref, send_ref, act_s, pre_s, mean_s, inv_s, flat_s, cross_s,
 ):
     step = pl.program_id(0)
-    tokens = x_ref.shape[1]
-    block = x_ref.shape[2]
+    per_step, tokens, block = x_ref.shape
     rows = tokens // 2
     half = block // 2
 
@@ -174,23 +190,28 @@
         flat_s[...] = jnp.sum(d_pre * (gain_a + gain_b), axis=1, keepdims=True) / features
         cross_s[...] = jnp.sum(d_pre * preact, axis=1, keepdims=True) / features
 
-    w_in = panel_ref[0, :block]
-    w_out = panel_ref[0, block:]
-    out = jnp.dot(act_s[...], w_out, preferred_element_type=wide)
-    d_normed = lax.dot_general(
-        pre_s[...], w_in, (((1,), (1,)), ((), ())), preferred_element_type=wide
-    )
-    standard = (x_ref[0].astype(wide) - mean_s[...]) * inv_s[...]
-    grad = inv_s[...] * (d_normed * gain_ref[0][:1] - flat_s[...] - standard * cross_s[...])
-    out, grad = out.astype(narrow), grad.astype(narrow)
-    side0 = jnp.concatenate([out[:, :half], grad[:, :half]], axis=1)
-    side1 = jnp.concatenate([out[:, half:], grad[:, half:]], axis=1)
     first = place_ref[0] == 0
-    keep = jnp.where(first, side0, side1)
-    send = jnp.where(first, side1, side0)
-    for index in range(2):
-        keep_ref[0, index, 0] = keep[index * rows : (index + 1) * rows]
-        send_ref[0, index, 0] = send[index * rows : (index + 1) * rows]
+    for index in range(per_step):
+        w_in = panel_ref[index, :block]
+        w_out = panel_ref[index, block:]
+        out = jnp.dot(act_s[...], w_out, preferred_element_type=wide).astype(narrow)
+        d_normed = lax.dot_general(
+            pre_s[...], w_in, (((1,), (1,)), ((), ())), preferred_element_type=wide
+        )
+        standard = (x_ref[index].astype(wide) - mean_s[...]) * inv_s[...]
+        grad = inv_s[...] * (d_normed * gain_ref[index][:1] - flat_s[...] - standard * cross_s[...])
+        grad = grad.astype(narrow)
+        side0 = jnp.concatenate([out[:, :half], grad[:, :half]], axis=1)
+        side1 = jnp.concatenate([out[:, half:], grad[:, half:]], axis=1)
+        keep = jnp.where(first, side0, side1)
+        send = jnp.where(first, side1, side0)
+        for part in range(2):
+            keep_ref[index, part, 0] = keep[part * rows : (part + 1) * rows]
+            send_ref[index, part, 0] = send[part * rows : (part + 1) * rows]
+
+
+def in_hbm(array):
+    return pltpu.with_memory_space_constraint(array, pltpu.HBM)
 
 
 def whole(shape):
@@ -221,11 +242,20 @@
     tokens = 2 * rows
     hidden = w_in.shape[1]
     features = piece * lax.axis_size(("h", "x", "k"))
-    steps = features // 2 // block
+    blocks = features // 2 // block
+    steps = blocks // 2
     other_core = [(0, 1), (1, 0)]
     place = jnp.stack([lax.axis_index("k"), lax.axis_index("h") % 2]).astype(jnp.int32)
 
-    panels = lax.all_gather(jnp.concatenate([w_in, w_out], axis=0), "y", axis=0)
+    weights = pl.pallas_call(
+        stack_kernel,
+        in_specs=[pl.BlockSpec(memory_space=pl.ANY)] * 2,
+        out_specs=pl.BlockSpec(memory_space=pl.ANY),
+        out_shape=jax.ShapeDtypeStruct((2 * block, hidden), narrow),
+        scratch_shapes=[pltpu.SemaphoreType.DMA((2,))],
+        name="stack",
+    )(w_in, w_out)
+    panels = in_hbm(lax.all_gather(weights, "y", axis=0))
 
     gain_rows = jnp.broadcast_to(jnp.concatenate([gain, gain])[None, :], (8, block))
     pack = jnp.concatenate([jnp.concatenate([inputs, grad_out], axis=1), gain_rows], axis=0)
@@ -236,12 +266,13 @@
     far0 = lax.ppermute(own0, "k", other_core)
     own1 = lax.all_gather(jnp.stack(near[1]), "x", axis=0)
     far1 = lax.ppermute(own1, "k", other_core)
-
-    tile = pl.BlockSpec((1, 1, rows + 8, block), lambda j, place: (j % 4, j // 4, 0, 0))
-    step_block = pl.BlockSpec((1, tokens, block), lambda j, place: (j, 0, 0))
-    gain_block = pl.BlockSpec((1, 8, block), lambda j, place: (j, 0, 0))
+    pieces = [in_hbm(piece) for piece in (own0, own1, far0, far1)]
+
+    tile = pl.BlockSpec((2, 1, rows + 8, block), lambda j, place: (j % 2, j // 2, 0, 0))
+    step_block = pl.BlockSpec((2, tokens, block), lambda j, place: (j, 0, 0))
+    gain_block = pl.BlockSpec((2, 8, block), lambda j, place: (j, 0, 0))
     panel_block = pl.BlockSpec(
-        (1,) + panels.shape[1:], lambda j, place: (((j // 4) ^ place[1]) * 4 + j % 4, 0, 0)
+        (2,) + panels.shape[1:], lambda j, place: (((j // 2) ^ place[1]) * 2 + j % 2, 0, 0)
     )
     stat_shape = (tokens, 128)
     column = pltpu.VMEM((tokens, 1), wide)
@@ -252,15 +283,15 @@
         [tile] * 4,
         [step_block, step_block, gain_block, whole(stat_shape)],
         [
-            jax.ShapeDtypeStruct((steps, tokens, block), narrow),
-            jax.ShapeDtypeStruct((steps, tokens, block), narrow),
-            jax.ShapeDtypeStruct((steps, 8, block), wide),
-            jax.ShapeDtypeStruct(stat_shape, wide),
+            pltpu.HBM((blocks, tokens, block), narrow),
+            pltpu.HBM((blocks, tokens, block), narrow),
+            pltpu.HBM((blocks, 8, block), wide),
+            pltpu.HBM(stat_shape, wide),
         ],
-        [column, column],
-        8,
+        [pltpu.VMEM(stat_shape, wide)] * 3,
+        12,
         "merge",
-    )(place, own0, own1, far0, far1)
+    )(place, *pieces)
 
     sums_shape = (2 * tokens + 16, hidden)
     sums = call(
@@ -277,12 +308,12 @@
         ],
         12,
         "first",
-    )(place, values, grads, gains, stats, panels)
+    )(place, in_hbm(values), in_hbm(grads), gains, stats, panels)
 
     far_sums = lax.ppermute(sums, "l", other_core)
 
     part_shape = (4, 2, 2, rows, block)
-    part_block = pl.BlockSpec((1, 2, 1, rows, block), lambda j, place: (j % 4, 0, j // 4, 0, 0))
+    part_block = pl.BlockSpec((2, 2, 1, rows, block), lambda j, place: (j % 2, 0, j // 2, 0, 0))
     part = jax.ShapeDtypeStruct(part_shape, narrow)
     keep, send = call(
         functools.partial(second_kernel, features),
@@ -297,7 +328,7 @@
         ],
         14,
         "second",
-    )(place, sums, far_sums, values, gains, panels)
+    )(place, sums, far_sums, in_hbm(values), gains, panels)
 
     got = lax.ppermute(send, "k", other_core)
     total = (keep.astype(wide) + got.astype(wide)).astype(narrow)

time: 177 us -> 191 us (1.079)
  the two profiles are of different devices: /device:TPU:96 before, /device:TPU:64 now
where the time goes in v3:
time: 191 us
  blocking collectives  59.6 us (31%)
  starting transfers between devices  46.2 us (24%)
  Pallas kernels  40.6 us (21%)
  waiting for transfers between devices  24.3 us (13%)
  between operations  14.3 us (7%)
  other arithmetic  3.14 us (2%)
  local copies, waits for them, and re-layouts  2.61 us (1%)
    all_to_all x1, blocking collectives, on_device(): total = lax.all_to_all(total, 'x', 0, 0)  29.2 us
    ppermute x4, starting transfers between devices, on_device(): lax.ppermute(pack, ('l', 'h'), gather_pairs(i, j))  22.2 us
    pallas_call x1, Pallas kernels, on_device(): pl.pallas_call(stack_kernel, in_specs=[pl.BlockSpec(memory_space=pl.ANY)]...  19 us
    ppermute x4, starting transfers between devices, on_device(): lax.ppermute(total[i, j], ('l', 'h'), scatter_pairs(i, j)).astype(wide)  16.3 us
    all_gather x1, blocking collectives, on_device(): own0 = lax.all_gather(jnp.stack(near[0]), 'x', axis=0)  15.9 us
    all_gather x1, blocking collectives, on_device(): own1 = lax.all_gather(jnp.stack(near[1]), 'x', axis=0)  14.5 us
    ppermute x1, waiting for transfers between devices, on_device(): far_sums = lax.ppermute(sums, 'l', other_core)  13.5 us
    pallas_call x1, Pallas kernels, on_device(): call(functools.partial(second_kernel, features), steps, [whole(sums_shape...  7.82 us
  transfers between devices with their start and end apart: 13, of which 5 were waited for; matrix products, arithmetic and copies ran while one was open for 1% of the time, Pallas kernels for 3%

profile of v3, /device:TPU:64, one launch (start us, length us, event | category | flops | bytes accessed | tf_op | source)
XLA Modules:
  0.0 190.7 jit_solution(6397567257697590601)
XLA Ops:
  7.2 0.0 all-gather.5.cloned.1.call-start
  7.2 19.0 %stack.37 = bf16[768,384]{1,0:T(8,128)(2,1)} custom-call(bf16[384,384]{1,0:T(8,128)(2,1)} %upper.1, bf16[384,384]{1,0:T(8,128)(2,1)} %lower.1), custom_call_target="tpu_custom_call" | custom-call | tf_op jit(solution)/shard_map/stack/pallas_call | solution.py:250
  26.2 0.0 all-gather.5.cloned.1.call-update
  26.2 0.8 pad_maximum_fusion.3
  27.0 1.0 pad_maximum_fusion.2
  28.1 6.9 %collective-permute-start.2 = (bf16[168,384]{1,0:T(8,128)(2,1)S(1)}, bf16[168,384]{1,0:T(8,128)(2,1)S(1)}, u32[]{:S(2)}, u32[]{:S(2)}) collective-permute-start(bf16[168,384]{1,0:T(8,128)(2,1)S(1)} %pad_maximum_fusion.2), channel_id=1, source_target_pairs={{0,16},{8,24},{16,272},{24,280},{256,0},{264,8},{272,256},{280,264... | collective-permute-start | bytes 387080 | tf_op jit(solution)/shard_map/ppermute | solution.py:263
  35.0 6.5 %collective-permute-start.3 = (bf16[168,384]{1,0:T(8,128)(2,1)S(1)}, bf16[168,384]{1,0:T(8,128)(2,1)S(1)}, u32[]{:S(2)}, u32[]{:S(2)}) collective-permute-start(bf16[168,384]{1,0:T(8,128)(2,1)S(1)} %pad_maximum_fusion.2), channel_id=1, source_target_pairs={{0,24},{8,16},{16,280},{24,272},{256,8},{264,0},{272,264},{280,256... | collective-permute-start | bytes 387080 | tf_op jit(solution)/shard_map/ppermute | solution.py:263
  41.5 2.8 %collective-permute-start = (bf16[168,384]{1,0:T(8,128)(2,1)S(1)}, bf16[168,384]{1,0:T(8,128)(2,1)S(1)}, u32[]{:S(2)}, u32[]{:S(2)}) collective-permute-start(bf16[168,384]{1,0:T(8,128)(2,1)S(1)} %pad_maximum_fusion.2), channel_id=1, source_target_pairs={{0,0},{8,8},{16,256},{24,264},{256,16},{264,24},{272,272},{280,280... | collective-permute-start | bytes 387080 | tf_op jit(solution)/shard_map/ppermute | solution.py:263
  44.3 6.0 %collective-permute-start.1 = (bf16[168,384]{1,0:T(8,128)(2,1)S(1)}, bf16[168,384]{1,0:T(8,128)(2,1)S(1)}, u32[]{:S(2)}, u32[]{:S(2)}) collective-permute-start(bf16[168,384]{1,0:T(8,128)(2,1)S(1)} %pad_maximum_fusion.2), channel_id=1, source_target_pairs={{0,8},{8,0},{16,264},{24,256},{256,24},{264,16},{272,280},{280,272... | collective-permute-start | bytes 387080 | tf_op jit(solution)/shard_map/ppermute | solution.py:263
  50.3 0.0 collective-permute-done.2
  50.3 0.0 collective-permute-done.3
  50.4 14.5 %all-gather.1 = bf16[8,168,384]{2,1,0:T(8,128)(2,1)S(1)} all-gather(bf16[2,168,384]{2,1,0:T(8,128)(2,1)S(1)} %pad_maximum_fusion.1), channel_id=3, replica_groups=mesh['l'=2,'y'=8,'h'=4,'x'=4,'k'=2] {'x'}, dimensions={0}, use_global_device_ids=true | all-gather | bytes 1290240 | tf_op jit(solution)/shard_map/all_gather | solution.py:267
  64.8 0.0 copy-start.3
  64.8 1.9 %collective-permute-start.5 = (bf16[4,2,168,384]{3,2,1,0:T(8,128)(2,1)S(1)}, bf16[4,2,168,384]{3,2,1,0:T(8,128)(2,1)S(1)}, u32[]{:S(2)}, u32[]{:S(2)}) collective-permute-start(bf16[4,2,168,384]{3,2,1,0:T(8,128)(2,1)S(1)} %bitcast.19), channel_id=1, source_target_pairs={{0,1},{1,0},{2,3},{3,2},{4,5},{5,4},{6,7},{7,6},{8,9},{9,8},{10,11... | collective-permute-start | bytes 3096584 | tf_op jit(solution)/shard_map/ppermute | solution.py:268
  66.8 0.0 collective-permute-done
  66.8 0.0 collective-permute-done.1
  66.8 15.9 %all-gather = bf16[8,168,384]{2,1,0:T(8,128)(2,1)S(1)} all-gather(bf16[2,168,384]{2,1,0:T(8,128)(2,1)S(1)} %pad_maximum_fusion), channel_id=2, replica_groups=mesh['l'=2,'y'=8,'h'=4,'x'=4,'k'=2] {'x'}, dimensions={0}, use_global_device_ids=true | all-gather | bytes 1290240 | tf_op jit(solution)/shard_map/all_gather | solution.py:265
  82.7 0.0 copy-start.4
  82.7 1.9 %collective-permute-start.4 = (bf16[4,2,168,384]{3,2,1,0:T(8,128)(2,1)S(1)}, bf16[4,2,168,384]{3,2,1,0:T(8,128)(2,1)}, u32[]{:S(2)}, u32[]{:S(2)}) collective-permute-start(bf16[4,2,168,384]{3,2,1,0:T(8,128)(2,1)S(1)} %bitcast.21), channel_id=1, source_target_pairs={{0,1},{1,0},{2,3},{3,2},{4,5},{5,4},{6,7},{7,6},{8,9},{9,8},{10,11... | collective-permute-start | bytes 3096584 | tf_op jit(solution)/shard_map/ppermute | solution.py:266
  84.7 0.1 pad_add_fusion.place_ref
  84.7 0.0 collective-permute-done.5.far1
  84.7 0.0 copy-start.5
  84.7 2.6 %collective-permute-done.4.far0 = bf16[4,2,168,384]{3,2,1,0:T(8,128)(2,1)} collective-permute-done((bf16[4,2,168,384]{3,2,1,0:T(8,128)(2,1)S(1)}, bf16[4,2,168,384]{3,2,1,0:T(8,128)(2,1)}, u32[]{:S(2)}, u32[]{:S(2)}) %collective-permute-start.4) | collective-permute-done | bytes 1032224 | tf_op jit(solution)/shard_map/ppermute | solution.py:266
  87.4 0.0 copy-done.3
  87.4 0.0 copy-done.4
  87.4 0.0 copy-done.5
  87.4 6.6 %merge.1 = (bf16[8,320,384]{2,1,0:T(8,128)(2,1)}, bf16[8,320,384]{2,1,0:T(8,128)(2,1)}, f32[8,8,384]{2,1,0:T(8,128)}, f32[320,128]{1,0:T(8,128)}) custom-call(s32[2]{0:T(128)S(1)} %pad_add_fusion.place_ref, bf16[4,2,168,384]{3,2,1,0:T(8,128)(2,1)} %bitcast.22, bf16[4,2,168,384]{3,2,1,0:T(8,128)(2,1)} %bitcast.20, ...), custom_call_target="tpu_custom_call" | custom-call | tf_op jit(solution)/shard_map/merge/pallas_call | solution.py:280
  94.0 0.0 all-gather.5.cloned.1.call-done
  94.1 0.0 copy-start
  94.1 0.9 copy-done
  94.9 0.0 copy-start.2
  94.9 0.9 copy-done.2
  95.9 0.0 copy-start.1
  95.9 7.1 %first.1.own_ref = bf16[656,384]{1,0:T(8,128)(2,1)S(1)} custom-call(s32[2]{0:T(128)S(1)} %pad_add_fusion.place_ref, bf16[8,320,384]{2,1,0:T(8,128)(2,1)} %get-tuple-element.8.x_ref, bf16[8,320,384]{2,1,0:T(8,128)(2,1)} %get-tuple-element.9.g_ref, f32[8,8,384]{2,1,0:T(8,128)S(1)} %copy-done, f32[320,128]{1,0:T(8,128)S(1)} %copy-done.2, ...), custom_call_target="tpu_custom_call" | custom-call | tf_op jit(solution)/shard_map/first/pallas_call | solution.py:297
  103.0 1.9 %collective-permute-start.6 = (bf16[656,384]{1,0:T(8,128)(2,1)S(1)}, bf16[656,384]{1,0:T(8,128)(2,1)S(1)}, u32[]{:S(2)}, u32[]{:S(2)}) collective-permute-start(bf16[656,384]{1,0:T(8,128)(2,1)S(1)} %first.1.own_ref), channel_id=1, source_target_pairs={{0,256},{256,0},{1,257},{257,1},{2,258},{258,2},{3,259},{259,3},{4... | collective-permute-start | bytes 1511432 | tf_op jit(solution)/shard_map/ppermute | solution.py:313
  104.9 13.5 %collective-permute-done.6.far_ref = bf16[656,384]{1,0:T(8,128)(2,1)S(1)} collective-permute-done((bf16[656,384]{1,0:T(8,128)(2,1)S(1)}, bf16[656,384]{1,0:T(8,128)(2,1)S(1)}, u32[]{:S(2)}, u32[]{:S(2)}) %collective-permute-start.6) | collective-permute-done | bytes 503840 | tf_op jit(solution)/shard_map/ppermute | solution.py:313
  118.4 0.0 copy-done.1
  118.4 7.8 %second.1 = (bf16[4,2,2,160,384]{4,3,2,1,0:T(8,128)(2,1)S(1)}, bf16[4,2,2,160,384]{4,3,2,1,0:T(8,128)(2,1)S(1)}) custom-call(s32[2]{0:T(128)S(1)} %pad_add_fusion.place_ref, bf16[656,384]{1,0:T(8,128)(2,1)S(1)} %first.1.own_ref, bf16[656,384]{1,0:T(8,128)(2,1)S(1)} %collective-permute-done.6.far_ref, bf16[8,320,384]{2,1,0:T(8,128)(2,1)} %get-tuple-element.8.x_ref, ...), custom_call_target="tpu_custom_call" | custom-call | tf_op jit(solution)/shard_map/second/pallas_call | solution.py:318
  126.2 1.9 %collective-permute-start.7 = (bf16[4,2,2,160,384]{4,3,2,1,0:T(8,128)(2,1)S(1)}, bf16[4,2,2,160,384]{4,3,2,1,0:T(8,128)(2,1)S(1)}, u32[]{:S(2)}, u32[]{:S(2)}) collective-permute-start(bf16[4,2,2,160,384]{4,3,2,1,0:T(8,128)(2,1)S(1)} %get-tuple-element.13), channel_id=1, source_target_pairs={{0,1},{1,0},{2,3},{3,2},{4,5},{5,4},{6,7},{7,6},{8,9},{9,8},{10,11... | collective-permute-start | bytes 5898248 | tf_op jit(solution)/shard_map/ppermute | solution.py:333
  128.2 3.9 %collective-permute-done.7 = bf16[4,2,2,160,384]{4,3,2,1,0:T(8,128)(2,1)S(1)} collective-permute-done((bf16[4,2,2,160,384]{4,3,2,1,0:T(8,128)(2,1)S(1)}, bf16[4,2,2,160,384]{4,3,2,1,0:T(8,128)(2,1)S(1)}, u32[]{:S(2)}, u32[]{:S(2)}) %collective-permute-start.7) | collective-permute-done | bytes 1966112 | tf_op jit(solution)/shard_map/ppermute | solution.py:333
  132.1 0.5 add_convert_fusion
  132.7 29.2 %all_to_all.5 = bf16[4,2,2,160,384]{4,3,2,1,0:T(8,128)(2,1)S(1)} all-to-all(bf16[4,2,2,160,384]{4,3,2,1,0:T(8,128)(2,1)S(1)} %add_convert_fusion), channel_id=1, replica_groups=mesh['l'=2,'y'=8,'h'=4,'x'=4,'k'=2] {'x'}, dimensions={0} | all-to-all | bytes 3932160 | tf_op jit(solution)/shard_map/all_to_all | solution.py:335
  161.9 0.5 reduce_sum.12
  162.4 0.1 slice_bitcast_fusion.3
  162.5 5.2 %collective-permute-start.10 = (bf16[160,384]{1,0:T(8,128)(2,1)S(1)}, bf16[160,384]{1,0:T(8,128)(2,1)S(1)}, u32[]{:S(2)}, u32[]{:S(2)}) collective-permute-start(bf16[160,384]{1,0:T(8,128)(2,1)S(1)} %get-tuple-element.16), channel_id=1, source_target_pairs={{0,256},{8,264},{16,0},{24,8},{256,272},{264,280},{272,16},{280,24... | collective-permute-start | bytes 368648 | tf_op jit(solution)/shard_map/ppermute | solution.py:338
  167.7 1.9 %collective-permute-start.11 = (bf16[160,384]{1,0:T(8,128)(2,1)S(1)}, bf16[160,384]{1,0:T(8,128)(2,1)S(1)}, u32[]{:S(2)}, u32[]{:S(2)}) collective-permute-start(bf16[160,384]{1,0:T(8,128)(2,1)S(1)} %get-tuple-element.15), channel_id=1, source_target_pairs={{0,264},{8,256},{16,8},{24,0},{256,280},{264,272},{272,24},{280,16... | collective-permute-start | bytes 368648 | tf_op jit(solution)/shard_map/ppermute | solution.py:338
  169.6 3.6 %collective-permute-start.8 = (bf16[160,384]{1,0:T(8,128)(2,1)S(1)}, bf16[160,384]{1,0:T(8,128)(2,1)S(1)}, u32[]{:S(2)}, u32[]{:S(2)}) collective-permute-start(bf16[160,384]{1,0:T(8,128)(2,1)S(1)} %get-tuple-element.14), channel_id=1, source_target_pairs={{0,0},{8,8},{16,256},{24,264},{256,16},{264,24},{272,272},{280,280... | collective-permute-start | bytes 368648 | tf_op jit(solution)/shard_map/ppermute | solution.py:338
  173.2 5.7 %collective-permute-start.9 = (bf16[160,384]{1,0:T(8,128)(2,1)S(1)}, bf16[160,384]{1,0:T(8,128)(2,1)S(1)}, u32[]{:S(2)}, u32[]{:S(2)}) collective-permute-start(bf16[160,384]{1,0:T(8,128)(2,1)S(1)} %get-tuple-element.17), channel_id=1, source_target_pairs={{0,8},{8,0},{16,264},{24,256},{256,24},{264,16},{272,280},{280,272... | collective-permute-start | bytes 368648 | tf_op jit(solution)/shard_map/ppermute | solution.py:338
  178.8 0.0 collective-permute-done.10
  178.8 0.0 collective-permute-done.11
  178.9 1.6 collective-permute-done.8
  180.5 2.5 %collective-permute-done.9 = bf16[160,384]{1,0:T(8,128)(2,1)S(1)} collective-permute-done((bf16[160,384]{1,0:T(8,128)(2,1)S(1)}, bf16[160,384]{1,0:T(8,128)(2,1)S(1)}, u32[]{:S(2)}, u32[]{:S(2)}) %collective-permute-start.9) | collective-permute-done | bytes 122912 | tf_op jit(solution)/shard_map/ppermute | solution.py:338
  183.0 0.1 add_convert_fusion.1
  183.1 0.7 fusion
  (3 shorter events, 0.1 us)
Async XLA Ops:
  7.2 86.9 %all-gather.5.cloned.1.call-start = ((), (), s32[]{:S(2)}) async-start(), calls=%async_computation.1 | async-start | bytes 5308416 | tf_op jit(solution)/shard_map/all_gather | solution.py:258
  28.1 22.3 %collective-permute-start.2 = (bf16[168,384]{1,0:T(8,128)(2,1)S(1)}, bf16[168,384]{1,0:T(8,128)(2,1)S(1)}, u32[]{:S(2)}, u32[]{:S(2)}) collective-permute-start(bf16[168,384]{1,0:T(8,128)(2,1)S(1)} %pad_maximum_fusion.2), channel_id=1, source_target_pairs={{0,16},{8,24},{16,272},{24,280},{256,0},{264,8},{272,256},{280,264... | collective-permute-start | bytes 387080 | tf_op jit(solution)/shard_map/ppermute | solution.py:263
  35.0 15.3 %collective-permute-start.3 = (bf16[168,384]{1,0:T(8,128)(2,1)S(1)}, bf16[168,384]{1,0:T(8,128)(2,1)S(1)}, u32[]{:S(2)}, u32[]{:S(2)}) collective-permute-start(bf16[168,384]{1,0:T(8,128)(2,1)S(1)} %pad_maximum_fusion.2), channel_id=1, source_target_pairs={{0,24},{8,16},{16,280},{24,272},{256,8},{264,0},{272,264},{280,256... | collective-permute-start | bytes 387080 | tf_op jit(solution)/shard_map/ppermute | solution.py:263
  41.5 25.3 %collective-permute-start = (bf16[168,384]{1,0:T(8,128)(2,1)S(1)}, bf16[168,384]{1,0:T(8,128)(2,1)S(1)}, u32[]{:S(2)}, u32[]{:S(2)}) collective-permute-start(bf16[168,384]{1,0:T(8,128)(2,1)S(1)} %pad_maximum_fusion.2), channel_id=1, source_target_pairs={{0,0},{8,8},{16,256},{24,264},{256,16},{264,24},{272,272},{280,280... | collective-permute-start | bytes 387080 | tf_op jit(solution)/shard_map/ppermute | solution.py:263
  44.3 22.5 %collective-permute-start.1 = (bf16[168,384]{1,0:T(8,128)(2,1)S(1)}, bf16[168,384]{1,0:T(8,128)(2,1)S(1)}, u32[]{:S(2)}, u32[]{:S(2)}) collective-permute-start(bf16[168,384]{1,0:T(8,128)(2,1)S(1)} %pad_maximum_fusion.2), channel_id=1, source_target_pairs={{0,8},{8,0},{16,264},{24,256},{256,24},{264,16},{272,280},{280,272... | collective-permute-start | bytes 387080 | tf_op jit(solution)/shard_map/ppermute | solution.py:263
  64.8 22.5 %copy-start.3 = (bf16[8,168,384]{2,1,0:T(8,128)(2,1)}, bf16[8,168,384]{2,1,0:T(8,128)(2,1)S(1)}, u32[]{:S(2)}) copy-start(bf16[8,168,384]{2,1,0:T(8,128)(2,1)S(1)} %all-gather.1) | copy-start | bytes 3096580
  64.8 19.9 %collective-permute-start.5 = (bf16[4,2,168,384]{3,2,1,0:T(8,128)(2,1)S(1)}, bf16[4,2,168,384]{3,2,1,0:T(8,128)(2,1)S(1)}, u32[]{:S(2)}, u32[]{:S(2)}) collective-permute-start(bf16[4,2,168,384]{3,2,1,0:T(8,128)(2,1)S(1)} %bitcast.19), channel_id=1, source_target_pairs={{0,1},{1,0},{2,3},{3,2},{4,5},{5,4},{6,7},{7,6},{8,9},{9,8},{10,11... | collective-permute-start | bytes 3096584 | tf_op jit(solution)/shard_map/ppermute | solution.py:268
  82.7 4.7 %copy-start.4 = (bf16[8,168,384]{2,1,0:T(8,128)(2,1)}, bf16[8,168,384]{2,1,0:T(8,128)(2,1)S(1)}, u32[]{:S(2)}) copy-start(bf16[8,168,384]{2,1,0:T(8,128)(2,1)S(1)} %all-gather) | copy-start | bytes 3096580
  82.7 4.7 %collective-permute-start.4 = (bf16[4,2,168,384]{3,2,1,0:T(8,128)(2,1)S(1)}, bf16[4,2,168,384]{3,2,1,0:T(8,128)(2,1)}, u32[]{:S(2)}, u32[]{:S(2)}) collective-permute-start(bf16[4,2,168,384]{3,2,1,0:T(8,128)(2,1)S(1)} %bitcast.21), channel_id=1, source_target_pairs={{0,1},{1,0},{2,3},{3,2},{4,5},{5,4},{6,7},{7,6},{8,9},{9,8},{10,11... | collective-permute-start | bytes 3096584 | tf_op jit(solution)/shard_map/ppermute | solution.py:266
  84.7 2.6 %copy-start.5 = (bf16[4,2,168,384]{3,2,1,0:T(8,128)(2,1)}, bf16[4,2,168,384]{3,2,1,0:T(8,128)(2,1)S(1)}, u32[]{:S(2)}) copy-start(bf16[4,2,168,384]{3,2,1,0:T(8,128)(2,1)S(1)} %collective-permute-done.5.far1) | copy-start | bytes 3096580
  94.1 0.9 copy-start
  94.9 0.9 copy-start.2
  95.9 22.5 %copy-start.1 = (f32[8,8,384]{2,1,0:T(8,128)S(1)}, f32[8,8,384]{2,1,0:T(8,128)}, u32[]{:S(2)}) copy-start(f32[8,8,384]{2,1,0:T(8,128)} %get-tuple-element.10.gain_ref) | copy-start | bytes 294916
  103.0 15.4 %collective-permute-start.6 = (bf16[656,384]{1,0:T(8,128)(2,1)S(1)}, bf16[656,384]{1,0:T(8,128)(2,1)S(1)}, u32[]{:S(2)}, u32[]{:S(2)}) collective-permute-start(bf16[656,384]{1,0:T(8,128)(2,1)S(1)} %first.1.own_ref), channel_id=1, source_target_pairs={{0,256},{256,0},{1,257},{257,1},{2,258},{258,2},{3,259},{259,3},{4... | collective-permute-start | bytes 1511432 | tf_op jit(solution)/shard_map/ppermute | solution.py:313
  126.2 5.9 %collective-permute-start.7 = (bf16[4,2,2,160,384]{4,3,2,1,0:T(8,128)(2,1)S(1)}, bf16[4,2,2,160,384]{4,3,2,1,0:T(8,128)(2,1)S(1)}, u32[]{:S(2)}, u32[]{:S(2)}) collective-permute-start(bf16[4,2,2,160,384]{4,3,2,1,0:T(8,128)(2,1)S(1)} %get-tuple-element.13), channel_id=1, source_target_pairs={{0,1},{1,0},{2,3},{3,2},{4,5},{5,4},{6,7},{7,6},{8,9},{9,8},{10,11... | collective-permute-start | bytes 5898248 | tf_op jit(solution)/shard_map/ppermute | solution.py:333
  162.5 16.3 %collective-permute-start.10 = (bf16[160,384]{1,0:T(8,128)(2,1)S(1)}, bf16[160,384]{1,0:T(8,128)(2,1)S(1)}, u32[]{:S(2)}, u32[]{:S(2)}) collective-permute-start(bf16[160,384]{1,0:T(8,128)(2,1)S(1)} %get-tuple-element.16), channel_id=1, source_target_pairs={{0,256},{8,264},{16,0},{24,8},{256,272},{264,280},{272,16},{280,24... | collective-permute-start | bytes 368648 | tf_op jit(solution)/shard_map/ppermute | solution.py:338
  167.7 11.2 %collective-permute-start.11 = (bf16[160,384]{1,0:T(8,128)(2,1)S(1)}, bf16[160,384]{1,0:T(8,128)(2,1)S(1)}, u32[]{:S(2)}, u32[]{:S(2)}) collective-permute-start(bf16[160,384]{1,0:T(8,128)(2,1)S(1)} %get-tuple-element.15), channel_id=1, source_target_pairs={{0,264},{8,256},{16,8},{24,0},{256,280},{264,272},{272,24},{280,16... | collective-permute-start | bytes 368648 | tf_op jit(solution)/shard_map/ppermute | solution.py:338
  169.6 10.9 %collective-permute-start.8 = (bf16[160,384]{1,0:T(8,128)(2,1)S(1)}, bf16[160,384]{1,0:T(8,128)(2,1)S(1)}, u32[]{:S(2)}, u32[]{:S(2)}) collective-permute-start(bf16[160,384]{1,0:T(8,128)(2,1)S(1)} %get-tuple-element.14), channel_id=1, source_target_pairs={{0,0},{8,8},{16,256},{24,264},{256,16},{264,24},{272,272},{280,280... | collective-permute-start | bytes 368648 | tf_op jit(solution)/shard_map/ppermute | solution.py:338
  173.2 9.8 %collective-permute-start.9 = (bf16[160,384]{1,0:T(8,128)(2,1)S(1)}, bf16[160,384]{1,0:T(8,128)(2,1)S(1)}, u32[]{:S(2)}, u32[]{:S(2)}) collective-permute-start(bf16[160,384]{1,0:T(8,128)(2,1)S(1)} %get-tuple-element.17), channel_id=1, source_target_pairs={{0,8},{8,0},{16,264},{24,256},{256,24},{264,16},{272,280},{280,272... | collective-permute-start | bytes 368648 | tf_op jit(solution)/shard_map/ppermute | solution.py:338
Sparse Core Ops, SparseCore 0:
  26.3 65.9 all-gather.4

commit v4 on v0

v4 whole, which is shorter than its diff:
```python
import functools

import jax
import jax.numpy as jnp
from jax import lax
from jax.experimental import pallas as pl
from jax.experimental.pallas import tpu as pltpu
from jax.sharding import Mesh
from jax.sharding import PartitionSpec as P

root_half = 0.7071067811865476
inv_root_tau = 0.3989422804014327
epsilon = 1e-06
narrow = jnp.bfloat16
wide = jnp.float32


def pairs_of(target):
    pairs = []
    for l in range(2):
        for h in range(4):
            new_l, new_high, new_low = target(l, h // 2, h % 2)
            pairs.append((l * 4 + h, new_l * 4 + new_high * 2 + new_low))
    return pairs


def gather_pairs(i, j):
    return pairs_of(lambda l, high, low: (high, l ^ i, low ^ j))


def scatter_pairs(i, j):
    return pairs_of(lambda l, high, low: (high ^ i, l, low ^ j))


def split3(value):
    high = value.astype(narrow).astype(wide)
    middle = (value - high).astype(narrow).astype(wide)
    return high, middle, value - high - middle


def ones_diagonal(rows, columns):
    row = lax.broadcasted_iota(jnp.int32, (rows, columns), 0)
    column = lax.broadcasted_iota(jnp.int32, (rows, columns), 1)
    return jnp.where(row == column, 1.0, 0.0).astype(narrow)


def halves(a, b):
    lane = lax.broadcasted_iota(jnp.int32, (a.shape[0], 128), 1) < 64
    a0, a1, a2 = (a[:, i : i + 128] for i in (0, 128, 256))
    b0, b1, b2 = (b[:, i : i + 128] for i in (0, 128, 256))
    a1_turned, a2_turned, b0_turned, b1_turned = (
        pltpu.roll(v, 64, 1) for v in (a1, a2, b0, b1)
    )
    left = [a0, jnp.where(lane, a1, b0_turned), jnp.where(lane, b0_turned, b1_turned)]
    right = [jnp.where(lane, a1_turned, a2_turned), jnp.where(lane, a2_turned, b1), b2]
    return left, right


def first_kernel(
    place_ref, own0, own1, far0, far1, panel_ref, x_ref, gain_ref, sums_ref,
    panel_s, sems, g_s, shift_s, table_s,
):
    blocks, rows_in, block = own0.shape[0] * own0.shape[1], own0.shape[2], own0.shape[3]
    tokens = x_ref.shape[0]
    rows, half = tokens // 2, block // 2
    first = place_ref[0] == 0
    flip = place_ref[1]

    def fetch(index):
        at = (index // 4 ^ flip) * 4 + index % 4
        return pltpu.make_async_copy(panel_ref.at[at], panel_s.at[index], sems.at[index])

    for index in range(blocks):
        fetch(index).start()

    def sides(own, far):
        a = jnp.where(first, own, far)
        b = jnp.where(first, far, own)
        left = jnp.concatenate([a[:, :half], b[:, :half]], axis=1)
        right = jnp.concatenate([a[:, half:], b[:, half:]], axis=1)
        return left, right

    means, spreads = [], []
    for part, (own, far) in enumerate(((own0, far0), (own1, far1))):
        at = slice(part * rows, (part + 1) * rows)
        total = jnp.zeros((rows, 128), wide)
        for index in range(blocks):
            x, j = index % 4, index // 4
            to = slice(index * block, (index + 1) * block)
            values, grads = sides(own[x, j, :rows], far[x, j, :rows])
            x_ref[at, to] = values
            g_s[at, to] = grads
            for lane in range(0, block, 128):
                total = total + values[:, lane : lane + 128].astype(wide)
            if part == 0:
                gain_ref[:, to], _ = sides(own[x, j, rows:].astype(wide), far[x, j, rows:].astype(wide))
        mean = jnp.sum(total, axis=1, keepdims=True) * (1.0 / (blocks * block))
        spread = jnp.zeros((rows, 128), wide)
        for lane in range(0, blocks * block, 128):
            shifted = x_ref[at, lane : lane + 128].astype(wide) - mean
            spread = spread + shifted * shifted
            shift_s[at, lane : lane + 128] = (shifted * gain_ref[:1, lane : lane + 128]).astype(narrow)
        means.append(mean)
        spreads.append(jnp.sum(spread, axis=1, keepdims=True))

    pre = act = gain_sum = None
    group = 4
    for start in range(0, blocks, group):
        for index in range(start, start + group):
            fetch(index).wait()
        to = slice(start * block, (start + group) * block)
        w_in = panel_s[start : start + group, :block].reshape(group * block, -1)
        w_out = jnp.concatenate([panel_s[start + i, block:] for i in range(group)], axis=1)
        p = jnp.dot(shift_s[:, to], w_in, preferred_element_type=wide)
        a = lax.dot_general(g_s[:, to], w_out, (((1,), (1,)), ((), ())), preferred_element_type=wide)
        v = jnp.dot(gain_ref[:, to].astype(narrow), w_in, preferred_element_type=wide)
        pre, act, gain_sum = (p, a, v) if pre is None else (pre + p, act + a, gain_sum + v)

    sums_ref[:tokens] = pre.astype(narrow)
    sums_ref[tokens : 2 * tokens] = act.astype(narrow)
    table_s[...] = jnp.zeros_like(table_s)
    for part in range(2):
        columns = split3(means[part]) + split3(spreads[part])
        lane = lax.broadcasted_iota(jnp.int32, (rows, 128), 1)
        table = jnp.zeros((rows, 128), wide)
        for index, column in enumerate(columns):
            table = jnp.where(lane == index, column, table)
        table_s[part * rows : (part + 1) * rows] = table.astype(narrow)
    lines = lax.dot_general(
        ones_diagonal(16, 128), table_s[...], (((1,), (1,)), ((), ())), preferred_element_type=wide
    )
    high = gain_sum[:1].astype(narrow).astype(wide)
    row = lax.broadcasted_iota(jnp.int32, lines.shape, 0)
    lines = jnp.where(row == 6, high, jnp.where(row == 7, gain_sum[:1] - high, lines))
    sums_ref[2 * tokens :] = lines.astype(narrow)


def second_kernel(
    features, place_ref, own_ref, far_ref, x_ref, gain_ref, panel_ref, keep_ref, send_ref
):
    tokens = x_ref.shape[0]
    blocks, block = panel_ref.shape[0], panel_ref.shape[1] // 2
    rows = tokens // 2

    def extras(ref):
        lines = ref[2 * tokens :]
        table = lax.dot_general(
            lines, ones_diagonal(16, 128), (((0,), (0,)), ((), ())), preferred_element_type=wide
        )[:tokens]
        center = table[:, 0:1] + table[:, 1:2] + table[:, 2:3]
        spread = table[:, 3:4] + table[:, 4:5] + table[:, 5:6]
        lines = lines.astype(wide)
        return center, spread, lines[6:7] + lines[7:8]

    mean_a, spread_a, gain_a = extras(own_ref)
    mean_b, spread_b, gain_b = extras(far_ref)
    gap = mean_a - mean_b
    mean = 0.5 * (mean_a + mean_b)
    spread = spread_a + spread_b + gap * gap * (features / 4)
    inverse = lax.rsqrt(spread / features + epsilon)
    total = own_ref[:tokens].astype(wide) + far_ref[:tokens].astype(wide)
    total = total + (mean_a - mean) * gain_a + (mean_b - mean) * gain_b
    preact = total * inverse
    act_grad = own_ref[tokens : 2 * tokens].astype(wide) + far_ref[tokens : 2 * tokens].astype(wide)
    bulk = 0.5 * (1.0 + lax.erf(preact * root_half))
    slope = bulk + preact * jnp.exp(-0.5 * preact * preact) * inv_root_tau
    activation = (preact * bulk).astype(narrow)
    d_pre = (act_grad * slope).astype(narrow)
    d_wide = d_pre.astype(wide)
    flat = inverse * jnp.sum(d_wide * (gain_a + gain_b), axis=1, keepdims=True) / features
    cross = inverse * inverse * jnp.sum(d_wide * preact, axis=1, keepdims=True) / features
    flat = flat - mean * cross

    first = place_ref[0] == 0
    flip = place_ref[1]
    group = 2
    for start in range(0, blocks, group):
        at = (start // 4 ^ flip) * 4 + start % 4
        w_in = panel_ref[pl.ds(at, group), :block].reshape(group * block, -1)
        w_out = jnp.concatenate([panel_ref[at + i, block:] for i in range(group)], axis=1)
        outs = jnp.dot(activation, w_out, preferred_element_type=wide)
        d_normed = lax.dot_general(
            d_pre, w_in, (((1,), (1,)), ((), ())), preferred_element_type=wide
        )
        to = slice(start * block, (start + group) * block)
        grads = inverse * (d_normed * gain_ref[:1, to]) - flat - x_ref[:, to].astype(wide) * cross
        for index in range(start, start + group):
            x, j = index % 4, index // 4
            own = slice((index - start) * block, (index - start + 1) * block)
            sides = halves(outs[:, own], grads[:, own])
            for lane in range(3):
                side0, side1 = (side[lane].astype(narrow) for side in sides)
                keep = jnp.where(first, side0, side1)
                send = jnp.where(first, side1, side0)
                for part in range(2):
                    keep_ref[x, part, j, :, lane * 128 : lane * 128 + 128] = keep[part * rows : (part + 1) * rows]
                    send_ref[x, part, j, :, lane * 128 : lane * 128 + 128] = send[part * rows : (part + 1) * rows]


def in_hbm(array):
    return pltpu.with_memory_space_constraint(array, pltpu.HBM)


def call(kernel, in_specs, out_shape, scratch_shapes, vmem, name):
    here = pl.BlockSpec(memory_space=pltpu.VMEM)
    specs = {"scalar": pl.BlockSpec(memory_space=pltpu.SMEM), "here": here, "any": pl.BlockSpec(memory_space=pl.ANY)}
    return pl.pallas_call(
        kernel,
        in_specs=[specs[spec] for spec in in_specs],
        out_specs=[here] * len(out_shape),
        out_shape=[jax.ShapeDtypeStruct(*shape) for shape in out_shape],
        scratch_shapes=scratch_shapes,
        compiler_params=pltpu.CompilerParams(vmem_limit_bytes=vmem * 2**20),
        name=name,
    )


def first_call(place, own0, own1, far0, far1, panels):
    blocks, twice, hidden = panels.shape
    block, rows = twice // 2, own0.shape[2] - 8
    tokens, width = 2 * rows, blocks * block
    return call(
        first_kernel,
        ["scalar", "here", "here", "here", "here", "any"],
        [((tokens, width), narrow), ((8, width), wide), ((2 * tokens + 16, hidden), narrow)],
        [
            pltpu.VMEM(panels.shape, narrow),
            pltpu.SemaphoreType.DMA((blocks,)),
            pltpu.VMEM((tokens, width), narrow),
            pltpu.VMEM((tokens, width), narrow),
            pltpu.VMEM((hidden, 128), narrow),
        ],
        30,
        "first",
    )(place, own0, own1, far0, far1, panels)


def second_call(features, place, sums, far_sums, values, gains, panels):
    block = panels.shape[1] // 2
    part = ((4, 2, 2, values.shape[0] // 2, block), narrow)
    return call(
        functools.partial(second_kernel, features),
        ["scalar", "here", "here", "here", "here", "here"],
        [part, part],
        [],
        30,
        "second",
    )(place, sums, far_sums, values, gains, panels)


def on_device(inputs, gain, w_in, w_out, grad_out):
    rows, piece = inputs.shape
    block = 2 * piece
    features = piece * lax.axis_size(("h", "x", "k"))
    other_core = [(0, 1), (1, 0)]
    place = jnp.stack([lax.axis_index("k"), lax.axis_index("h") % 2]).astype(jnp.int32)

    panels = lax.all_gather(jnp.concatenate([w_in, w_out], axis=0), "y", axis=0)

    gain_rows = jnp.broadcast_to(jnp.concatenate([gain, gain])[None, :], (8, block))
    pack = jnp.concatenate([jnp.concatenate([inputs, grad_out], axis=1), gain_rows], axis=0)
    near = [
        [lax.ppermute(pack, ("l", "h"), gather_pairs(i, j)) for j in range(2)] for i in range(2)
    ]
    own0 = lax.all_gather(jnp.stack(near[0]), "x", axis=0)
    far0 = lax.ppermute(own0, "k", other_core)
    own1 = lax.all_gather(jnp.stack(near[1]), "x", axis=0)
    far1 = lax.ppermute(own1, "k", other_core)

    values, gains, sums = first_call(place, own0, own1, far0, far1, in_hbm(panels))
    far_sums = lax.ppermute(sums, "l", other_core)
    keep, send = second_call(features, place, sums, far_sums, values, gains, panels)

    got = lax.ppermute(send, "k", other_core)
    total = (keep.astype(wide) + got.astype(wide)).astype(narrow)
    total = lax.all_to_all(total, "x", 0, 0)
    total = jnp.sum(total.astype(wide), axis=0).astype(narrow)
    shares = [
        lax.ppermute(total[i, j], ("l", "h"), scatter_pairs(i, j)).astype(wide)
        for i in range(2)
        for j in range(2)
    ]
    total = (shares[0] + shares[1] + shares[2] + shares[3]).astype(narrow)
    return (total[:, :piece], total[:, piece:])


def solution(mesh):
    fine = Mesh(mesh.devices.reshape(2, 8, 4, 4, 2), ("l", "y", "h", "x", "k"))
    row, col = ("l", "y"), ("h", "x", "k")
    in_specs = (P(row, col), P(col), P(row, col), P(col, row), P(row, col))
    out_specs = (P(row, col), P(row, col))
    return jax.shard_map(
        on_device, mesh=fine, in_specs=in_specs, out_specs=out_specs, check_vma=False
    )
```

time: 743 us -> 175 us (0.24)
  the two profiles are of different devices: /device:TPU:16 before, /device:TPU:64 now
where the time goes in v4:
time: 175 us; the launch traced here: 174 us
  blocking collectives  59.6 us (34%)
  starting transfers between devices  46.7 us (27%)
  waiting for transfers between devices  35 us (20%)
  between operations  14.2 us (8%)
  Pallas kernels  12.5 us (7%)
  other arithmetic  5.08 us (3%)
    all_to_all x1, blocking collectives, on_device(): total = lax.all_to_all(total, 'x', 0, 0)  29.3 us
    ppermute x4, starting transfers between devices, on_device(): lax.ppermute(pack, ('l', 'h'), gather_pairs(i, j))  19.5 us
    ppermute x4, starting transfers between devices, on_device(): lax.ppermute(total[i, j], ('l', 'h'), scatter_pairs(i, j)).astype(wide)  19.1 us
    all_gather x1, blocking collectives, on_device(): own0 = lax.all_gather(jnp.stack(near[0]), 'x', axis=0)  15.9 us
    all_gather x1, blocking collectives, on_device(): own1 = lax.all_gather(jnp.stack(near[1]), 'x', axis=0)  14.5 us
    ppermute x1, waiting for transfers between devices, on_device(): far_sums = lax.ppermute(sums, 'l', other_core)  12.8 us
    all_gather x1, waiting for transfers between devices, on_device(): panels = lax.all_gather(jnp.concatenate([w_in, w_out], axis=0), 'y', axis=0)  8.46 us
    pallas_call x1, Pallas kernels, first_call(): call(first_kernel, ['scalar', 'here', 'here', 'here', 'here', 'any'], [((...  8.27 us
  transfers between devices with their start and end apart: 13, of which 6 were waited for; matrix products, arithmetic and copies ran while one was open for 1% of the time, Pallas kernels for 0%

profile of v4, /device:TPU:64, one launch (start us, length us, event | category | flops | bytes accessed | tf_op | source)
XLA Modules:
  0.0 174.0 jit_solution(16418561561052141959)
XLA Ops:
  7.2 0.0 all-gather.5.cloned.1.call-start
  7.2 1.9 %pad_maximum_fusion = bf16[768,384]{1,0:T(8,128)(2,1)} fusion(bf16[384,384]{1,0:T(8,128)(2,1)} %param.8, bf16[384,384]{1,0:T(8,128)(2,1)} %param.7), kind=kLoop, calls=%fused_computation.1 | loop fusion | flops 1179648 | bytes 1179648 | tf_op jit(solution)/shard_map/concatenate | solution.py:258
  9.2 0.0 all-gather.5.cloned.1.call-update
  9.2 0.8 pad_maximum_fusion.4
  10.0 1.0 pad_maximum_fusion.3
  11.0 4.3 %collective-permute-start.3 = (bf16[168,384]{1,0:T(8,128)(2,1)S(1)}, bf16[168,384]{1,0:T(8,128)(2,1)S(1)}, u32[]{:S(2)}, u32[]{:S(2)}) collective-permute-start(bf16[168,384]{1,0:T(8,128)(2,1)S(1)} %pad_maximum_fusion.3), channel_id=1, source_target_pairs={{0,24},{8,16},{16,280},{24,272},{256,8},{264,0},{272,264},{280,256... | collective-permute-start | bytes 387080 | tf_op jit(solution)/shard_map/ppermute | solution.py:263
  15.3 8.2 %collective-permute-start.2 = (bf16[168,384]{1,0:T(8,128)(2,1)S(1)}, bf16[168,384]{1,0:T(8,128)(2,1)S(1)}, u32[]{:S(2)}, u32[]{:S(2)}) collective-permute-start(bf16[168,384]{1,0:T(8,128)(2,1)S(1)} %pad_maximum_fusion.3), channel_id=1, source_target_pairs={{0,16},{8,24},{16,272},{24,280},{256,0},{264,8},{272,256},{280,264... | collective-permute-start | bytes 387080 | tf_op jit(solution)/shard_map/ppermute | solution.py:263
  23.5 2.8 %collective-permute-start.1 = (bf16[168,384]{1,0:T(8,128)(2,1)S(1)}, bf16[168,384]{1,0:T(8,128)(2,1)S(1)}, u32[]{:S(2)}, u32[]{:S(2)}) collective-permute-start(bf16[168,384]{1,0:T(8,128)(2,1)S(1)} %pad_maximum_fusion.3), channel_id=1, source_target_pairs={{0,8},{8,0},{16,264},{24,256},{256,24},{264,16},{272,280},{280,272... | collective-permute-start | bytes 387080 | tf_op jit(solution)/shard_map/ppermute | solution.py:263
  26.4 4.2 %collective-permute-start = (bf16[168,384]{1,0:T(8,128)(2,1)S(1)}, bf16[168,384]{1,0:T(8,128)(2,1)S(1)}, u32[]{:S(2)}, u32[]{:S(2)}) collective-permute-start(bf16[168,384]{1,0:T(8,128)(2,1)S(1)} %pad_maximum_fusion.3), channel_id=1, source_target_pairs={{0,0},{8,8},{16,256},{24,264},{256,16},{264,24},{272,272},{280,280... | collective-permute-start | bytes 387080 | tf_op jit(solution)/shard_map/ppermute | solution.py:263
  30.6 0.0 collective-permute-done.3
  30.6 0.0 collective-permute-done.2
  30.6 14.5 %all-gather.1 = bf16[8,168,384]{2,1,0:T(8,128)(2,1)S(1)} all-gather(bf16[2,168,384]{2,1,0:T(8,128)(2,1)S(1)} %pad_maximum_fusion.2), channel_id=3, replica_groups=mesh['l'=2,'y'=8,'h'=4,'x'=4,'k'=2] {'x'}, dimensions={0}, use_global_device_ids=true | all-gather | bytes 1290240 | tf_op jit(solution)/shard_map/all_gather | solution.py:267
  45.1 1.9 %collective-permute-start.5 = (bf16[4,2,168,384]{3,2,1,0:T(8,128)(2,1)S(1)}, bf16[4,2,168,384]{3,2,1,0:T(8,128)(2,1)S(1)}, u32[]{:S(2)}, u32[]{:S(2)}) collective-permute-start(bf16[4,2,168,384]{3,2,1,0:T(8,128)(2,1)S(1)} %bitcast.21), channel_id=1, source_target_pairs={{0,1},{1,0},{2,3},{3,2},{4,5},{5,4},{6,7},{7,6},{8,9},{9,8},{10,11... | collective-permute-start | bytes 3096584 | tf_op jit(solution)/shard_map/ppermute | solution.py:268
  47.0 0.0 collective-permute-done.1
  47.0 0.0 collective-permute-done
  47.1 15.9 %all-gather = bf16[8,168,384]{2,1,0:T(8,128)(2,1)S(1)} all-gather(bf16[2,168,384]{2,1,0:T(8,128)(2,1)S(1)} %pad_maximum_fusion.1), channel_id=2, replica_groups=mesh['l'=2,'y'=8,'h'=4,'x'=4,'k'=2] {'x'}, dimensions={0}, use_global_device_ids=true | all-gather | bytes 1290240 | tf_op jit(solution)/shard_map/all_gather | solution.py:265
  63.0 1.9 %collective-permute-start.4 = (bf16[4,2,168,384]{3,2,1,0:T(8,128)(2,1)S(1)}, bf16[4,2,168,384]{3,2,1,0:T(8,128)(2,1)}, u32[]{:S(2)}, u32[]{:S(2)}) collective-permute-start(bf16[4,2,168,384]{3,2,1,0:T(8,128)(2,1)S(1)} %bitcast.23), channel_id=1, source_target_pairs={{0,1},{1,0},{2,3},{3,2},{4,5},{5,4},{6,7},{7,6},{8,9},{9,8},{10,11... | collective-permute-start | bytes 3096584 | tf_op jit(solution)/shard_map/ppermute | solution.py:266
  64.9 0.1 pad_add_fusion.place_ref
  65.0 0.0 collective-permute-done.5.far1
  65.0 2.6 %collective-permute-done.4.far0 = bf16[4,2,168,384]{3,2,1,0:T(8,128)(2,1)} collective-permute-done((bf16[4,2,168,384]{3,2,1,0:T(8,128)(2,1)S(1)}, bf16[4,2,168,384]{3,2,1,0:T(8,128)(2,1)}, u32[]{:S(2)}, u32[]{:S(2)}) %collective-permute-start.4) | collective-permute-done | bytes 1032224 | tf_op jit(solution)/shard_map/ppermute | solution.py:266
  67.6 8.5 %all-gather.5.cloned.1.call-done = bf16[6144,384]{1,0:T(8,128)(2,1)} async-done(((bf16[768,384]{1,0:T(8,128)(2,1)}), bf16[6144,384]{1,0:T(8,128)(2,1)}) %all-gather.5.cloned.1.call-update) | async-done | bytes 4718608 | tf_op jit(solution)/shard_map/all_gather | solution.py:258
  76.1 0.0 slice-start
  76.1 0.0 slice-start.1
  76.1 8.3 %first.1 = (bf16[320,3072]{1,0:T(8,128)(2,1)S(1)}, f32[8,3072]{1,0:T(8,128)S(1)}, bf16[656,384]{1,0:T(8,128)(2,1)S(1)}) custom-call(s32[2]{0:T(128)S(1)} %pad_add_fusion.place_ref, bf16[4,2,168,384]{3,2,1,0:T(8,128)(2,1)S(1)} %bitcast.24, bf16[4,2,168,384]{3,2,1,0:T(8,128)(2,1)S(1)} %bitcast.22, bf16[4,2,168,384]{3,2,1,0:T(8,128)(2,1)} %collective-permute-done.4.far0, ...), custom_call_target="tpu_custom_call" | custom-call | tf_op jit(solution)/shard_map/first/pallas_call | solution.py:222
  84.4 2.3 %collective-permute-start.6 = (bf16[656,384]{1,0:T(8,128)(2,1)S(1)}, bf16[656,384]{1,0:T(8,128)(2,1)S(1)}, u32[]{:S(2)}, u32[]{:S(2)}) collective-permute-start(bf16[656,384]{1,0:T(8,128)(2,1)S(1)} %get-tuple-element.7.own_ref), channel_id=1, source_target_pairs={{0,256},{256,0},{1,257},{257,1},{2,258},{258,2},{3,259},{259,3},{4... | collective-permute-start | bytes 1511432 | tf_op jit(solution)/shard_map/ppermute | solution.py:271
  86.7 12.8 %collective-permute-done.6.far_ref = bf16[656,384]{1,0:T(8,128)(2,1)S(1)} collective-permute-done((bf16[656,384]{1,0:T(8,128)(2,1)S(1)}, bf16[656,384]{1,0:T(8,128)(2,1)S(1)}, u32[]{:S(2)}, u32[]{:S(2)}) %collective-permute-start.6) | collective-permute-done | bytes 503840 | tf_op jit(solution)/shard_map/ppermute | solution.py:271
  99.5 0.0 slice-done
  99.5 0.0 slice-done.1
  99.5 4.2 %second.1 = (bf16[4,2,2,160,384]{4,3,2,1,0:T(8,128)(2,1)S(1)}, bf16[4,2,2,160,384]{4,3,2,1,0:T(8,128)(2,1)S(1)}) custom-call(s32[2]{0:T(128)S(1)} %pad_add_fusion.place_ref, bf16[656,384]{1,0:T(8,128)(2,1)S(1)} %get-tuple-element.7.own_ref, bf16[656,384]{1,0:T(8,128)(2,1)S(1)} %collective-permute-done.6.far_ref, ...), custom_call_target="tpu_custom_call" | custom-call | tf_op jit(solution)/shard_map/second/pallas_call | solution.py:241
  103.7 1.9 %collective-permute-start.7 = (bf16[4,2,2,160,384]{4,3,2,1,0:T(8,128)(2,1)S(1)}, bf16[4,2,2,160,384]{4,3,2,1,0:T(8,128)(2,1)S(1)}, u32[]{:S(2)}, u32[]{:S(2)}) collective-permute-start(bf16[4,2,2,160,384]{4,3,2,1,0:T(8,128)(2,1)S(1)} %get-tuple-element.11), channel_id=1, source_target_pairs={{0,1},{1,0},{2,3},{3,2},{4,5},{5,4},{6,7},{7,6},{8,9},{9,8},{10,11... | collective-permute-start | bytes 5898248 | tf_op jit(solution)/shard_map/ppermute | solution.py:274
  105.7 3.9 %collective-permute-done.7 = bf16[4,2,2,160,384]{4,3,2,1,0:T(8,128)(2,1)S(1)} collective-permute-done((bf16[4,2,2,160,384]{4,3,2,1,0:T(8,128)(2,1)S(1)}, bf16[4,2,2,160,384]{4,3,2,1,0:T(8,128)(2,1)S(1)}, u32[]{:S(2)}, u32[]{:S(2)}) %collective-permute-start.7) | collective-permute-done | bytes 1966112 | tf_op jit(solution)/shard_map/ppermute | solution.py:274
  109.6 0.5 add_convert_fusion
  110.1 29.3 %all_to_all.5 = bf16[4,2,2,160,384]{4,3,2,1,0:T(8,128)(2,1)S(1)} all-to-all(bf16[4,2,2,160,384]{4,3,2,1,0:T(8,128)(2,1)S(1)} %add_convert_fusion), channel_id=1, replica_groups=mesh['l'=2,'y'=8,'h'=4,'x'=4,'k'=2] {'x'}, dimensions={0} | all-to-all | bytes 3932160 | tf_op jit(solution)/shard_map/all_to_all | solution.py:276
  139.4 0.5 reduce_sum.12
  140.0 0.1 slice_bitcast_fusion.3
  140.0 6.9 %collective-permute-start.8 = (bf16[160,384]{1,0:T(8,128)(2,1)S(1)}, bf16[160,384]{1,0:T(8,128)(2,1)S(1)}, u32[]{:S(2)}, u32[]{:S(2)}) collective-permute-start(bf16[160,384]{1,0:T(8,128)(2,1)S(1)} %get-tuple-element.12), channel_id=1, source_target_pairs={{0,0},{8,8},{16,256},{24,264},{256,16},{264,24},{272,272},{280,280... | collective-permute-start | bytes 368648 | tf_op jit(solution)/shard_map/ppermute | solution.py:279
  147.0 1.9 %collective-permute-start.11 = (bf16[160,384]{1,0:T(8,128)(2,1)S(1)}, bf16[160,384]{1,0:T(8,128)(2,1)S(1)}, u32[]{:S(2)}, u32[]{:S(2)}) collective-permute-start(bf16[160,384]{1,0:T(8,128)(2,1)S(1)} %get-tuple-element.13), channel_id=1, source_target_pairs={{0,264},{8,256},{16,8},{24,0},{256,280},{264,272},{272,24},{280,16... | collective-permute-start | bytes 368648 | tf_op jit(solution)/shard_map/ppermute | solution.py:279
  148.9 4.6 %collective-permute-start.10 = (bf16[160,384]{1,0:T(8,128)(2,1)S(1)}, bf16[160,384]{1,0:T(8,128)(2,1)S(1)}, u32[]{:S(2)}, u32[]{:S(2)}) collective-permute-start(bf16[160,384]{1,0:T(8,128)(2,1)S(1)} %get-tuple-element.14), channel_id=1, source_target_pairs={{0,256},{8,264},{16,0},{24,8},{256,272},{264,280},{272,16},{280,24... | collective-permute-start | bytes 368648 | tf_op jit(solution)/shard_map/ppermute | solution.py:279
  153.5 5.7 %collective-permute-start.9 = (bf16[160,384]{1,0:T(8,128)(2,1)S(1)}, bf16[160,384]{1,0:T(8,128)(2,1)S(1)}, u32[]{:S(2)}, u32[]{:S(2)}) collective-permute-start(bf16[160,384]{1,0:T(8,128)(2,1)S(1)} %get-tuple-element.15), channel_id=1, source_target_pairs={{0,8},{8,0},{16,264},{24,256},{256,24},{264,16},{272,280},{280,272... | collective-permute-start | bytes 368648 | tf_op jit(solution)/shard_map/ppermute | solution.py:279
  159.2 0.0 collective-permute-done.8
  159.2 0.0 collective-permute-done.11
  159.2 2.5 %collective-permute-done.10 = bf16[160,384]{1,0:T(8,128)(2,1)S(1)} collective-permute-done((bf16[160,384]{1,0:T(8,128)(2,1)S(1)}, bf16[160,384]{1,0:T(8,128)(2,1)S(1)}, u32[]{:S(2)}, u32[]{:S(2)}) %collective-permute-start.10) | collective-permute-done | bytes 122912 | tf_op jit(solution)/shard_map/ppermute | solution.py:279
  161.7 4.6 %collective-permute-done.9 = bf16[160,384]{1,0:T(8,128)(2,1)S(1)} collective-permute-done((bf16[160,384]{1,0:T(8,128)(2,1)S(1)}, bf16[160,384]{1,0:T(8,128)(2,1)S(1)}, u32[]{:S(2)}, u32[]{:S(2)}) %collective-permute-start.9) | collective-permute-done | bytes 122912 | tf_op jit(solution)/shard_map/ppermute | solution.py:279
  166.3 0.1 add_convert_fusion.1
  166.4 0.7 fusion
  (4 shorter events, 0.1 us)
Async XLA Ops:
  7.2 68.9 %all-gather.5.cloned.1.call-start = ((), (), s32[]{:S(2)}) async-start(), calls=%async_computation.1 | async-start | bytes 5308416 | tf_op jit(solution)/shard_map/all_gather | solution.py:258
  11.0 19.6 %collective-permute-start.3 = (bf16[168,384]{1,0:T(8,128)(2,1)S(1)}, bf16[168,384]{1,0:T(8,128)(2,1)S(1)}, u32[]{:S(2)}, u32[]{:S(2)}) collective-permute-start(bf16[168,384]{1,0:T(8,128)(2,1)S(1)} %pad_maximum_fusion.3), channel_id=1, source_target_pairs={{0,24},{8,16},{16,280},{24,272},{256,8},{264,0},{272,264},{280,256... | collective-permute-start | bytes 387080 | tf_op jit(solution)/shard_map/ppermute | solution.py:263
  15.3 15.3 %collective-permute-start.2 = (bf16[168,384]{1,0:T(8,128)(2,1)S(1)}, bf16[168,384]{1,0:T(8,128)(2,1)S(1)}, u32[]{:S(2)}, u32[]{:S(2)}) collective-permute-start(bf16[168,384]{1,0:T(8,128)(2,1)S(1)} %pad_maximum_fusion.3), channel_id=1, source_target_pairs={{0,16},{8,24},{16,272},{24,280},{256,0},{264,8},{272,256},{280,264... | collective-permute-start | bytes 387080 | tf_op jit(solution)/shard_map/ppermute | solution.py:263
  23.5 23.5 %collective-permute-start.1 = (bf16[168,384]{1,0:T(8,128)(2,1)S(1)}, bf16[168,384]{1,0:T(8,128)(2,1)S(1)}, u32[]{:S(2)}, u32[]{:S(2)}) collective-permute-start(bf16[168,384]{1,0:T(8,128)(2,1)S(1)} %pad_maximum_fusion.3), channel_id=1, source_target_pairs={{0,8},{8,0},{16,264},{24,256},{256,24},{264,16},{272,280},{280,272... | collective-permute-start | bytes 387080 | tf_op jit(solution)/shard_map/ppermute | solution.py:263
  26.4 20.7 %collective-permute-start = (bf16[168,384]{1,0:T(8,128)(2,1)S(1)}, bf16[168,384]{1,0:T(8,128)(2,1)S(1)}, u32[]{:S(2)}, u32[]{:S(2)}) collective-permute-start(bf16[168,384]{1,0:T(8,128)(2,1)S(1)} %pad_maximum_fusion.3), channel_id=1, source_target_pairs={{0,0},{8,8},{16,256},{24,264},{256,16},{264,24},{272,272},{280,280... | collective-permute-start | bytes 387080 | tf_op jit(solution)/shard_map/ppermute | solution.py:263
  45.1 19.9 %collective-permute-start.5 = (bf16[4,2,168,384]{3,2,1,0:T(8,128)(2,1)S(1)}, bf16[4,2,168,384]{3,2,1,0:T(8,128)(2,1)S(1)}, u32[]{:S(2)}, u32[]{:S(2)}) collective-permute-start(bf16[4,2,168,384]{3,2,1,0:T(8,128)(2,1)S(1)} %bitcast.21), channel_id=1, source_target_pairs={{0,1},{1,0},{2,3},{3,2},{4,5},{5,4},{6,7},{7,6},{8,9},{9,8},{10,11... | collective-permute-start | bytes 3096584 | tf_op jit(solution)/shard_map/ppermute | solution.py:268
  63.0 4.7 %collective-permute-start.4 = (bf16[4,2,168,384]{3,2,1,0:T(8,128)(2,1)S(1)}, bf16[4,2,168,384]{3,2,1,0:T(8,128)(2,1)}, u32[]{:S(2)}, u32[]{:S(2)}) collective-permute-start(bf16[4,2,168,384]{3,2,1,0:T(8,128)(2,1)S(1)} %bitcast.23), channel_id=1, source_target_pairs={{0,1},{1,0},{2,3},{3,2},{4,5},{5,4},{6,7},{7,6},{8,9},{9,8},{10,11... | collective-permute-start | bytes 3096584 | tf_op jit(solution)/shard_map/ppermute | solution.py:266
  76.1 23.4 %slice-start = ((s8[4718592]{0:T(1024)(128)(4,1)}), s8[4194304]{0:T(1024)(128)(4,1)S(1)}, s32[]{:S(2)}) async-start(s8[4718592]{0:T(1024)(128)(4,1)} %bitcast.18), calls=%async_computation.2 | async-start | bytes 8388608
  76.1 23.4 %slice-start.1 = ((s8[4718592]{0:T(1024)(128)(4,1)}), s8[524288]{0:T(1024)(128)(4,1)S(1)}, s32[]{:S(2)}) async-start(s8[4718592]{0:T(1024)(128)(4,1)} %bitcast.18), calls=%async_computation.3 | async-start | bytes 1048576
  84.4 15.1 %collective-permute-start.6 = (bf16[656,384]{1,0:T(8,128)(2,1)S(1)}, bf16[656,384]{1,0:T(8,128)(2,1)S(1)}, u32[]{:S(2)}, u32[]{:S(2)}) collective-permute-start(bf16[656,384]{1,0:T(8,128)(2,1)S(1)} %get-tuple-element.7.own_ref), channel_id=1, source_target_pairs={{0,256},{256,0},{1,257},{257,1},{2,258},{258,2},{3,259},{259,3},{4... | collective-permute-start | bytes 1511432 | tf_op jit(solution)/shard_map/ppermute | solution.py:271
  103.7 5.9 %collective-permute-start.7 = (bf16[4,2,2,160,384]{4,3,2,1,0:T(8,128)(2,1)S(1)}, bf16[4,2,2,160,384]{4,3,2,1,0:T(8,128)(2,1)S(1)}, u32[]{:S(2)}, u32[]{:S(2)}) collective-permute-start(bf16[4,2,2,160,384]{4,3,2,1,0:T(8,128)(2,1)S(1)} %get-tuple-element.11), channel_id=1, source_target_pairs={{0,1},{1,0},{2,3},{3,2},{4,5},{5,4},{6,7},{7,6},{8,9},{9,8},{10,11... | collective-permute-start | bytes 5898248 | tf_op jit(solution)/shard_map/ppermute | solution.py:274
  140.0 19.2 %collective-permute-start.8 = (bf16[160,384]{1,0:T(8,128)(2,1)S(1)}, bf16[160,384]{1,0:T(8,128)(2,1)S(1)}, u32[]{:S(2)}, u32[]{:S(2)}) collective-permute-start(bf16[160,384]{1,0:T(8,128)(2,1)S(1)} %get-tuple-element.12), channel_id=1, source_target_pairs={{0,0},{8,8},{16,256},{24,264},{256,16},{264,24},{272,272},{280,280... | collective-permute-start | bytes 368648 | tf_op jit(solution)/shard_map/ppermute | solution.py:279
  147.0 12.3 %collective-permute-start.11 = (bf16[160,384]{1,0:T(8,128)(2,1)S(1)}, bf16[160,384]{1,0:T(8,128)(2,1)S(1)}, u32[]{:S(2)}, u32[]{:S(2)}) collective-permute-start(bf16[160,384]{1,0:T(8,128)(2,1)S(1)} %get-tuple-element.13), channel_id=1, source_target_pairs={{0,264},{8,256},{16,8},{24,0},{256,280},{264,272},{272,24},{280,16... | collective-permute-start | bytes 368648 | tf_op jit(solution)/shard_map/ppermute | solution.py:279
  148.9 12.8 %collective-permute-start.10 = (bf16[160,384]{1,0:T(8,128)(2,1)S(1)}, bf16[160,384]{1,0:T(8,128)(2,1)S(1)}, u32[]{:S(2)}, u32[]{:S(2)}) collective-permute-start(bf16[160,384]{1,0:T(8,128)(2,1)S(1)} %get-tuple-element.14), channel_id=1, source_target_pairs={{0,256},{8,264},{16,0},{24,8},{256,272},{264,280},{272,16},{280,24... | collective-permute-start | bytes 368648 | tf_op jit(solution)/shard_map/ppermute | solution.py:279
  153.5 12.8 %collective-permute-start.9 = (bf16[160,384]{1,0:T(8,128)(2,1)S(1)}, bf16[160,384]{1,0:T(8,128)(2,1)S(1)}, u32[]{:S(2)}, u32[]{:S(2)}) collective-permute-start(bf16[160,384]{1,0:T(8,128)(2,1)S(1)} %get-tuple-element.15), channel_id=1, source_target_pairs={{0,8},{8,0},{16,264},{24,256},{256,24},{264,16},{272,280},{280,272... | collective-permute-start | bytes 368648 | tf_op jit(solution)/shard_map/ppermute | solution.py:279
Sparse Core Ops, SparseCore 0:
  10.1 65.9 all-gather.4

commit v5 on v4

--- a/solution.py
+++ b/solution.py
@@ -56,22 +56,13 @@
     return left, right
 
 
-def first_kernel(
-    place_ref, own0, own1, far0, far1, panel_ref, x_ref, gain_ref, sums_ref,
-    panel_s, sems, g_s, shift_s, table_s,
+def merge_kernel(
+    place_ref, own0, own1, far0, far1, x_ref, shift_ref, g_ref, gain_ref, table_ref
 ):
-    blocks, rows_in, block = own0.shape[0] * own0.shape[1], own0.shape[2], own0.shape[3]
+    blocks, block = own0.shape[0] * own0.shape[1], own0.shape[3]
     tokens = x_ref.shape[0]
     rows, half = tokens // 2, block // 2
     first = place_ref[0] == 0
-    flip = place_ref[1]
-
-    def fetch(index):
-        at = (index // 4 ^ flip) * 4 + index % 4
-        return pltpu.make_async_copy(panel_ref.at[at], panel_s.at[index], sems.at[index])
-
-    for index in range(blocks):
-        fetch(index).start()
 
     def sides(own, far):
         a = jnp.where(first, own, far)
@@ -80,7 +71,7 @@
         right = jnp.concatenate([a[:, half:], b[:, half:]], axis=1)
         return left, right
 
-    means, spreads = [], []
+    table_ref[...] = jnp.zeros_like(table_ref)
     for part, (own, far) in enumerate(((own0, far0), (own1, far1))):
         at = slice(part * rows, (part + 1) * rows)
         total = jnp.zeros((rows, 128), wide)
@@ -89,7 +80,8 @@
             to = slice(index * block, (index + 1) * block)
             values, grads = sides(own[x, j, :rows], far[x, j, :rows])
             x_ref[at, to] = values
-            g_s[at, to] = grads
+            wide_to = slice(index % 2 * block, (index % 2 + 1) * block)
+            g_ref[index // 2, at, wide_to] = grads
             for lane in range(0, block, 128):
                 total = total + values[:, lane : lane + 128].astype(wide)
             if part == 0:
@@ -99,35 +91,56 @@
         for lane in range(0, blocks * block, 128):
             shifted = x_ref[at, lane : lane + 128].astype(wide) - mean
             spread = spread + shifted * shifted
-            shift_s[at, lane : lane + 128] = (shifted * gain_ref[:1, lane : lane + 128]).astype(narrow)
-        means.append(mean)
-        spreads.append(jnp.sum(spread, axis=1, keepdims=True))
-
-    pre = act = gain_sum = None
-    group = 4
-    for start in range(0, blocks, group):
-        for index in range(start, start + group):
-            fetch(index).wait()
-        to = slice(start * block, (start + group) * block)
-        w_in = panel_s[start : start + group, :block].reshape(group * block, -1)
-        w_out = jnp.concatenate([panel_s[start + i, block:] for i in range(group)], axis=1)
-        p = jnp.dot(shift_s[:, to], w_in, preferred_element_type=wide)
-        a = lax.dot_general(g_s[:, to], w_out, (((1,), (1,)), ((), ())), preferred_element_type=wide)
-        v = jnp.dot(gain_ref[:, to].astype(narrow), w_in, preferred_element_type=wide)
-        pre, act, gain_sum = (p, a, v) if pre is None else (pre + p, act + a, gain_sum + v)
-
-    sums_ref[:tokens] = pre.astype(narrow)
-    sums_ref[tokens : 2 * tokens] = act.astype(narrow)
-    table_s[...] = jnp.zeros_like(table_s)
-    for part in range(2):
-        columns = split3(means[part]) + split3(spreads[part])
+            pair, to = lane // (2 * block), lane % (2 * block)
+            shift_ref[pair, at, to : to + 128] = (shifted * gain_ref[:1, lane : lane + 128]).astype(narrow)
+        columns = split3(mean) + split3(jnp.sum(spread, axis=1, keepdims=True))
         lane = lax.broadcasted_iota(jnp.int32, (rows, 128), 1)
         table = jnp.zeros((rows, 128), wide)
         for index, column in enumerate(columns):
             table = jnp.where(lane == index, column, table)
-        table_s[part * rows : (part + 1) * rows] = table.astype(narrow)
+        table_ref[at] = table.astype(narrow)
+
+
+def first_kernel(
+    place_ref, gain_ref, table_ref, shift_ref, g_ref, panel_ref, sums_ref,
+    shift_s, g_s, panel_s, sems,
+):
+    pairs, tokens, width = shift_ref.shape
+    block = width // 2
+    flip = place_ref[1]
+
+    def fetch(pair):
+        at = (pair // 2 ^ flip) * 2 + pair % 2
+        moves = (
+            (shift_ref.at[pair], shift_s.at[pair]),
+            (g_ref.at[pair], g_s.at[pair]),
+            (panel_ref.at[pl.ds(at * 2, 2)], panel_s.at[pair]),
+        )
+        return [
+            pltpu.make_async_copy(source, target, sems.at[pair, i])
+            for i, (source, target) in enumerate(moves)
+        ]
+
+    for pair in range(pairs):
+        for copy in fetch(pair):
+            copy.start()
+
+    pre = act = gain_sum = None
+    for pair in range(pairs):
+        for copy in fetch(pair):
+            copy.wait()
+        to = slice(pair * width, (pair + 1) * width)
+        w_in = panel_s[pair, :, :block].reshape(width, -1)
+        w_out = jnp.concatenate([panel_s[pair, i, block:] for i in range(2)], axis=1)
+        p = jnp.dot(shift_s[pair], w_in, preferred_element_type=wide)
+        a = lax.dot_general(g_s[pair], w_out, (((1,), (1,)), ((), ())), preferred_element_type=wide)
+        v = jnp.dot(gain_ref[:, to].astype(narrow), w_in, preferred_element_type=wide)
+        pre, act, gain_sum = (p, a, v) if pre is None else (pre + p, act + a, gain_sum + v)
+
+    sums_ref[:tokens] = pre.astype(narrow)
+    sums_ref[tokens : 2 * tokens] = act.astype(narrow)
     lines = lax.dot_general(
-        ones_diagonal(16, 128), table_s[...], (((1,), (1,)), ((), ())), preferred_element_type=wide
+        ones_diagonal(16, 128), table_ref[...], (((1,), (1,)), ((), ())), preferred_element_type=wide
     )
     high = gain_sum[:1].astype(narrow).astype(wide)
     row = lax.broadcasted_iota(jnp.int32, lines.shape, 0)
@@ -136,7 +149,7 @@
 
 
 def second_kernel(
-    features, place_ref, own_ref, far_ref, x_ref, gain_ref, panel_ref, keep_ref, send_ref
+    features, place_ref, own_ref, far_ref, x_ref, gain_ref, panel_ref, *out_refs
 ):
     tokens = x_ref.shape[0]
     blocks, block = panel_ref.shape[0], panel_ref.shape[1] // 2
@@ -192,9 +205,12 @@
                 side0, side1 = (side[lane].astype(narrow) for side in sides)
                 keep = jnp.where(first, side0, side1)
                 send = jnp.where(first, side1, side0)
+                to = slice(lane * 128, lane * 128 + 128)
                 for part in range(2):
-                    keep_ref[x, part, j, :, lane * 128 : lane * 128 + 128] = keep[part * rows : (part + 1) * rows]
-                    send_ref[x, part, j, :, lane * 128 : lane * 128 + 128] = send[part * rows : (part + 1) * rows]
+                    at = slice(part * rows, (part + 1) * rows)
+                    target = x if part == 0 else (x - place_ref[2]) & 3
+                    out_refs[part][target, j, :, to] = keep[at]
+                    out_refs[2 + part][target, j, :, to] = send[at]
 
 
 def in_hbm(array):
@@ -208,40 +224,58 @@
         kernel,
         in_specs=[specs[spec] for spec in in_specs],
         out_specs=[here] * len(out_shape),
-        out_shape=[jax.ShapeDtypeStruct(*shape) for shape in out_shape],
+        out_shape=out_shape,
         scratch_shapes=scratch_shapes,
         compiler_params=pltpu.CompilerParams(vmem_limit_bytes=vmem * 2**20),
         name=name,
     )
 
 
-def first_call(place, own0, own1, far0, far1, panels):
+def merge_call(place, own0, own1, far0, far1, hidden):
+    blocks, block = own0.shape[0] * own0.shape[1], own0.shape[3]
+    tokens, width = 2 * (own0.shape[2] - 8), blocks * block
+    return call(
+        merge_kernel,
+        ["scalar", "here", "here", "here", "here"],
+        [
+            pltpu.HBM((tokens, width), narrow),
+            pltpu.HBM((blocks // 2, tokens, 2 * block), narrow),
+            pltpu.HBM((blocks // 2, tokens, 2 * block), narrow),
+            jax.ShapeDtypeStruct((8, width), wide),
+            jax.ShapeDtypeStruct((hidden, 128), narrow),
+        ],
+        [],
+        30,
+        "merge",
+    )(place, own0, own1, far0, far1)
+
+
+def first_call(place, shifted, grads, gains, table, panels):
     blocks, twice, hidden = panels.shape
-    block, rows = twice // 2, own0.shape[2] - 8
-    tokens, width = 2 * rows, blocks * block
-    return call(
+    pairs, tokens, width = shifted.shape
+    (sums,) = call(
         first_kernel,
-        ["scalar", "here", "here", "here", "here", "any"],
-        [((tokens, width), narrow), ((8, width), wide), ((2 * tokens + 16, hidden), narrow)],
+        ["scalar", "here", "here", "any", "any", "any"],
+        [jax.ShapeDtypeStruct((2 * tokens + 16, hidden), narrow)],
         [
-            pltpu.VMEM(panels.shape, narrow),
-            pltpu.SemaphoreType.DMA((blocks,)),
-            pltpu.VMEM((tokens, width), narrow),
-            pltpu.VMEM((tokens, width), narrow),
-            pltpu.VMEM((hidden, 128), narrow),
+            pltpu.VMEM(shifted.shape, narrow),
+            pltpu.VMEM(grads.shape, narrow),
+            pltpu.VMEM((pairs, blocks // pairs, twice, hidden), narrow),
+            pltpu.SemaphoreType.DMA((pairs, 3)),
         ],
         30,
         "first",
-    )(place, own0, own1, far0, far1, panels)
+    )(place, gains, table, in_hbm(shifted), in_hbm(grads), in_hbm(panels))
+    return sums
 
 
 def second_call(features, place, sums, far_sums, values, gains, panels):
     block = panels.shape[1] // 2
-    part = ((4, 2, 2, values.shape[0] // 2, block), narrow)
+    part = jax.ShapeDtypeStruct((4, 2, values.shape[0] // 2, block), narrow)
     return call(
         functools.partial(second_kernel, features),
         ["scalar", "here", "here", "here", "here", "here"],
-        [part, part],
+        [part] * 4,
         [],
         30,
         "second",
@@ -253,7 +287,7 @@
     block = 2 * piece
     features = piece * lax.axis_size(("h", "x", "k"))
     other_core = [(0, 1), (1, 0)]
-    place = jnp.stack([lax.axis_index("k"), lax.axis_index("h") % 2]).astype(jnp.int32)
+    place = jnp.stack([lax.axis_index("k"), lax.axis_index("h") % 2, lax.axis_index("x")]).astype(jnp.int32)
 
     panels = lax.all_gather(jnp.concatenate([w_in, w_out], axis=0), "y", axis=0)
 
@@ -267,19 +301,24 @@
     own1 = lax.all_gather(jnp.stack(near[1]), "x", axis=0)
     far1 = lax.ppermute(own1, "k", other_core)
 
-    values, gains, sums = first_call(place, own0, own1, far0, far1, in_hbm(panels))
+    values, shifted, grads, gains, table = merge_call(place, own0, own1, far0, far1, w_in.shape[1])
+    sums = first_call(place, shifted, grads, gains, table, panels)
     far_sums = lax.ppermute(sums, "l", other_core)
-    keep, send = second_call(features, place, sums, far_sums, values, gains, panels)
-
-    got = lax.ppermute(send, "k", other_core)
-    total = (keep.astype(wide) + got.astype(wide)).astype(narrow)
-    total = lax.all_to_all(total, "x", 0, 0)
-    total = jnp.sum(total.astype(wide), axis=0).astype(narrow)
-    shares = [
-        lax.ppermute(total[i, j], ("l", "h"), scatter_pairs(i, j)).astype(wide)
-        for i in range(2)
-        for j in range(2)
+    outs = second_call(features, place, sums, far_sums, values, gains, panels)
+
+    got = [lax.ppermute(send, "k", other_core) for send in outs[2:]]
+    def add(a, b):
+        return (a.astype(wide) + b.astype(wide)).astype(narrow)
+
+    first = lax.all_to_all(add(outs[0], got[0]), "x", 0, 0)
+    second = [add(outs[1][d], got[1][d]) for d in range(4)]
+    second = [second[0]] + [
+        lax.ppermute(second[d], "x", [(x, (x + d) % 4) for x in range(4)]) for d in (1, 3, 2)
     ]
+    shares = []
+    for i, parts in enumerate(([first[x] for x in range(4)], second)):
+        part = sum(part.astype(wide) for part in parts).astype(narrow)
+        shares += [lax.ppermute(part[j], ("l", "h"), scatter_pairs(i, j)).astype(wide) for j in range(2)]
     total = (shares[0] + shares[1] + shares[2] + shares[3]).astype(narrow)
     return (total[:, :piece], total[:, piece:])
 

time: 175 us -> 162 us (0.926)
  blocking collectives: 59.6 us -> 30.4 us
  starting transfers between devices: 46.7 us -> 65.3 us
  waiting for transfers between devices: 35 us -> 26.7 us
  Pallas kernels: 12.5 us -> 16 us
  other arithmetic: 5.08 us -> 7.53 us
    all_to_all x1 -> x0, blocking collectives: 29.3 us -> none  [on_device(): total = lax.all_to_all(total, 'x', 0, 0)]
    ppermute x5 -> x9, starting transfers between devices: 21.1 us -> 33.5 us  [the longest x4 18.8 us: on_device(): lax.ppermute(part[j], ('l', 'h'), scatter_pairs(i, j)).astype(wide)]
    all_gather x1, waiting for transfers between devices: 8.46 us -> 0.01 us  [on_device(): panels = lax.all_gather(jnp.concatenate([w_in, w_out], axis=0), 'y', axis=0)]
    pallas_call x1 -> x2, Pallas kernels: 8.27 us -> 11.8 us  [the longest x1 5.97 us: first_call(): call(first_kernel, ['scalar', 'here', 'here', 'any', 'any', 'any'], [jax....]
    all_to_all x0 -> x1, starting transfers between devices: none -> 3.51 us  [on_device(): first = lax.all_to_all(add(outs[0], got[0]), 'x', 0, 0)]
    convert_element_type x1 -> x3, other arithmetic: 0.54 us -> 3.42 us  [the longest x2 2.2 us: add(): return (a.astype(wide) + b.astype(wide)).astype(narrow)]
    ppermute x4, starting transfers between devices: 19.5 us -> 22.2 us  [on_device(): lax.ppermute(pack, ('l', 'h'), gather_pairs(i, j))]
    ppermute x5 -> x9, waiting for transfers between devices: 11 us -> 9.51 us  [the longest x4 6.57 us: on_device(): lax.ppermute(part[j], ('l', 'h'), scatter_pairs(i, j)).astype(wide)]
  transfers between devices with their start and end apart: 13 -> 18, of which waited for: 6 -> 7; matrix products, arithmetic and copies ran while one was open for 1% -> 3% of each run, Pallas kernels for 0% -> 4%
where the time goes in v5:
time: 162 us; the launch traced here: 161 us
  starting transfers between devices  65.3 us (40%)
  blocking collectives  30.4 us (19%)
  waiting for transfers between devices  26.7 us (16%)
  Pallas kernels  16 us (10%)
  between operations  14.3 us (9%)
  other arithmetic  7.53 us (5%)
    ppermute x4, starting transfers between devices, on_device(): lax.ppermute(pack, ('l', 'h'), gather_pairs(i, j))  22.2 us
    ppermute x4, starting transfers between devices, on_device(): lax.ppermute(part[j], ('l', 'h'), scatter_pairs(i, j)).astype(wide)  18.8 us
    all_gather x1, blocking collectives, on_device(): own0 = lax.all_gather(jnp.stack(near[0]), 'x', axis=0)  15.9 us
    all_gather x1, blocking collectives, on_device(): own1 = lax.all_gather(jnp.stack(near[1]), 'x', axis=0)  14.5 us
    ppermute x1, waiting for transfers between devices, on_device(): far_sums = lax.ppermute(sums, 'l', other_core)  13.2 us
    ppermute x3, starting transfers between devices, on_device(): lax.ppermute(second[d], 'x', [(x, (x + d) % 4) for x in range(4)])  10.4 us
    ppermute x4, waiting for transfers between devices, on_device(): lax.ppermute(part[j], ('l', 'h'), scatter_pairs(i, j)).astype(wide)  6.57 us
    pallas_call x1, Pallas kernels, first_call(): call(first_kernel, ['scalar', 'here', 'here', 'any', 'any', 'any'], [jax....  5.97 us
  transfers between devices with their start and end apart: 18, of which 7 were waited for; matrix products, arithmetic and copies ran while one was open for 3% of the time, Pallas kernels for 4%

profile of v5, /device:TPU:64, one launch (start us, length us, event | category | flops | bytes accessed | tf_op | source)
XLA Modules:
  0.0 161.0 jit_solution(4658959610663657970)
XLA Ops:
  7.2 0.0 all-gather.5.cloned.1.call-start
  7.2 1.9 %pad_maximum_fusion = bf16[768,384]{1,0:T(8,128)(2,1)} fusion(bf16[384,384]{1,0:T(8,128)(2,1)} %param.8, bf16[384,384]{1,0:T(8,128)(2,1)} %param.7), kind=kLoop, calls=%fused_computation.1 | loop fusion | flops 1179648 | bytes 1179648 | tf_op jit(solution)/shard_map/concatenate | solution.py:292
  9.1 0.0 all-gather.5.cloned.1.call-update
  9.2 0.8 pad_maximum_fusion.4
  10.0 1.0 pad_maximum_fusion.3
  11.0 6.9 %collective-permute-start.2 = (bf16[168,384]{1,0:T(8,128)(2,1)S(1)}, bf16[168,384]{1,0:T(8,128)(2,1)S(1)}, u32[]{:S(2)}, u32[]{:S(2)}) collective-permute-start(bf16[168,384]{1,0:T(8,128)(2,1)S(1)} %pad_maximum_fusion.3), channel_id=1, source_target_pairs={{0,16},{8,24},{16,272},{24,280},{256,0},{264,8},{272,256},{280,264... | collective-permute-start | bytes 387080 | tf_op jit(solution)/shard_map/ppermute | solution.py:297
  18.0 6.5 %collective-permute-start.3 = (bf16[168,384]{1,0:T(8,128)(2,1)S(1)}, bf16[168,384]{1,0:T(8,128)(2,1)S(1)}, u32[]{:S(2)}, u32[]{:S(2)}) collective-permute-start(bf16[168,384]{1,0:T(8,128)(2,1)S(1)} %pad_maximum_fusion.3), channel_id=1, source_target_pairs={{0,24},{8,16},{16,280},{24,272},{256,8},{264,0},{272,264},{280,256... | collective-permute-start | bytes 387080 | tf_op jit(solution)/shard_map/ppermute | solution.py:297
  24.4 2.8 %collective-permute-start = (bf16[168,384]{1,0:T(8,128)(2,1)S(1)}, bf16[168,384]{1,0:T(8,128)(2,1)S(1)}, u32[]{:S(2)}, u32[]{:S(2)}) collective-permute-start(bf16[168,384]{1,0:T(8,128)(2,1)S(1)} %pad_maximum_fusion.3), channel_id=1, source_target_pairs={{0,0},{8,8},{16,256},{24,264},{256,16},{264,24},{272,272},{280,280... | collective-permute-start | bytes 387080 | tf_op jit(solution)/shard_map/ppermute | solution.py:297
  27.3 6.0 %collective-permute-start.1 = (bf16[168,384]{1,0:T(8,128)(2,1)S(1)}, bf16[168,384]{1,0:T(8,128)(2,1)S(1)}, u32[]{:S(2)}, u32[]{:S(2)}) collective-permute-start(bf16[168,384]{1,0:T(8,128)(2,1)S(1)} %pad_maximum_fusion.3), channel_id=1, source_target_pairs={{0,8},{8,0},{16,264},{24,256},{256,24},{264,16},{272,280},{280,272... | collective-permute-start | bytes 387080 | tf_op jit(solution)/shard_map/ppermute | solution.py:297
  33.3 0.0 collective-permute-done.2
  33.3 0.0 collective-permute-done.3
  33.3 14.5 %all-gather.1 = bf16[8,168,384]{2,1,0:T(8,128)(2,1)S(1)} all-gather(bf16[2,168,384]{2,1,0:T(8,128)(2,1)S(1)} %pad_maximum_fusion.2), channel_id=3, replica_groups=mesh['l'=2,'y'=8,'h'=4,'x'=4,'k'=2] {'x'}, dimensions={0}, use_global_device_ids=true | all-gather | bytes 1290240 | tf_op jit(solution)/shard_map/all_gather | solution.py:301
  47.8 1.9 %collective-permute-start.5 = (bf16[4,2,168,384]{3,2,1,0:T(8,128)(2,1)S(1)}, bf16[4,2,168,384]{3,2,1,0:T(8,128)(2,1)S(1)}, u32[]{:S(2)}, u32[]{:S(2)}) collective-permute-start(bf16[4,2,168,384]{3,2,1,0:T(8,128)(2,1)S(1)} %bitcast.33), channel_id=1, source_target_pairs={{0,1},{1,0},{2,3},{3,2},{4,5},{5,4},{6,7},{7,6},{8,9},{9,8},{10,11... | collective-permute-start | bytes 3096584 | tf_op jit(solution)/shard_map/ppermute | solution.py:302
  49.7 0.0 collective-permute-done
  49.7 0.0 collective-permute-done.1
  49.8 15.9 %all-gather = bf16[8,168,384]{2,1,0:T(8,128)(2,1)S(1)} all-gather(bf16[2,168,384]{2,1,0:T(8,128)(2,1)S(1)} %pad_maximum_fusion.1), channel_id=2, replica_groups=mesh['l'=2,'y'=8,'h'=4,'x'=4,'k'=2] {'x'}, dimensions={0}, use_global_device_ids=true | all-gather | bytes 1290240 | tf_op jit(solution)/shard_map/all_gather | solution.py:299
  65.7 1.9 %collective-permute-start.4 = (bf16[4,2,168,384]{3,2,1,0:T(8,128)(2,1)S(1)}, bf16[4,2,168,384]{3,2,1,0:T(8,128)(2,1)}, u32[]{:S(2)}, u32[]{:S(2)}) collective-permute-start(bf16[4,2,168,384]{3,2,1,0:T(8,128)(2,1)S(1)} %bitcast.35), channel_id=1, source_target_pairs={{0,1},{1,0},{2,3},{3,2},{4,5},{5,4},{6,7},{7,6},{8,9},{9,8},{10,11... | collective-permute-start | bytes 3096584 | tf_op jit(solution)/shard_map/ppermute | solution.py:300
  67.6 0.1 pad_add_fusion.place_ref
  67.7 0.0 collective-permute-done.5.far1
  67.7 2.6 %collective-permute-done.4.far0 = bf16[4,2,168,384]{3,2,1,0:T(8,128)(2,1)} collective-permute-done((bf16[4,2,168,384]{3,2,1,0:T(8,128)(2,1)S(1)}, bf16[4,2,168,384]{3,2,1,0:T(8,128)(2,1)}, u32[]{:S(2)}, u32[]{:S(2)}) %collective-permute-start.4) | collective-permute-done | bytes 1032224 | tf_op jit(solution)/shard_map/ppermute | solution.py:300
  70.3 5.8 %merge.1 = (bf16[320,3072]{1,0:T(8,128)(2,1)}, bf16[4,320,768]{2,1,0:T(8,128)(2,1)}, bf16[4,320,768]{2,1,0:T(8,128)(2,1)}, f32[8,3072]{1,0:T(8,128)S(1)}, bf16[384,128]{1,0:T(8,128)(2,1)S(1)}) custom-call(s32[3]{0:T(128)S(1)} %pad_add_fusion.place_ref, bf16[4,2,168,384]{3,2,1,0:T(8,128)(2,1)S(1)} %bitcast.36, bf16[4,2,168,384]{3,2,1,0:T(8,128)(2,1)S(1)} %bitcast.34, ...), custom_call_target="tpu_custom_call" | custom-call | tf_op jit(solution)/shard_map/merge/pallas_call | solution.py:237
  76.2 0.0 all-gather.5.cloned.1.call-done
  76.2 0.0 slice-start
  76.2 0.0 slice-start.1
  76.2 0.0 copy-start
  76.2 6.0 %first.1.own_ref = bf16[656,384]{1,0:T(8,128)(2,1)S(1)} custom-call(s32[3]{0:T(128)S(1)} %pad_add_fusion.place_ref, f32[8,3072]{1,0:T(8,128)S(1)} %get-tuple-element.11.gain_ref, bf16[384,128]{1,0:T(8,128)(2,1)S(1)} %get-tuple-element.12.table_ref, bf16[4,320,768]{2,1,0:T(8,128)(2,1)} %get-tuple-element.13.shift_ref, ...), custom_call_target="tpu_custom_call" | custom-call | tf_op jit(solution)/shard_map/first/pallas_call | solution.py:256
  82.1 2.2 %collective-permute-start.6 = (bf16[656,384]{1,0:T(8,128)(2,1)S(1)}, bf16[656,384]{1,0:T(8,128)(2,1)S(1)}, u32[]{:S(2)}, u32[]{:S(2)}) collective-permute-start(bf16[656,384]{1,0:T(8,128)(2,1)S(1)} %first.1.own_ref), channel_id=1, source_target_pairs={{0,256},{256,0},{1,257},{257,1},{2,258},{258,2},{3,259},{259,3},{4... | collective-permute-start | bytes 1511432 | tf_op jit(solution)/shard_map/ppermute | solution.py:306
  84.4 13.2 %collective-permute-done.6.far_ref = bf16[656,384]{1,0:T(8,128)(2,1)S(1)} collective-permute-done((bf16[656,384]{1,0:T(8,128)(2,1)S(1)}, bf16[656,384]{1,0:T(8,128)(2,1)S(1)}, u32[]{:S(2)}, u32[]{:S(2)}) %collective-permute-start.6) | collective-permute-done | bytes 503840 | tf_op jit(solution)/shard_map/ppermute | solution.py:306
  97.5 0.0 slice-done
  97.5 0.0 slice-done.1
  97.6 0.0 copy-done
  97.6 4.2 %second.1 = (bf16[4,2,160,384]{3,2,1,0:T(8,128)(2,1)S(1)}, bf16[4,2,160,384]{3,2,1,0:T(8,128)(2,1)S(1)}, bf16[4,2,160,384]{3,2,1,0:T(8,128)(2,1)S(1)}, bf16[4,2,160,384]{3,2,1,0:T(8,128)(2,1)S(1)}) custom-call(s32[3]{0:T(128)S(1)} %pad_add_fusion.place_ref, bf16[656,384]{1,0:T(8,128)(2,1)S(1)} %first.1.own_ref, ...), custom_call_target="tpu_custom_call" | custom-call | tf_op jit(solution)/shard_map/second/pallas_call | solution.py:275
  101.8 1.9 %collective-permute-start.10 = (bf16[4,2,160,384]{3,2,1,0:T(8,128)(2,1)S(1)}, bf16[4,2,160,384]{3,2,1,0:T(8,128)(2,1)S(1)}, u32[]{:S(2)}, u32[]{:S(2)}) collective-permute-start(bf16[4,2,160,384]{3,2,1,0:T(8,128)(2,1)S(1)} %get-tuple-element.19), channel_id=1, source_target_pairs={{0,1},{1,0},{2,3},{3,2},{4,5},{5,4},{6,7},{7,6},{8,9},{9,8},{10,11... | collective-permute-start | bytes 2949128 | tf_op jit(solution)/shard_map/ppermute | solution.py:309
  103.7 2.4 %collective-permute-start.7 = (bf16[4,2,160,384]{3,2,1,0:T(8,128)(2,1)S(1)}, bf16[4,2,160,384]{3,2,1,0:T(8,128)(2,1)S(1)}, u32[]{:S(2)}, u32[]{:S(2)}) collective-permute-start(bf16[4,2,160,384]{3,2,1,0:T(8,128)(2,1)S(1)} %get-tuple-element.17), channel_id=1, source_target_pairs={{0,1},{1,0},{2,3},{3,2},{4,5},{5,4},{6,7},{7,6},{8,9},{9,8},{10,11... | collective-permute-start | bytes 2949128 | tf_op jit(solution)/shard_map/ppermute | solution.py:309
  106.1 0.1 collective-permute-done.10
  106.3 1.0 fusion.4
  107.2 3.6 %collective-permute-start.11 = (bf16[2,160,384]{2,1,0:T(8,128)(2,1)}, bf16[2,160,384]{2,1,0:T(8,128)(2,1)S(1)}, u32[]{:S(2)}, u32[]{:S(2)}) collective-permute-start(bf16[2,160,384]{2,1,0:T(8,128)(2,1)} %get-tuple-element.20), channel_id=1, source_target_pairs={{0,2},{2,4},{4,6},{6,0},{1,3},{3,5},{5,7},{7,1},{8,10},{10,12},{12... | collective-permute-start | bytes 737288 | tf_op jit(solution)/shard_map/ppermute | solution.py:316
  110.8 3.4 %collective-permute-start.12 = (bf16[2,160,384]{2,1,0:T(8,128)(2,1)}, bf16[2,160,384]{2,1,0:T(8,128)(2,1)}, u32[]{:S(2)}, u32[]{:S(2)}) collective-permute-start(bf16[2,160,384]{2,1,0:T(8,128)(2,1)} %get-tuple-element.22), channel_id=1, source_target_pairs={{0,6},{2,0},{4,2},{6,4},{1,7},{3,1},{5,3},{7,5},{8,14},{10,8},{12,... | collective-permute-start | bytes 737288 | tf_op jit(solution)/shard_map/ppermute | solution.py:316
  114.3 3.3 %collective-permute-start.13 = (bf16[2,160,384]{2,1,0:T(8,128)(2,1)S(1)}, bf16[2,160,384]{2,1,0:T(8,128)(2,1)}, u32[]{:S(2)}, u32[]{:S(2)}) collective-permute-start(bf16[2,160,384]{2,1,0:T(8,128)(2,1)S(1)} %get-tuple-element.21), channel_id=1, source_target_pairs={{0,4},{2,6},{4,0},{6,2},{1,5},{3,7},{5,1},{7,3},{8,12},{10,14},{12... | collective-permute-start | bytes 737288 | tf_op jit(solution)/shard_map/ppermute | solution.py:316
  117.6 0.0 collective-permute-done.7
  117.6 1.2 add_convert_fusion
  118.9 3.5 %all-to-all-start = ((bf16[4,2,160,384]{3,2,1,0:T(8,128)(2,1)}), bf16[4,2,160,384]{3,2,1,0:T(8,128)(2,1)S(1)}, u32[]{:S(2)}, u32[]{:S(2)}) async-start(bf16[4,2,160,384]{3,2,1,0:T(8,128)(2,1)} %add_convert_fusion), calls=%async_computation | async-start | bytes 1966080 | tf_op jit(solution)/shard_map/all_to_all | solution.py:313
  122.4 0.0 collective-permute-done.11
  122.4 0.0 collective-permute-done.12
  122.4 2.8 %collective-permute-done.13 = bf16[2,160,384]{2,1,0:T(8,128)(2,1)} collective-permute-done((bf16[2,160,384]{2,1,0:T(8,128)(2,1)S(1)}, bf16[2,160,384]{2,1,0:T(8,128)(2,1)}, u32[]{:S(2)}, u32[]{:S(2)}) %collective-permute-start.13) | collective-permute-done | bytes 245792 | tf_op jit(solution)/shard_map/ppermute | solution.py:316
  125.2 1.2 fusion.2
  126.5 6.8 %collective-permute-start.14 = (bf16[160,384]{1,0:T(8,128)(2,1)S(1)}, bf16[160,384]{1,0:T(8,128)(2,1)S(1)}, u32[]{:S(2)}, u32[]{:S(2)}) collective-permute-start(bf16[160,384]{1,0:T(8,128)(2,1)S(1)} %get-tuple-element.25), channel_id=1, source_target_pairs={{0,256},{8,264},{16,0},{24,8},{256,272},{264,280},{272,16},{280,24... | collective-permute-start | bytes 368648 | tf_op jit(solution)/shard_map/ppermute | solution.py:321
  133.2 1.9 %collective-permute-start.15 = (bf16[160,384]{1,0:T(8,128)(2,1)S(1)}, bf16[160,384]{1,0:T(8,128)(2,1)S(1)}, u32[]{:S(2)}, u32[]{:S(2)}) collective-permute-start(bf16[160,384]{1,0:T(8,128)(2,1)S(1)} %get-tuple-element.26), channel_id=1, source_target_pairs={{0,264},{8,256},{16,8},{24,0},{256,280},{264,272},{272,24},{280,16... | collective-permute-start | bytes 368648 | tf_op jit(solution)/shard_map/ppermute | solution.py:321
  135.2 1.3 all-to-all-done
  136.5 0.1 add_convert_fusion.5
  136.7 6.9 %collective-permute-start.8 = (bf16[160,384]{1,0:T(8,128)(2,1)S(1)}, bf16[160,384]{1,0:T(8,128)(2,1)S(1)}, u32[]{:S(2)}, u32[]{:S(2)}) collective-permute-start(bf16[160,384]{1,0:T(8,128)(2,1)S(1)} %get-tuple-element.23), channel_id=1, source_target_pairs={{0,0},{8,8},{16,256},{24,264},{256,16},{264,24},{272,272},{280,280... | collective-permute-start | bytes 368648 | tf_op jit(solution)/shard_map/ppermute | solution.py:321
  143.6 3.2 %collective-permute-start.9 = (bf16[160,384]{1,0:T(8,128)(2,1)S(1)}, bf16[160,384]{1,0:T(8,128)(2,1)S(1)}, u32[]{:S(2)}, u32[]{:S(2)}) collective-permute-start(bf16[160,384]{1,0:T(8,128)(2,1)S(1)} %get-tuple-element.24), channel_id=1, source_target_pairs={{0,8},{8,0},{16,264},{24,256},{256,24},{264,16},{272,280},{280,272... | collective-permute-start | bytes 368648 | tf_op jit(solution)/shard_map/ppermute | solution.py:321
  146.8 0.0 collective-permute-done.14
  146.8 0.0 collective-permute-done.15
  146.8 0.3 collective-permute-done.8
  147.1 6.2 %collective-permute-done.9 = bf16[160,384]{1,0:T(8,128)(2,1)S(1)} collective-permute-done((bf16[160,384]{1,0:T(8,128)(2,1)S(1)}, bf16[160,384]{1,0:T(8,128)(2,1)S(1)}, u32[]{:S(2)}, u32[]{:S(2)}) %collective-permute-start.9) | collective-permute-done | bytes 122912 | tf_op jit(solution)/shard_map/ppermute | solution.py:321
  153.4 0.1 add_convert_fusion.6
  153.4 0.7 fusion.7
  (6 shorter events, 0.1 us)
Async XLA Ops:
  7.2 69.0 %all-gather.5.cloned.1.call-start = ((), (), s32[]{:S(2)}) async-start(), calls=%async_computation.1 | async-start | bytes 5308416 | tf_op jit(solution)/shard_map/all_gather | solution.py:292
  11.0 22.3 %collective-permute-start.2 = (bf16[168,384]{1,0:T(8,128)(2,1)S(1)}, bf16[168,384]{1,0:T(8,128)(2,1)S(1)}, u32[]{:S(2)}, u32[]{:S(2)}) collective-permute-start(bf16[168,384]{1,0:T(8,128)(2,1)S(1)} %pad_maximum_fusion.3), channel_id=1, source_target_pairs={{0,16},{8,24},{16,272},{24,280},{256,0},{264,8},{272,256},{280,264... | collective-permute-start | bytes 387080 | tf_op jit(solution)/shard_map/ppermute | solution.py:297
  18.0 15.3 %collective-permute-start.3 = (bf16[168,384]{1,0:T(8,128)(2,1)S(1)}, bf16[168,384]{1,0:T(8,128)(2,1)S(1)}, u32[]{:S(2)}, u32[]{:S(2)}) collective-permute-start(bf16[168,384]{1,0:T(8,128)(2,1)S(1)} %pad_maximum_fusion.3), channel_id=1, source_target_pairs={{0,24},{8,16},{16,280},{24,272},{256,8},{264,0},{272,264},{280,256... | collective-permute-start | bytes 387080 | tf_op jit(solution)/shard_map/ppermute | solution.py:297
  24.4 25.3 %collective-permute-start = (bf16[168,384]{1,0:T(8,128)(2,1)S(1)}, bf16[168,384]{1,0:T(8,128)(2,1)S(1)}, u32[]{:S(2)}, u32[]{:S(2)}) collective-permute-start(bf16[168,384]{1,0:T(8,128)(2,1)S(1)} %pad_maximum_fusion.3), channel_id=1, source_target_pairs={{0,0},{8,8},{16,256},{24,264},{256,16},{264,24},{272,272},{280,280... | collective-permute-start | bytes 387080 | tf_op jit(solution)/shard_map/ppermute | solution.py:297
  27.3 22.5 %collective-permute-start.1 = (bf16[168,384]{1,0:T(8,128)(2,1)S(1)}, bf16[168,384]{1,0:T(8,128)(2,1)S(1)}, u32[]{:S(2)}, u32[]{:S(2)}) collective-permute-start(bf16[168,384]{1,0:T(8,128)(2,1)S(1)} %pad_maximum_fusion.3), channel_id=1, source_target_pairs={{0,8},{8,0},{16,264},{24,256},{256,24},{264,16},{272,280},{280,272... | collective-permute-start | bytes 387080 | tf_op jit(solution)/shard_map/ppermute | solution.py:297
  47.8 19.9 %collective-permute-start.5 = (bf16[4,2,168,384]{3,2,1,0:T(8,128)(2,1)S(1)}, bf16[4,2,168,384]{3,2,1,0:T(8,128)(2,1)S(1)}, u32[]{:S(2)}, u32[]{:S(2)}) collective-permute-start(bf16[4,2,168,384]{3,2,1,0:T(8,128)(2,1)S(1)} %bitcast.33), channel_id=1, source_target_pairs={{0,1},{1,0},{2,3},{3,2},{4,5},{5,4},{6,7},{7,6},{8,9},{9,8},{10,11... | collective-permute-start | bytes 3096584 | tf_op jit(solution)/shard_map/ppermute | solution.py:302
  65.7 4.7 %collective-permute-start.4 = (bf16[4,2,168,384]{3,2,1,0:T(8,128)(2,1)S(1)}, bf16[4,2,168,384]{3,2,1,0:T(8,128)(2,1)}, u32[]{:S(2)}, u32[]{:S(2)}) collective-permute-start(bf16[4,2,168,384]{3,2,1,0:T(8,128)(2,1)S(1)} %bitcast.35), channel_id=1, source_target_pairs={{0,1},{1,0},{2,3},{3,2},{4,5},{5,4},{6,7},{7,6},{8,9},{9,8},{10,11... | collective-permute-start | bytes 3096584 | tf_op jit(solution)/shard_map/ppermute | solution.py:300
  76.2 21.4 %slice-start = ((s8[4718592]{0:T(1024)(128)(4,1)}), s8[4194304]{0:T(1024)(128)(4,1)S(1)}, s32[]{:S(2)}) async-start(s8[4718592]{0:T(1024)(128)(4,1)} %bitcast.30), calls=%async_computation.2 | async-start | bytes 8388608
  76.2 21.4 %slice-start.1 = ((s8[4718592]{0:T(1024)(128)(4,1)}), s8[524288]{0:T(1024)(128)(4,1)S(1)}, s32[]{:S(2)}) async-start(s8[4718592]{0:T(1024)(128)(4,1)} %bitcast.30), calls=%async_computation.3 | async-start | bytes 1048576
  76.2 21.4 %copy-start = (bf16[320,3072]{1,0:T(8,128)(2,1)S(1)}, bf16[320,3072]{1,0:T(8,128)(2,1)}, u32[]{:S(2)}) copy-start(bf16[320,3072]{1,0:T(8,128)(2,1)} %get-tuple-element.15.x_ref) | copy-start | bytes 5898244
  82.1 15.4 %collective-permute-start.6 = (bf16[656,384]{1,0:T(8,128)(2,1)S(1)}, bf16[656,384]{1,0:T(8,128)(2,1)S(1)}, u32[]{:S(2)}, u32[]{:S(2)}) collective-permute-start(bf16[656,384]{1,0:T(8,128)(2,1)S(1)} %first.1.own_ref), channel_id=1, source_target_pairs={{0,256},{256,0},{1,257},{257,1},{2,258},{258,2},{3,259},{259,3},{4... | collective-permute-start | bytes 1511432 | tf_op jit(solution)/shard_map/ppermute | solution.py:306
  101.8 4.5 %collective-permute-start.10 = (bf16[4,2,160,384]{3,2,1,0:T(8,128)(2,1)S(1)}, bf16[4,2,160,384]{3,2,1,0:T(8,128)(2,1)S(1)}, u32[]{:S(2)}, u32[]{:S(2)}) collective-permute-start(bf16[4,2,160,384]{3,2,1,0:T(8,128)(2,1)S(1)} %get-tuple-element.19), channel_id=1, source_target_pairs={{0,1},{1,0},{2,3},{3,2},{4,5},{5,4},{6,7},{7,6},{8,9},{9,8},{10,11... | collective-permute-start | bytes 2949128 | tf_op jit(solution)/shard_map/ppermute | solution.py:309
  103.7 13.9 %collective-permute-start.7 = (bf16[4,2,160,384]{3,2,1,0:T(8,128)(2,1)S(1)}, bf16[4,2,160,384]{3,2,1,0:T(8,128)(2,1)S(1)}, u32[]{:S(2)}, u32[]{:S(2)}) collective-permute-start(bf16[4,2,160,384]{3,2,1,0:T(8,128)(2,1)S(1)} %get-tuple-element.17), channel_id=1, source_target_pairs={{0,1},{1,0},{2,3},{3,2},{4,5},{5,4},{6,7},{7,6},{8,9},{9,8},{10,11... | collective-permute-start | bytes 2949128 | tf_op jit(solution)/shard_map/ppermute | solution.py:309
  107.2 15.2 %collective-permute-start.11 = (bf16[2,160,384]{2,1,0:T(8,128)(2,1)}, bf16[2,160,384]{2,1,0:T(8,128)(2,1)S(1)}, u32[]{:S(2)}, u32[]{:S(2)}) collective-permute-start(bf16[2,160,384]{2,1,0:T(8,128)(2,1)} %get-tuple-element.20), channel_id=1, source_target_pairs={{0,2},{2,4},{4,6},{6,0},{1,3},{3,5},{5,7},{7,1},{8,10},{10,12},{12... | collective-permute-start | bytes 737288 | tf_op jit(solution)/shard_map/ppermute | solution.py:316
  110.8 11.5 %collective-permute-start.12 = (bf16[2,160,384]{2,1,0:T(8,128)(2,1)}, bf16[2,160,384]{2,1,0:T(8,128)(2,1)}, u32[]{:S(2)}, u32[]{:S(2)}) collective-permute-start(bf16[2,160,384]{2,1,0:T(8,128)(2,1)} %get-tuple-element.22), channel_id=1, source_target_pairs={{0,6},{2,0},{4,2},{6,4},{1,7},{3,1},{5,3},{7,5},{8,14},{10,8},{12,... | collective-permute-start | bytes 737288 | tf_op jit(solution)/shard_map/ppermute | solution.py:316
  114.3 10.9 %collective-permute-start.13 = (bf16[2,160,384]{2,1,0:T(8,128)(2,1)S(1)}, bf16[2,160,384]{2,1,0:T(8,128)(2,1)}, u32[]{:S(2)}, u32[]{:S(2)}) collective-permute-start(bf16[2,160,384]{2,1,0:T(8,128)(2,1)S(1)} %get-tuple-element.21), channel_id=1, source_target_pairs={{0,4},{2,6},{4,0},{6,2},{1,5},{3,7},{5,1},{7,3},{8,12},{10,14},{12... | collective-permute-start | bytes 737288 | tf_op jit(solution)/shard_map/ppermute | solution.py:316
  118.9 17.6 %all-to-all-start = ((bf16[4,2,160,384]{3,2,1,0:T(8,128)(2,1)}), bf16[4,2,160,384]{3,2,1,0:T(8,128)(2,1)S(1)}, u32[]{:S(2)}, u32[]{:S(2)}) async-start(bf16[4,2,160,384]{3,2,1,0:T(8,128)(2,1)} %add_convert_fusion), calls=%async_computation | async-start | bytes 1966080 | tf_op jit(solution)/shard_map/all_to_all | solution.py:313
  126.5 20.3 %collective-permute-start.14 = (bf16[160,384]{1,0:T(8,128)(2,1)S(1)}, bf16[160,384]{1,0:T(8,128)(2,1)S(1)}, u32[]{:S(2)}, u32[]{:S(2)}) collective-permute-start(bf16[160,384]{1,0:T(8,128)(2,1)S(1)} %get-tuple-element.25), channel_id=1, source_target_pairs={{0,256},{8,264},{16,0},{24,8},{256,272},{264,280},{272,16},{280,24... | collective-permute-start | bytes 368648 | tf_op jit(solution)/shard_map/ppermute | solution.py:321
  133.2 13.5 %collective-permute-start.15 = (bf16[160,384]{1,0:T(8,128)(2,1)S(1)}, bf16[160,384]{1,0:T(8,128)(2,1)S(1)}, u32[]{:S(2)}, u32[]{:S(2)}) collective-permute-start(bf16[160,384]{1,0:T(8,128)(2,1)S(1)} %get-tuple-element.26), channel_id=1, source_target_pairs={{0,264},{8,256},{16,8},{24,0},{256,280},{264,272},{272,24},{280,16... | collective-permute-start | bytes 368648 | tf_op jit(solution)/shard_map/ppermute | solution.py:321
  136.7 10.5 %collective-permute-start.8 = (bf16[160,384]{1,0:T(8,128)(2,1)S(1)}, bf16[160,384]{1,0:T(8,128)(2,1)S(1)}, u32[]{:S(2)}, u32[]{:S(2)}) collective-permute-start(bf16[160,384]{1,0:T(8,128)(2,1)S(1)} %get-tuple-element.23), channel_id=1, source_target_pairs={{0,0},{8,8},{16,256},{24,264},{256,16},{264,24},{272,272},{280,280... | collective-permute-start | bytes 368648 | tf_op jit(solution)/shard_map/ppermute | solution.py:321
  143.6 9.8 %collective-permute-start.9 = (bf16[160,384]{1,0:T(8,128)(2,1)S(1)}, bf16[160,384]{1,0:T(8,128)(2,1)S(1)}, u32[]{:S(2)}, u32[]{:S(2)}) collective-permute-start(bf16[160,384]{1,0:T(8,128)(2,1)S(1)} %get-tuple-element.24), channel_id=1, source_target_pairs={{0,8},{8,0},{16,264},{24,256},{256,24},{264,16},{272,280},{280,272... | collective-permute-start | bytes 368648 | tf_op jit(solution)/shard_map/ppermute | solution.py:321
Sparse Core Ops, SparseCore 0:
  10.1 65.9 all-gather.4

commit v6 on v5

--- a/solution.py
+++ b/solution.py
@@ -13,6 +13,7 @@
 epsilon = 1e-06
 narrow = jnp.bfloat16
 wide = jnp.float32
+relative = (True, True)
 
 
 def pairs_of(target):
@@ -60,8 +61,7 @@
     place_ref, own0, own1, far0, far1, x_ref, shift_ref, g_ref, gain_ref, table_ref
 ):
     blocks, block = own0.shape[0] * own0.shape[1], own0.shape[3]
-    tokens = x_ref.shape[0]
-    rows, half = tokens // 2, block // 2
+    rows, half = x_ref.shape[1], block // 2
     first = place_ref[0] == 0
 
     def sides(own, far):
@@ -79,7 +79,7 @@
             x, j = index % 4, index // 4
             to = slice(index * block, (index + 1) * block)
             values, grads = sides(own[x, j, :rows], far[x, j, :rows])
-            x_ref[at, to] = values
+            x_ref[part, :, to] = values
             wide_to = slice(index % 2 * block, (index % 2 + 1) * block)
             g_ref[index // 2, at, wide_to] = grads
             for lane in range(0, block, 128):
@@ -89,7 +89,7 @@
         mean = jnp.sum(total, axis=1, keepdims=True) * (1.0 / (blocks * block))
         spread = jnp.zeros((rows, 128), wide)
         for lane in range(0, blocks * block, 128):
-            shifted = x_ref[at, lane : lane + 128].astype(wide) - mean
+            shifted = x_ref[part, :, lane : lane + 128].astype(wide) - mean
             spread = spread + shifted * shifted
             pair, to = lane // (2 * block), lane % (2 * block)
             shift_ref[pair, at, to : to + 128] = (shifted * gain_ref[:1, lane : lane + 128]).astype(narrow)
@@ -98,11 +98,11 @@
         table = jnp.zeros((rows, 128), wide)
         for index, column in enumerate(columns):
             table = jnp.where(lane == index, column, table)
-        table_ref[at] = table.astype(narrow)
+        table_ref[part, :rows] = table.astype(narrow)
 
 
 def first_kernel(
-    place_ref, gain_ref, table_ref, shift_ref, g_ref, panel_ref, sums_ref,
+    place_ref, gain_ref, table_ref, shift_ref, g_ref, panel_ref, sums0_ref, sums1_ref,
     shift_s, g_s, panel_s, sems,
 ):
     pairs, tokens, width = shift_ref.shape
@@ -137,29 +137,31 @@
         v = jnp.dot(gain_ref[:, to].astype(narrow), w_in, preferred_element_type=wide)
         pre, act, gain_sum = (p, a, v) if pre is None else (pre + p, act + a, gain_sum + v)
 
-    sums_ref[:tokens] = pre.astype(narrow)
-    sums_ref[tokens : 2 * tokens] = act.astype(narrow)
-    lines = lax.dot_general(
-        ones_diagonal(16, 128), table_ref[...], (((1,), (1,)), ((), ())), preferred_element_type=wide
-    )
+    rows = tokens // 2
     high = gain_sum[:1].astype(narrow).astype(wide)
-    row = lax.broadcasted_iota(jnp.int32, lines.shape, 0)
-    lines = jnp.where(row == 6, high, jnp.where(row == 7, gain_sum[:1] - high, lines))
-    sums_ref[2 * tokens :] = lines.astype(narrow)
+    for part, sums_ref in enumerate((sums0_ref, sums1_ref)):
+        at = slice(part * rows, (part + 1) * rows)
+        sums_ref[:rows] = pre[at].astype(narrow)
+        sums_ref[rows:tokens] = act[at].astype(narrow)
+        lines = lax.dot_general(
+            ones_diagonal(16, 128), table_ref[part], (((1,), (1,)), ((), ())), preferred_element_type=wide
+        )
+        row = lax.broadcasted_iota(jnp.int32, lines.shape, 0)
+        lines = jnp.where(row == 6, high, jnp.where(row == 7, gain_sum[:1] - high, lines))
+        sums_ref[tokens:] = lines.astype(narrow)
 
 
 def second_kernel(
-    features, place_ref, own_ref, far_ref, x_ref, gain_ref, panel_ref, *out_refs
+    features, part, place_ref, own_ref, far_ref, x_ref, gain_ref, panel_ref, keep_ref, send_ref
 ):
-    tokens = x_ref.shape[0]
+    rows = x_ref.shape[1]
     blocks, block = panel_ref.shape[0], panel_ref.shape[1] // 2
-    rows = tokens // 2
 
     def extras(ref):
-        lines = ref[2 * tokens :]
+        lines = ref[2 * rows :]
         table = lax.dot_general(
             lines, ones_diagonal(16, 128), (((0,), (0,)), ((), ())), preferred_element_type=wide
-        )[:tokens]
+        )[:rows]
         center = table[:, 0:1] + table[:, 1:2] + table[:, 2:3]
         spread = table[:, 3:4] + table[:, 4:5] + table[:, 5:6]
         lines = lines.astype(wide)
@@ -171,10 +173,10 @@
     mean = 0.5 * (mean_a + mean_b)
     spread = spread_a + spread_b + gap * gap * (features / 4)
     inverse = lax.rsqrt(spread / features + epsilon)
-    total = own_ref[:tokens].astype(wide) + far_ref[:tokens].astype(wide)
+    total = own_ref[:rows].astype(wide) + far_ref[:rows].astype(wide)
     total = total + (mean_a - mean) * gain_a + (mean_b - mean) * gain_b
     preact = total * inverse
-    act_grad = own_ref[tokens : 2 * tokens].astype(wide) + far_ref[tokens : 2 * tokens].astype(wide)
+    act_grad = own_ref[rows : 2 * rows].astype(wide) + far_ref[rows : 2 * rows].astype(wide)
     bulk = 0.5 * (1.0 + lax.erf(preact * root_half))
     slope = bulk + preact * jnp.exp(-0.5 * preact * preact) * inv_root_tau
     activation = (preact * bulk).astype(narrow)
@@ -196,21 +198,19 @@
             d_pre, w_in, (((1,), (1,)), ((), ())), preferred_element_type=wide
         )
         to = slice(start * block, (start + group) * block)
-        grads = inverse * (d_normed * gain_ref[:1, to]) - flat - x_ref[:, to].astype(wide) * cross
+        grads = inverse * (d_normed * gain_ref[:1, to]) - flat - x_ref[part, :, to].astype(wide) * cross
         for index in range(start, start + group):
             x, j = index % 4, index // 4
             own = slice((index - start) * block, (index - start + 1) * block)
+            target = (x - place_ref[2]) & 3 if relative[part] else x
             sides = halves(outs[:, own], grads[:, own])
             for lane in range(3):
                 side0, side1 = (side[lane].astype(narrow) for side in sides)
                 keep = jnp.where(first, side0, side1)
                 send = jnp.where(first, side1, side0)
                 to = slice(lane * 128, lane * 128 + 128)
-                for part in range(2):
-                    at = slice(part * rows, (part + 1) * rows)
-                    target = x if part == 0 else (x - place_ref[2]) & 3
-                    out_refs[part][target, j, :, to] = keep[at]
-                    out_refs[2 + part][target, j, :, to] = send[at]
+                keep_ref[target, j, :, to] = keep
+                send_ref[target, j, :, to] = send
 
 
 def in_hbm(array):
@@ -238,11 +238,11 @@
         merge_kernel,
         ["scalar", "here", "here", "here", "here"],
         [
-            pltpu.HBM((tokens, width), narrow),
+            pltpu.HBM((2, tokens // 2, width), narrow),
             pltpu.HBM((blocks // 2, tokens, 2 * block), narrow),
             pltpu.HBM((blocks // 2, tokens, 2 * block), narrow),
             jax.ShapeDtypeStruct((8, width), wide),
-            jax.ShapeDtypeStruct((hidden, 128), narrow),
+            jax.ShapeDtypeStruct((2, hidden, 128), narrow),
         ],
         [],
         30,
@@ -253,10 +253,11 @@
 def first_call(place, shifted, grads, gains, table, panels):
     blocks, twice, hidden = panels.shape
     pairs, tokens, width = shifted.shape
-    (sums,) = call(
+    sums = jax.ShapeDtypeStruct((tokens + 16, hidden), narrow)
+    return call(
         first_kernel,
         ["scalar", "here", "here", "any", "any", "any"],
-        [jax.ShapeDtypeStruct((2 * tokens + 16, hidden), narrow)],
+        [sums, sums],
         [
             pltpu.VMEM(shifted.shape, narrow),
             pltpu.VMEM(grads.shape, narrow),
@@ -266,16 +267,14 @@
         30,
         "first",
     )(place, gains, table, in_hbm(shifted), in_hbm(grads), in_hbm(panels))
-    return sums
-
-
-def second_call(features, place, sums, far_sums, values, gains, panels):
-    block = panels.shape[1] // 2
-    part = jax.ShapeDtypeStruct((4, 2, values.shape[0] // 2, block), narrow)
+
+
+def second_call(features, part, place, sums, far_sums, values, gains, panels):
+    out = jax.ShapeDtypeStruct((4, 2, values.shape[1], panels.shape[1] // 2), narrow)
     return call(
-        functools.partial(second_kernel, features),
+        functools.partial(second_kernel, features, part),
         ["scalar", "here", "here", "here", "here", "here"],
-        [part] * 4,
+        [out, out],
         [],
         30,
         "second",
@@ -303,20 +302,26 @@
 
     values, shifted, grads, gains, table = merge_call(place, own0, own1, far0, far1, w_in.shape[1])
     sums = first_call(place, shifted, grads, gains, table, panels)
-    far_sums = lax.ppermute(sums, "l", other_core)
-    outs = second_call(features, place, sums, far_sums, values, gains, panels)
-
-    got = [lax.ppermute(send, "k", other_core) for send in outs[2:]]
+    far_sums = [lax.ppermute(part, "l", other_core) for part in sums]
+    keep, got = [], []
+    for i in range(2):
+        kept, send = second_call(features, i, place, sums[i], far_sums[i], values, gains, panels)
+        keep.append(kept)
+        got.append(lax.ppermute(send, "k", other_core))
+
     def add(a, b):
         return (a.astype(wide) + b.astype(wide)).astype(narrow)
 
-    first = lax.all_to_all(add(outs[0], got[0]), "x", 0, 0)
-    second = [add(outs[1][d], got[1][d]) for d in range(4)]
-    second = [second[0]] + [
-        lax.ppermute(second[d], "x", [(x, (x + d) % 4) for x in range(4)]) for d in (1, 3, 2)
-    ]
     shares = []
-    for i, parts in enumerate(([first[x] for x in range(4)], second)):
+    for i in range(2):
+        if relative[i]:
+            parts = [add(keep[i][d], got[i][d]) for d in range(4)]
+            parts = [parts[0]] + [
+                lax.ppermute(parts[d], "x", [(x, (x + d) % 4) for x in range(4)]) for d in (1, 3, 2)
+            ]
+        else:
+            parts = lax.all_to_all(add(keep[i], got[i]), "x", 0, 0)
+            parts = [parts[x] for x in range(4)]
         part = sum(part.astype(wide) for part in parts).astype(narrow)
         shares += [lax.ppermute(part[j], ("l", "h"), scatter_pairs(i, j)).astype(wide) for j in range(2)]
     total = (shares[0] + shares[1] + shares[2] + shares[3]).astype(narrow)

time: 162 us -> 158 us (0.975)
  the two profiles are of different devices: /device:TPU:64 before, /device:TPU:4 now
where the time goes in v6:
time: 158 us; the launch traced here: 157 us
  starting transfers between devices  69.4 us (44%)
  blocking collectives  28.8 us (18%)
  waiting for transfers between devices  21.5 us (14%)
  Pallas kernels  17.4 us (11%)
  between operations  14.4 us (9%)
  other arithmetic  4.69 us (3%)
    ppermute x6, starting transfers between devices, on_device(): lax.ppermute(parts[d], 'x', [(x, (x + d) % 4) for x in range(4)])  21.5 us
    ppermute x4, starting transfers between devices, on_device(): lax.ppermute(pack, ('l', 'h'), gather_pairs(i, j))  17.8 us
    ppermute x4, starting transfers between devices, on_device(): lax.ppermute(part[j], ('l', 'h'), scatter_pairs(i, j)).astype(wide)  16.1 us
    all_gather x1, blocking collectives, on_device(): own0 = lax.all_gather(jnp.stack(near[0]), 'x', axis=0)  15.9 us
    all_gather x1, blocking collectives, on_device(): own1 = lax.all_gather(jnp.stack(near[1]), 'x', axis=0)  12.9 us
    ppermute x4, waiting for transfers between devices, on_device(): lax.ppermute(part[j], ('l', 'h'), scatter_pairs(i, j)).astype(wide)  7.08 us
    pallas_call x1, Pallas kernels, first_call(): call(first_kernel, ['scalar', 'here', 'here', 'any', 'any', 'any'], [sums...  6 us
    pallas_call x1, Pallas kernels, merge_call(): call(merge_kernel, ['scalar', 'here', 'here', 'here', 'here'], [pltpu.HBM...  5.86 us
  transfers between devices with their start and end apart: 21, of which 6 were waited for; matrix products, arithmetic and copies ran while one was open for 2% of the time, Pallas kernels for 7%

profile of v6, /device:TPU:4, one launch (start us, length us, event | category | flops | bytes accessed | tf_op | source)
XLA Modules:
  0.0 157.1 jit_solution(5841078054694561492)
XLA Ops:
  7.2 0.0 all-gather.5.cloned.1.call-start
  7.2 1.9 %pad_maximum_fusion = bf16[768,384]{1,0:T(8,128)(2,1)} fusion(bf16[384,384]{1,0:T(8,128)(2,1)} %param.8, bf16[384,384]{1,0:T(8,128)(2,1)} %param.7), kind=kLoop, calls=%fused_computation | loop fusion | flops 1179648 | bytes 1179648 | tf_op jit(solution)/shard_map/concatenate | solution.py:291
  9.1 0.0 all-gather.5.cloned.1.call-update
  9.2 0.8 pad_maximum_fusion.4
  10.0 1.0 pad_maximum_fusion.3
  11.0 10.9 %collective-permute-start.2 = (bf16[168,384]{1,0:T(8,128)(2,1)S(1)}, bf16[168,384]{1,0:T(8,128)(2,1)S(1)}, u32[]{:S(2)}, u32[]{:S(2)}) collective-permute-start(bf16[168,384]{1,0:T(8,128)(2,1)S(1)} %pad_maximum_fusion.3), channel_id=1, source_target_pairs={{0,16},{8,24},{16,272},{24,280},{256,0},{264,8},{272,256},{280,264... | collective-permute-start | bytes 387080 | tf_op jit(solution)/shard_map/ppermute | solution.py:296
  21.9 3.4 %collective-permute-start.3 = (bf16[168,384]{1,0:T(8,128)(2,1)S(1)}, bf16[168,384]{1,0:T(8,128)(2,1)S(1)}, u32[]{:S(2)}, u32[]{:S(2)}) collective-permute-start(bf16[168,384]{1,0:T(8,128)(2,1)S(1)} %pad_maximum_fusion.3), channel_id=1, source_target_pairs={{0,24},{8,16},{16,280},{24,272},{256,8},{264,0},{272,264},{280,256... | collective-permute-start | bytes 387080 | tf_op jit(solution)/shard_map/ppermute | solution.py:296
  25.3 0.7 collective-permute-start
  26.0 2.8 %collective-permute-start.1 = (bf16[168,384]{1,0:T(8,128)(2,1)S(1)}, bf16[168,384]{1,0:T(8,128)(2,1)S(1)}, u32[]{:S(2)}, u32[]{:S(2)}) collective-permute-start(bf16[168,384]{1,0:T(8,128)(2,1)S(1)} %pad_maximum_fusion.3), channel_id=1, source_target_pairs={{0,8},{8,0},{16,264},{24,256},{256,24},{264,16},{272,280},{280,272... | collective-permute-start | bytes 387080 | tf_op jit(solution)/shard_map/ppermute | solution.py:296
  28.8 0.0 collective-permute-done.2
  28.8 2.6 %collective-permute-done.3 = bf16[168,384]{1,0:T(8,128)(2,1)S(1)} collective-permute-done((bf16[168,384]{1,0:T(8,128)(2,1)S(1)}, bf16[168,384]{1,0:T(8,128)(2,1)S(1)}, u32[]{:S(2)}, u32[]{:S(2)}) %collective-permute-start.3) | collective-permute-done | bytes 129056 | tf_op jit(solution)/shard_map/ppermute | solution.py:296
  31.5 12.9 %all-gather.1 = bf16[8,168,384]{2,1,0:T(8,128)(2,1)S(1)} all-gather(bf16[2,168,384]{2,1,0:T(8,128)(2,1)S(1)} %pad_maximum_fusion.2), channel_id=3, replica_groups=mesh['l'=2,'y'=8,'h'=4,'x'=4,'k'=2] {'x'}, dimensions={0}, use_global_device_ids=true | all-gather | bytes 1290240 | tf_op jit(solution)/shard_map/all_gather | solution.py:300
  44.3 1.9 %collective-permute-start.5 = (bf16[4,2,168,384]{3,2,1,0:T(8,128)(2,1)S(1)}, bf16[4,2,168,384]{3,2,1,0:T(8,128)(2,1)S(1)}, u32[]{:S(2)}, u32[]{:S(2)}) collective-permute-start(bf16[4,2,168,384]{3,2,1,0:T(8,128)(2,1)S(1)} %bitcast.45), channel_id=1, source_target_pairs={{0,1},{1,0},{2,3},{3,2},{4,5},{5,4},{6,7},{7,6},{8,9},{9,8},{10,11... | collective-permute-start | bytes 3096584 | tf_op jit(solution)/shard_map/ppermute | solution.py:301
  46.3 0.0 collective-permute-done
  46.3 0.0 collective-permute-done.1
  46.3 15.9 %all-gather = bf16[8,168,384]{2,1,0:T(8,128)(2,1)S(1)} all-gather(bf16[2,168,384]{2,1,0:T(8,128)(2,1)S(1)} %pad_maximum_fusion.1), channel_id=2, replica_groups=mesh['l'=2,'y'=8,'h'=4,'x'=4,'k'=2] {'x'}, dimensions={0}, use_global_device_ids=true | all-gather | bytes 1290240 | tf_op jit(solution)/shard_map/all_gather | solution.py:298
  62.3 1.9 %collective-permute-start.4 = (bf16[4,2,168,384]{3,2,1,0:T(8,128)(2,1)S(1)}, bf16[4,2,168,384]{3,2,1,0:T(8,128)(2,1)}, u32[]{:S(2)}, u32[]{:S(2)}) collective-permute-start(bf16[4,2,168,384]{3,2,1,0:T(8,128)(2,1)S(1)} %bitcast.47), channel_id=1, source_target_pairs={{0,1},{1,0},{2,3},{3,2},{4,5},{5,4},{6,7},{7,6},{8,9},{9,8},{10,11... | collective-permute-start | bytes 3096584 | tf_op jit(solution)/shard_map/ppermute | solution.py:299
  64.2 0.1 pad_add_fusion.place_ref
  64.3 0.0 collective-permute-done.5.far1
  64.3 2.6 %collective-permute-done.4.far0 = bf16[4,2,168,384]{3,2,1,0:T(8,128)(2,1)} collective-permute-done((bf16[4,2,168,384]{3,2,1,0:T(8,128)(2,1)S(1)}, bf16[4,2,168,384]{3,2,1,0:T(8,128)(2,1)}, u32[]{:S(2)}, u32[]{:S(2)}) %collective-permute-start.4) | collective-permute-done | bytes 1032224 | tf_op jit(solution)/shard_map/ppermute | solution.py:299
  66.9 5.9 %merge.1 = (bf16[2,160,3072]{2,1,0:T(8,128)(2,1)}, bf16[4,320,768]{2,1,0:T(8,128)(2,1)}, bf16[4,320,768]{2,1,0:T(8,128)(2,1)}, f32[8,3072]{1,0:T(8,128)S(1)}, bf16[2,384,128]{2,1,0:T(8,128)(2,1)S(1)}) custom-call(s32[3]{0:T(128)S(1)} %pad_add_fusion.place_ref, bf16[4,2,168,384]{3,2,1,0:T(8,128)(2,1)S(1)} %bitcast.48, bf16[4,2,168,384]{3,2,1,0:T(8,128)(2,1)S(1)} %bitcast.46, ...), custom_call_target="tpu_custom_call" | custom-call | tf_op jit(solution)/shard_map/merge/pallas_call | solution.py:237
  72.8 4.0 %all-gather.5.cloned.1.call-done = bf16[6144,384]{1,0:T(8,128)(2,1)} async-done(((bf16[768,384]{1,0:T(8,128)(2,1)}), bf16[6144,384]{1,0:T(8,128)(2,1)}) %all-gather.5.cloned.1.call-update) | async-done | bytes 4718608 | tf_op jit(solution)/shard_map/all_gather | solution.py:291
  76.8 0.0 slice-start
  76.8 0.0 slice-start.1
  76.8 6.0 %first.1 = (bf16[336,384]{1,0:T(8,128)(2,1)S(1)}, bf16[336,384]{1,0:T(8,128)(2,1)S(1)}) custom-call(s32[3]{0:T(128)S(1)} %pad_add_fusion.place_ref, f32[8,3072]{1,0:T(8,128)S(1)} %get-tuple-element.13.gain_ref, bf16[2,384,128]{2,1,0:T(8,128)(2,1)S(1)} %get-tuple-element.14.table_ref, bf16[4,320,768]{2,1,0:T(8,128)(2,1)} %get-tuple-element.15.shift_ref, ...), custom_call_target="tpu_custom_call" | custom-call | tf_op jit(solution)/shard_map/first/pallas_call | solution.py:257
  82.8 3.6 %collective-permute-start.6 = (bf16[336,384]{1,0:T(8,128)(2,1)S(1)}, bf16[336,384]{1,0:T(8,128)(2,1)S(1)}, u32[]{:S(2)}, u32[]{:S(2)}) collective-permute-start(bf16[336,384]{1,0:T(8,128)(2,1)S(1)} %get-tuple-element.17.own_ref), channel_id=1, source_target_pairs={{0,256},{256,0},{1,257},{257,1},{2,258},{258,2},{3,259},{259,3},{4... | collective-permute-start | bytes 774152 | tf_op jit(solution)/shard_map/ppermute | solution.py:305
  86.3 2.3 %collective-permute-start.13 = (bf16[336,384]{1,0:T(8,128)(2,1)S(1)}, bf16[336,384]{1,0:T(8,128)(2,1)S(1)}, u32[]{:S(2)}, u32[]{:S(2)}) collective-permute-start(bf16[336,384]{1,0:T(8,128)(2,1)S(1)} %get-tuple-element.21.own_ref), channel_id=1, source_target_pairs={{0,256},{256,0},{1,257},{257,1},{2,258},{258,2},{3,259},{259,3},{4... | collective-permute-start | bytes 774152 | tf_op jit(solution)/shard_map/ppermute | solution.py:305
  88.6 5.1 %collective-permute-done.6.far_ref = bf16[336,384]{1,0:T(8,128)(2,1)S(1)} collective-permute-done((bf16[336,384]{1,0:T(8,128)(2,1)S(1)}, bf16[336,384]{1,0:T(8,128)(2,1)S(1)}, u32[]{:S(2)}, u32[]{:S(2)}) %collective-permute-start.6) | collective-permute-done | bytes 258080 | tf_op jit(solution)/shard_map/ppermute | solution.py:305
  93.8 0.0 slice-done
  93.8 0.0 slice-done.1
  93.8 0.0 copy-done
  93.8 2.8 %second.2 = (bf16[4,2,160,384]{3,2,1,0:T(8,128)(2,1)S(1)}, bf16[4,2,160,384]{3,2,1,0:T(8,128)(2,1)S(1)}) custom-call(s32[3]{0:T(128)S(1)} %pad_add_fusion.place_ref, bf16[336,384]{1,0:T(8,128)(2,1)S(1)} %get-tuple-element.17.own_ref, bf16[336,384]{1,0:T(8,128)(2,1)S(1)} %collective-permute-done.6.far_ref, bf16[2,160,3072]{2,1,0:T(8,128)(2,1)S(1)} %copy-done, ...), custom_call_target="tpu_custom_call" | custom-call | tf_op jit(solution)/shard_map/second/pallas_call | solution.py:274
  96.6 1.9 %collective-permute-start.7 = (bf16[4,2,160,384]{3,2,1,0:T(8,128)(2,1)S(1)}, bf16[4,2,160,384]{3,2,1,0:T(8,128)(2,1)S(1)}, u32[]{:S(2)}, u32[]{:S(2)}) collective-permute-start(bf16[4,2,160,384]{3,2,1,0:T(8,128)(2,1)S(1)} %get-tuple-element.20), channel_id=1, source_target_pairs={{0,1},{1,0},{2,3},{3,2},{4,5},{5,4},{6,7},{7,6},{8,9},{9,8},{10,11... | collective-permute-start | bytes 2949128 | tf_op jit(solution)/shard_map/ppermute | solution.py:310
  98.5 0.0 collective-permute-done.13.far_ref
  98.5 2.8 %second.3 = (bf16[4,2,160,384]{3,2,1,0:T(8,128)(2,1)S(1)}, bf16[4,2,160,384]{3,2,1,0:T(8,128)(2,1)S(1)}) custom-call(s32[3]{0:T(128)S(1)} %pad_add_fusion.place_ref, bf16[336,384]{1,0:T(8,128)(2,1)S(1)} %get-tuple-element.21.own_ref, bf16[336,384]{1,0:T(8,128)(2,1)S(1)} %collective-permute-done.13.far_ref, bf16[2,160,3072]{2,1,0:T(8,128)(2,1)S(1)} %copy-done, ...), custom_call_target="tpu_custom_call" | custom-call | tf_op jit(solution)/shard_map/second/pallas_call | solution.py:274
  101.3 2.4 %collective-permute-start.14 = (bf16[4,2,160,384]{3,2,1,0:T(8,128)(2,1)S(1)}, bf16[4,2,160,384]{3,2,1,0:T(8,128)(2,1)S(1)}, u32[]{:S(2)}, u32[]{:S(2)}) collective-permute-start(bf16[4,2,160,384]{3,2,1,0:T(8,128)(2,1)S(1)} %get-tuple-element.23), channel_id=1, source_target_pairs={{0,1},{1,0},{2,3},{3,2},{4,5},{5,4},{6,7},{7,6},{8,9},{9,8},{10,11... | collective-permute-start | bytes 2949128 | tf_op jit(solution)/shard_map/ppermute | solution.py:310
  103.7 0.0 collective-permute-done.7
  103.7 0.2 fusion.7
  103.9 2.4 %collective-permute-start.10 = (bf16[2,160,384]{2,1,0:T(8,128)(2,1)S(1)}, bf16[2,160,384]{2,1,0:T(8,128)(2,1)S(1)}, u32[]{:S(2)}, u32[]{:S(2)}) collective-permute-start(bf16[2,160,384]{2,1,0:T(8,128)(2,1)S(1)} %get-tuple-element.25), channel_id=1, source_target_pairs={{0,4},{2,6},{4,0},{6,2},{1,5},{3,7},{5,1},{7,3},{8,12},{10,14},{12... | collective-permute-start | bytes 737288 | tf_op jit(solution)/shard_map/ppermute | solution.py:320
  106.4 3.9 %collective-permute-start.8 = (bf16[2,160,384]{2,1,0:T(8,128)(2,1)S(1)}, bf16[2,160,384]{2,1,0:T(8,128)(2,1)S(1)}, u32[]{:S(2)}, u32[]{:S(2)}) collective-permute-start(bf16[2,160,384]{2,1,0:T(8,128)(2,1)S(1)} %get-tuple-element.24), channel_id=1, source_target_pairs={{0,2},{2,4},{4,6},{6,0},{1,3},{3,5},{5,7},{7,1},{8,10},{10,12},{12... | collective-permute-start | bytes 737288 | tf_op jit(solution)/shard_map/ppermute | solution.py:320
  110.3 1.9 %collective-permute-start.9 = (bf16[2,160,384]{2,1,0:T(8,128)(2,1)S(1)}, bf16[2,160,384]{2,1,0:T(8,128)(2,1)S(1)}, u32[]{:S(2)}, u32[]{:S(2)}) collective-permute-start(bf16[2,160,384]{2,1,0:T(8,128)(2,1)S(1)} %get-tuple-element.26), channel_id=1, source_target_pairs={{0,6},{2,0},{4,2},{6,4},{1,7},{3,1},{5,3},{7,5},{8,14},{10,8},{12,... | collective-permute-start | bytes 737288 | tf_op jit(solution)/shard_map/ppermute | solution.py:320
  112.3 0.0 collective-permute-done.14
  112.3 0.2 fusion.11
  112.5 4.0 %collective-permute-start.15 = (bf16[2,160,384]{2,1,0:T(8,128)(2,1)S(1)}, bf16[2,160,384]{2,1,0:T(8,128)(2,1)S(1)}, u32[]{:S(2)}, u32[]{:S(2)}) collective-permute-start(bf16[2,160,384]{2,1,0:T(8,128)(2,1)S(1)} %get-tuple-element.27), channel_id=1, source_target_pairs={{0,2},{2,4},{4,6},{6,0},{1,3},{3,5},{5,7},{7,1},{8,10},{10,12},{12... | collective-permute-start | bytes 737288 | tf_op jit(solution)/shard_map/ppermute | solution.py:320
  116.5 1.9 %collective-permute-start.16 = (bf16[2,160,384]{2,1,0:T(8,128)(2,1)S(1)}, bf16[2,160,384]{2,1,0:T(8,128)(2,1)S(1)}, u32[]{:S(2)}, u32[]{:S(2)}) collective-permute-start(bf16[2,160,384]{2,1,0:T(8,128)(2,1)S(1)} %get-tuple-element.29), channel_id=1, source_target_pairs={{0,6},{2,0},{4,2},{6,4},{1,7},{3,1},{5,3},{7,5},{8,14},{10,8},{12,... | collective-permute-start | bytes 737288 | tf_op jit(solution)/shard_map/ppermute | solution.py:320
  118.5 0.0 collective-permute-done.10
  118.5 7.2 %collective-permute-start.17 = (bf16[2,160,384]{2,1,0:T(8,128)(2,1)S(1)}, bf16[2,160,384]{2,1,0:T(8,128)(2,1)S(1)}, u32[]{:S(2)}, u32[]{:S(2)}) collective-permute-start(bf16[2,160,384]{2,1,0:T(8,128)(2,1)S(1)} %get-tuple-element.28), channel_id=1, source_target_pairs={{0,4},{2,6},{4,0},{6,2},{1,5},{3,7},{5,1},{7,3},{8,12},{10,14},{12... | collective-permute-start | bytes 737288 | tf_op jit(solution)/shard_map/ppermute | solution.py:320
  125.7 0.0 collective-permute-done.8
  125.7 0.0 collective-permute-done.9
  125.7 0.2 fusion.5
  125.9 0.7 collective-permute-start.11
  126.6 4.6 %collective-permute-start.12 = (bf16[160,384]{1,0:T(8,128)(2,1)S(1)}, bf16[160,384]{1,0:T(8,128)(2,1)S(1)}, u32[]{:S(2)}, u32[]{:S(2)}) collective-permute-start(bf16[160,384]{1,0:T(8,128)(2,1)S(1)} %get-tuple-element.31), channel_id=1, source_target_pairs={{0,8},{8,0},{16,264},{24,256},{256,24},{264,16},{272,280},{280,272... | collective-permute-start | bytes 368648 | tf_op jit(solution)/shard_map/ppermute | solution.py:326
  131.2 0.0 collective-permute-done.15
  131.2 0.0 collective-permute-done.16
  131.2 0.0 collective-permute-done.17
  131.2 0.2 fusion.2
  131.4 8.4 %collective-permute-start.18 = (bf16[160,384]{1,0:T(8,128)(2,1)S(1)}, bf16[160,384]{1,0:T(8,128)(2,1)S(1)}, u32[]{:S(2)}, u32[]{:S(2)}) collective-permute-start(bf16[160,384]{1,0:T(8,128)(2,1)S(1)} %get-tuple-element.32), channel_id=1, source_target_pairs={{0,256},{8,264},{16,0},{24,8},{256,272},{264,280},{272,16},{280,24... | collective-permute-start | bytes 368648 | tf_op jit(solution)/shard_map/ppermute | solution.py:326
  139.8 2.5 %collective-permute-start.19 = (bf16[160,384]{1,0:T(8,128)(2,1)S(1)}, bf16[160,384]{1,0:T(8,128)(2,1)S(1)}, u32[]{:S(2)}, u32[]{:S(2)}) collective-permute-start(bf16[160,384]{1,0:T(8,128)(2,1)S(1)} %get-tuple-element.33), channel_id=1, source_target_pairs={{0,264},{8,256},{16,8},{24,0},{256,280},{264,272},{272,24},{280,16... | collective-permute-start | bytes 368648 | tf_op jit(solution)/shard_map/ppermute | solution.py:326
  142.3 0.0 collective-permute-done.11
  142.3 0.0 collective-permute-done.12
  142.3 4.5 %collective-permute-done.18 = bf16[160,384]{1,0:T(8,128)(2,1)S(1)} collective-permute-done((bf16[160,384]{1,0:T(8,128)(2,1)S(1)}, bf16[160,384]{1,0:T(8,128)(2,1)S(1)}, u32[]{:S(2)}, u32[]{:S(2)}) %collective-permute-start.18) | collective-permute-done | bytes 122912 | tf_op jit(solution)/shard_map/ppermute | solution.py:326
  146.8 2.6 %collective-permute-done.19 = bf16[160,384]{1,0:T(8,128)(2,1)S(1)} collective-permute-done((bf16[160,384]{1,0:T(8,128)(2,1)S(1)}, bf16[160,384]{1,0:T(8,128)(2,1)S(1)}, u32[]{:S(2)}, u32[]{:S(2)}) %collective-permute-start.19) | collective-permute-done | bytes 122912 | tf_op jit(solution)/shard_map/ppermute | solution.py:326
  149.4 0.1 add_convert_fusion.8
  149.5 0.7 fusion.14
  (7 shorter events, 0.1 us)
Async XLA Ops:
  7.2 69.6 %all-gather.5.cloned.1.call-start = ((), (), s32[]{:S(2)}) async-start(), calls=%async_computation | async-start | bytes 5308416 | tf_op jit(solution)/shard_map/all_gather | solution.py:291
  11.0 17.8 %collective-permute-start.2 = (bf16[168,384]{1,0:T(8,128)(2,1)S(1)}, bf16[168,384]{1,0:T(8,128)(2,1)S(1)}, u32[]{:S(2)}, u32[]{:S(2)}) collective-permute-start(bf16[168,384]{1,0:T(8,128)(2,1)S(1)} %pad_maximum_fusion.3), channel_id=1, source_target_pairs={{0,16},{8,24},{16,272},{24,280},{256,0},{264,8},{272,256},{280,264... | collective-permute-start | bytes 387080 | tf_op jit(solution)/shard_map/ppermute | solution.py:296
  21.9 9.5 %collective-permute-start.3 = (bf16[168,384]{1,0:T(8,128)(2,1)S(1)}, bf16[168,384]{1,0:T(8,128)(2,1)S(1)}, u32[]{:S(2)}, u32[]{:S(2)}) collective-permute-start(bf16[168,384]{1,0:T(8,128)(2,1)S(1)} %pad_maximum_fusion.3), channel_id=1, source_target_pairs={{0,24},{8,16},{16,280},{24,272},{256,8},{264,0},{272,264},{280,256... | collective-permute-start | bytes 387080 | tf_op jit(solution)/shard_map/ppermute | solution.py:296
  25.3 20.9 %collective-permute-start = (bf16[168,384]{1,0:T(8,128)(2,1)S(1)}, bf16[168,384]{1,0:T(8,128)(2,1)S(1)}, u32[]{:S(2)}, u32[]{:S(2)}) collective-permute-start(bf16[168,384]{1,0:T(8,128)(2,1)S(1)} %pad_maximum_fusion.3), channel_id=1, source_target_pairs={{0,0},{8,8},{16,256},{24,264},{256,16},{264,24},{272,272},{280,280... | collective-permute-start | bytes 387080 | tf_op jit(solution)/shard_map/ppermute | solution.py:296
  26.0 20.3 %collective-permute-start.1 = (bf16[168,384]{1,0:T(8,128)(2,1)S(1)}, bf16[168,384]{1,0:T(8,128)(2,1)S(1)}, u32[]{:S(2)}, u32[]{:S(2)}) collective-permute-start(bf16[168,384]{1,0:T(8,128)(2,1)S(1)} %pad_maximum_fusion.3), channel_id=1, source_target_pairs={{0,8},{8,0},{16,264},{24,256},{256,24},{264,16},{272,280},{280,272... | collective-permute-start | bytes 387080 | tf_op jit(solution)/shard_map/ppermute | solution.py:296
  44.3 19.9 %collective-permute-start.5 = (bf16[4,2,168,384]{3,2,1,0:T(8,128)(2,1)S(1)}, bf16[4,2,168,384]{3,2,1,0:T(8,128)(2,1)S(1)}, u32[]{:S(2)}, u32[]{:S(2)}) collective-permute-start(bf16[4,2,168,384]{3,2,1,0:T(8,128)(2,1)S(1)} %bitcast.45), channel_id=1, source_target_pairs={{0,1},{1,0},{2,3},{3,2},{4,5},{5,4},{6,7},{7,6},{8,9},{9,8},{10,11... | collective-permute-start | bytes 3096584 | tf_op jit(solution)/shard_map/ppermute | solution.py:301
  62.3 4.7 %collective-permute-start.4 = (bf16[4,2,168,384]{3,2,1,0:T(8,128)(2,1)S(1)}, bf16[4,2,168,384]{3,2,1,0:T(8,128)(2,1)}, u32[]{:S(2)}, u32[]{:S(2)}) collective-permute-start(bf16[4,2,168,384]{3,2,1,0:T(8,128)(2,1)S(1)} %bitcast.47), channel_id=1, source_target_pairs={{0,1},{1,0},{2,3},{3,2},{4,5},{5,4},{6,7},{7,6},{8,9},{9,8},{10,11... | collective-permute-start | bytes 3096584 | tf_op jit(solution)/shard_map/ppermute | solution.py:299
  76.8 17.0 %slice-start = ((s8[4718592]{0:T(1024)(128)(4,1)}), s8[4194304]{0:T(1024)(128)(4,1)S(1)}, s32[]{:S(2)}) async-start(s8[4718592]{0:T(1024)(128)(4,1)} %bitcast.41), calls=%async_computation.1 | async-start | bytes 8388608
  76.8 17.0 %slice-start.1 = ((s8[4718592]{0:T(1024)(128)(4,1)}), s8[524288]{0:T(1024)(128)(4,1)S(1)}, s32[]{:S(2)}) async-start(s8[4718592]{0:T(1024)(128)(4,1)} %bitcast.41), calls=%async_computation.2 | async-start | bytes 1048576
  76.8 17.0 %copy-start = (bf16[2,160,3072]{2,1,0:T(8,128)(2,1)S(1)}, bf16[2,160,3072]{2,1,0:T(8,128)(2,1)}, u32[]{:S(2)}) copy-start(bf16[2,160,3072]{2,1,0:T(8,128)(2,1)} %get-tuple-element.18.x_ref) | copy-start | bytes 5898244
  82.8 11.0 %collective-permute-start.6 = (bf16[336,384]{1,0:T(8,128)(2,1)S(1)}, bf16[336,384]{1,0:T(8,128)(2,1)S(1)}, u32[]{:S(2)}, u32[]{:S(2)}) collective-permute-start(bf16[336,384]{1,0:T(8,128)(2,1)S(1)} %get-tuple-element.17.own_ref), channel_id=1, source_target_pairs={{0,256},{256,0},{1,257},{257,1},{2,258},{258,2},{3,259},{259,3},{4... | collective-permute-start | bytes 774152 | tf_op jit(solution)/shard_map/ppermute | solution.py:305
  86.3 12.2 %collective-permute-start.13 = (bf16[336,384]{1,0:T(8,128)(2,1)S(1)}, bf16[336,384]{1,0:T(8,128)(2,1)S(1)}, u32[]{:S(2)}, u32[]{:S(2)}) collective-permute-start(bf16[336,384]{1,0:T(8,128)(2,1)S(1)} %get-tuple-element.21.own_ref), channel_id=1, source_target_pairs={{0,256},{256,0},{1,257},{257,1},{2,258},{258,2},{3,259},{259,3},{4... | collective-permute-start | bytes 774152 | tf_op jit(solution)/shard_map/ppermute | solution.py:305
  96.6 7.1 %collective-permute-start.7 = (bf16[4,2,160,384]{3,2,1,0:T(8,128)(2,1)S(1)}, bf16[4,2,160,384]{3,2,1,0:T(8,128)(2,1)S(1)}, u32[]{:S(2)}, u32[]{:S(2)}) collective-permute-start(bf16[4,2,160,384]{3,2,1,0:T(8,128)(2,1)S(1)} %get-tuple-element.20), channel_id=1, source_target_pairs={{0,1},{1,0},{2,3},{3,2},{4,5},{5,4},{6,7},{7,6},{8,9},{9,8},{10,11... | collective-permute-start | bytes 2949128 | tf_op jit(solution)/shard_map/ppermute | solution.py:310
  101.3 10.9 %collective-permute-start.14 = (bf16[4,2,160,384]{3,2,1,0:T(8,128)(2,1)S(1)}, bf16[4,2,160,384]{3,2,1,0:T(8,128)(2,1)S(1)}, u32[]{:S(2)}, u32[]{:S(2)}) collective-permute-start(bf16[4,2,160,384]{3,2,1,0:T(8,128)(2,1)S(1)} %get-tuple-element.23), channel_id=1, source_target_pairs={{0,1},{1,0},{2,3},{3,2},{4,5},{5,4},{6,7},{7,6},{8,9},{9,8},{10,11... | collective-permute-start | bytes 2949128 | tf_op jit(solution)/shard_map/ppermute | solution.py:310
  103.9 14.5 %collective-permute-start.10 = (bf16[2,160,384]{2,1,0:T(8,128)(2,1)S(1)}, bf16[2,160,384]{2,1,0:T(8,128)(2,1)S(1)}, u32[]{:S(2)}, u32[]{:S(2)}) collective-permute-start(bf16[2,160,384]{2,1,0:T(8,128)(2,1)S(1)} %get-tuple-element.25), channel_id=1, source_target_pairs={{0,4},{2,6},{4,0},{6,2},{1,5},{3,7},{5,1},{7,3},{8,12},{10,14},{12... | collective-permute-start | bytes 737288 | tf_op jit(solution)/shard_map/ppermute | solution.py:320
  106.4 19.3 %collective-permute-start.8 = (bf16[2,160,384]{2,1,0:T(8,128)(2,1)S(1)}, bf16[2,160,384]{2,1,0:T(8,128)(2,1)S(1)}, u32[]{:S(2)}, u32[]{:S(2)}) collective-permute-start(bf16[2,160,384]{2,1,0:T(8,128)(2,1)S(1)} %get-tuple-element.24), channel_id=1, source_target_pairs={{0,2},{2,4},{4,6},{6,0},{1,3},{3,5},{5,7},{7,1},{8,10},{10,12},{12... | collective-permute-start | bytes 737288 | tf_op jit(solution)/shard_map/ppermute | solution.py:320
  110.3 15.4 %collective-permute-start.9 = (bf16[2,160,384]{2,1,0:T(8,128)(2,1)S(1)}, bf16[2,160,384]{2,1,0:T(8,128)(2,1)S(1)}, u32[]{:S(2)}, u32[]{:S(2)}) collective-permute-start(bf16[2,160,384]{2,1,0:T(8,128)(2,1)S(1)} %get-tuple-element.26), channel_id=1, source_target_pairs={{0,6},{2,0},{4,2},{6,4},{1,7},{3,1},{5,3},{7,5},{8,14},{10,8},{12,... | collective-permute-start | bytes 737288 | tf_op jit(solution)/shard_map/ppermute | solution.py:320
  112.5 18.7 %collective-permute-start.15 = (bf16[2,160,384]{2,1,0:T(8,128)(2,1)S(1)}, bf16[2,160,384]{2,1,0:T(8,128)(2,1)S(1)}, u32[]{:S(2)}, u32[]{:S(2)}) collective-permute-start(bf16[2,160,384]{2,1,0:T(8,128)(2,1)S(1)} %get-tuple-element.27), channel_id=1, source_target_pairs={{0,2},{2,4},{4,6},{6,0},{1,3},{3,5},{5,7},{7,1},{8,10},{10,12},{12... | collective-permute-start | bytes 737288 | tf_op jit(solution)/shard_map/ppermute | solution.py:320
  116.5 14.7 %collective-permute-start.16 = (bf16[2,160,384]{2,1,0:T(8,128)(2,1)S(1)}, bf16[2,160,384]{2,1,0:T(8,128)(2,1)S(1)}, u32[]{:S(2)}, u32[]{:S(2)}) collective-permute-start(bf16[2,160,384]{2,1,0:T(8,128)(2,1)S(1)} %get-tuple-element.29), channel_id=1, source_target_pairs={{0,6},{2,0},{4,2},{6,4},{1,7},{3,1},{5,3},{7,5},{8,14},{10,8},{12,... | collective-permute-start | bytes 737288 | tf_op jit(solution)/shard_map/ppermute | solution.py:320
  118.5 12.8 %collective-permute-start.17 = (bf16[2,160,384]{2,1,0:T(8,128)(2,1)S(1)}, bf16[2,160,384]{2,1,0:T(8,128)(2,1)S(1)}, u32[]{:S(2)}, u32[]{:S(2)}) collective-permute-start(bf16[2,160,384]{2,1,0:T(8,128)(2,1)S(1)} %get-tuple-element.28), channel_id=1, source_target_pairs={{0,4},{2,6},{4,0},{6,2},{1,5},{3,7},{5,1},{7,3},{8,12},{10,14},{12... | collective-permute-start | bytes 737288 | tf_op jit(solution)/shard_map/ppermute | solution.py:320
  125.9 16.4 %collective-permute-start.11 = (bf16[160,384]{1,0:T(8,128)(2,1)S(1)}, bf16[160,384]{1,0:T(8,128)(2,1)S(1)}, u32[]{:S(2)}, u32[]{:S(2)}) collective-permute-start(bf16[160,384]{1,0:T(8,128)(2,1)S(1)} %get-tuple-element.30), channel_id=1, source_target_pairs={{0,0},{8,8},{16,256},{24,264},{256,16},{264,24},{272,272},{280,280... | collective-permute-start | bytes 368648 | tf_op jit(solution)/shard_map/ppermute | solution.py:326
  126.6 15.7 %collective-permute-start.12 = (bf16[160,384]{1,0:T(8,128)(2,1)S(1)}, bf16[160,384]{1,0:T(8,128)(2,1)S(1)}, u32[]{:S(2)}, u32[]{:S(2)}) collective-permute-start(bf16[160,384]{1,0:T(8,128)(2,1)S(1)} %get-tuple-element.31), channel_id=1, source_target_pairs={{0,8},{8,0},{16,264},{24,256},{256,24},{264,16},{272,280},{280,272... | collective-permute-start | bytes 368648 | tf_op jit(solution)/shard_map/ppermute | solution.py:326
  131.4 15.4 %collective-permute-start.18 = (bf16[160,384]{1,0:T(8,128)(2,1)S(1)}, bf16[160,384]{1,0:T(8,128)(2,1)S(1)}, u32[]{:S(2)}, u32[]{:S(2)}) collective-permute-start(bf16[160,384]{1,0:T(8,128)(2,1)S(1)} %get-tuple-element.32), channel_id=1, source_target_pairs={{0,256},{8,264},{16,0},{24,8},{256,272},{264,280},{272,16},{280,24... | collective-permute-start | bytes 368648 | tf_op jit(solution)/shard_map/ppermute | solution.py:326
  139.8 9.6 %collective-permute-start.19 = (bf16[160,384]{1,0:T(8,128)(2,1)S(1)}, bf16[160,384]{1,0:T(8,128)(2,1)S(1)}, u32[]{:S(2)}, u32[]{:S(2)}) collective-permute-start(bf16[160,384]{1,0:T(8,128)(2,1)S(1)} %get-tuple-element.33), channel_id=1, source_target_pairs={{0,264},{8,256},{16,8},{24,0},{256,280},{264,272},{272,24},{280,16... | collective-permute-start | bytes 368648 | tf_op jit(solution)/shard_map/ppermute | solution.py:326
Sparse Core Ops, SparseCore 0:
  10.1 66.6 all-gather.4

commit v7 on v6

--- a/solution.py
+++ b/solution.py
@@ -13,8 +13,6 @@
 epsilon = 1e-06
 narrow = jnp.bfloat16
 wide = jnp.float32
-relative = (True, True)
-
 
 def pairs_of(target):
     pairs = []
@@ -73,7 +71,6 @@
 
     table_ref[...] = jnp.zeros_like(table_ref)
     for part, (own, far) in enumerate(((own0, far0), (own1, far1))):
-        at = slice(part * rows, (part + 1) * rows)
         total = jnp.zeros((rows, 128), wide)
         for index in range(blocks):
             x, j = index % 4, index // 4
@@ -81,7 +78,7 @@
             values, grads = sides(own[x, j, :rows], far[x, j, :rows])
             x_ref[part, :, to] = values
             wide_to = slice(index % 2 * block, (index % 2 + 1) * block)
-            g_ref[index // 2, at, wide_to] = grads
+            g_ref[part, index // 2, :, wide_to] = grads
             for lane in range(0, block, 128):
                 total = total + values[:, lane : lane + 128].astype(wide)
             if part == 0:
@@ -92,7 +89,7 @@
             shifted = x_ref[part, :, lane : lane + 128].astype(wide) - mean
             spread = spread + shifted * shifted
             pair, to = lane // (2 * block), lane % (2 * block)
-            shift_ref[pair, at, to : to + 128] = (shifted * gain_ref[:1, lane : lane + 128]).astype(narrow)
+            shift_ref[part, pair, :, to : to + 128] = (shifted * gain_ref[:1, lane : lane + 128]).astype(narrow)
         columns = split3(mean) + split3(jnp.sum(spread, axis=1, keepdims=True))
         lane = lax.broadcasted_iota(jnp.int32, (rows, 128), 1)
         table = jnp.zeros((rows, 128), wide)
@@ -102,20 +99,20 @@
 
 
 def first_kernel(
-    place_ref, gain_ref, table_ref, shift_ref, g_ref, panel_ref, sums0_ref, sums1_ref,
+    part, place_ref, gain_ref, table_ref, shift_ref, g_ref, panel_ref, sums_ref,
     shift_s, g_s, panel_s, sems,
 ):
-    pairs, tokens, width = shift_ref.shape
+    pairs, rows, width = shift_s.shape
     block = width // 2
     flip = place_ref[1]
 
+    def panels_at(pair):
+        return panel_ref.at[pl.ds(((pair // 2 ^ flip) * 2 + pair % 2) * 2, 2)]
+
     def fetch(pair):
-        at = (pair // 2 ^ flip) * 2 + pair % 2
-        moves = (
-            (shift_ref.at[pair], shift_s.at[pair]),
-            (g_ref.at[pair], g_s.at[pair]),
-            (panel_ref.at[pl.ds(at * 2, 2)], panel_s.at[pair]),
-        )
+        moves = [(shift_ref.at[part, pair], shift_s.at[pair]), (g_ref.at[part, pair], g_s.at[pair])]
+        if part == 0:
+            moves.append((panels_at(pair), panel_s.at[pair]))
         return [
             pltpu.make_async_copy(source, target, sems.at[pair, i])
             for i, (source, target) in enumerate(moves)
@@ -130,25 +127,23 @@
         for copy in fetch(pair):
             copy.wait()
         to = slice(pair * width, (pair + 1) * width)
-        w_in = panel_s[pair, :, :block].reshape(width, -1)
-        w_out = jnp.concatenate([panel_s[pair, i, block:] for i in range(2)], axis=1)
+        panel = panel_s[pair] if part == 0 else panels_at(pair)[...]
+        w_in = panel[:, :block].reshape(width, -1)
+        w_out = jnp.concatenate([panel[i, block:] for i in range(2)], axis=1)
         p = jnp.dot(shift_s[pair], w_in, preferred_element_type=wide)
         a = lax.dot_general(g_s[pair], w_out, (((1,), (1,)), ((), ())), preferred_element_type=wide)
         v = jnp.dot(gain_ref[:, to].astype(narrow), w_in, preferred_element_type=wide)
         pre, act, gain_sum = (p, a, v) if pre is None else (pre + p, act + a, gain_sum + v)
 
-    rows = tokens // 2
+    sums_ref[:rows] = pre.astype(narrow)
+    sums_ref[rows : 2 * rows] = act.astype(narrow)
+    lines = lax.dot_general(
+        ones_diagonal(16, 128), table_ref[part], (((1,), (1,)), ((), ())), preferred_element_type=wide
+    )
     high = gain_sum[:1].astype(narrow).astype(wide)
-    for part, sums_ref in enumerate((sums0_ref, sums1_ref)):
-        at = slice(part * rows, (part + 1) * rows)
-        sums_ref[:rows] = pre[at].astype(narrow)
-        sums_ref[rows:tokens] = act[at].astype(narrow)
-        lines = lax.dot_general(
-            ones_diagonal(16, 128), table_ref[part], (((1,), (1,)), ((), ())), preferred_element_type=wide
-        )
-        row = lax.broadcasted_iota(jnp.int32, lines.shape, 0)
-        lines = jnp.where(row == 6, high, jnp.where(row == 7, gain_sum[:1] - high, lines))
-        sums_ref[tokens:] = lines.astype(narrow)
+    row = lax.broadcasted_iota(jnp.int32, lines.shape, 0)
+    lines = jnp.where(row == 6, high, jnp.where(row == 7, gain_sum[:1] - high, lines))
+    sums_ref[2 * rows :] = lines.astype(narrow)
 
 
 def second_kernel(
@@ -202,7 +197,7 @@
         for index in range(start, start + group):
             x, j = index % 4, index // 4
             own = slice((index - start) * block, (index - start + 1) * block)
-            target = (x - place_ref[2]) & 3 if relative[part] else x
+            target = (x - place_ref[2]) & 3
             sides = halves(outs[:, own], grads[:, own])
             for lane in range(3):
                 side0, side1 = (side[lane].astype(narrow) for side in sides)
@@ -239,8 +234,8 @@
         ["scalar", "here", "here", "here", "here"],
         [
             pltpu.HBM((2, tokens // 2, width), narrow),
-            pltpu.HBM((blocks // 2, tokens, 2 * block), narrow),
-            pltpu.HBM((blocks // 2, tokens, 2 * block), narrow),
+            pltpu.HBM((2, blocks // 2, tokens // 2, 2 * block), narrow),
+            pltpu.HBM((2, blocks // 2, tokens // 2, 2 * block), narrow),
             jax.ShapeDtypeStruct((8, width), wide),
             jax.ShapeDtypeStruct((2, hidden, 128), narrow),
         ],
@@ -250,23 +245,24 @@
     )(place, own0, own1, far0, far1)
 
 
-def first_call(place, shifted, grads, gains, table, panels):
+def first_call(part, place, shifted, grads, gains, table, panels):
     blocks, twice, hidden = panels.shape
-    pairs, tokens, width = shifted.shape
-    sums = jax.ShapeDtypeStruct((tokens + 16, hidden), narrow)
-    return call(
-        first_kernel,
-        ["scalar", "here", "here", "any", "any", "any"],
-        [sums, sums],
+    _, pairs, rows, width = shifted.shape
+    panel_copy = (pairs, blocks // pairs, twice, hidden) if part == 0 else (1, 16, 128)
+    (sums,) = call(
+        functools.partial(first_kernel, part),
+        ["scalar", "here", "here", "any", "any", "here" if part else "any"],
+        [jax.ShapeDtypeStruct((2 * rows + 16, hidden), narrow)],
         [
-            pltpu.VMEM(shifted.shape, narrow),
-            pltpu.VMEM(grads.shape, narrow),
-            pltpu.VMEM((pairs, blocks // pairs, twice, hidden), narrow),
+            pltpu.VMEM((pairs, rows, width), narrow),
+            pltpu.VMEM((pairs, rows, width), narrow),
+            pltpu.VMEM(panel_copy, narrow),
             pltpu.SemaphoreType.DMA((pairs, 3)),
         ],
         30,
         "first",
-    )(place, gains, table, in_hbm(shifted), in_hbm(grads), in_hbm(panels))
+    )(place, gains, table, in_hbm(shifted), in_hbm(grads), panels if part else in_hbm(panels))
+    return sums
 
 
 def second_call(features, part, place, sums, far_sums, values, gains, panels):
@@ -301,7 +297,7 @@
     far1 = lax.ppermute(own1, "k", other_core)
 
     values, shifted, grads, gains, table = merge_call(place, own0, own1, far0, far1, w_in.shape[1])
-    sums = first_call(place, shifted, grads, gains, table, panels)
+    sums = [first_call(i, place, shifted, grads, gains, table, panels) for i in range(2)]
     far_sums = [lax.ppermute(part, "l", other_core) for part in sums]
     keep, got = [], []
     for i in range(2):
@@ -314,14 +310,10 @@
 
     shares = []
     for i in range(2):
-        if relative[i]:
-            parts = [add(keep[i][d], got[i][d]) for d in range(4)]
-            parts = [parts[0]] + [
-                lax.ppermute(parts[d], "x", [(x, (x + d) % 4) for x in range(4)]) for d in (1, 3, 2)
-            ]
-        else:
-            parts = lax.all_to_all(add(keep[i], got[i]), "x", 0, 0)
-            parts = [parts[x] for x in range(4)]
+        parts = [add(keep[i][d], got[i][d]) for d in range(4)]
+        parts = [parts[0]] + [
+            lax.ppermute(parts[d], "x", [(x, (x + d) % 4) for x in range(4)]) for d in (3, 1, 2)
+        ]
         part = sum(part.astype(wide) for part in parts).astype(narrow)
         shares += [lax.ppermute(part[j], ("l", "h"), scatter_pairs(i, j)).astype(wide) for j in range(2)]
     total = (shares[0] + shares[1] + shares[2] + shares[3]).astype(narrow)

time: 158 us -> 157 us (level)
  the two profiles are of different devices: /device:TPU:4 before, /device:TPU:26 now
where the time goes in v7:
time: 157 us
  starting transfers between devices  67.2 us (43%)
  blocking collectives  30.6 us (19%)
  Pallas kernels  20.3 us (13%)
  waiting for transfers between devices  18.7 us (12%)
  between operations  14.4 us (9%)
  other arithmetic  4.69 us (3%)
    ppermute x6, starting transfers between devices, on_device(): lax.ppermute(parts[d], 'x', [(x, (x + d) % 4) for x in range(4)])  21.5 us
    ppermute x4, starting transfers between devices, on_device(): lax.ppermute(pack, ('l', 'h'), gather_pairs(i, j))  17.8 us
    all_gather x1, blocking collectives, on_device(): own0 = lax.all_gather(jnp.stack(near[0]), 'x', axis=0)  15.3 us
    all_gather x1, blocking collectives, on_device(): own1 = lax.all_gather(jnp.stack(near[1]), 'x', axis=0)  15.2 us
    ppermute x4, starting transfers between devices, on_device(): lax.ppermute(part[j], ('l', 'h'), scatter_pairs(i, j)).astype(wide)  13.9 us
    pallas_call x2, Pallas kernels, first_call(): call(functools.partial(first_kernel, part), ['scalar', 'here', 'here', 'a...  8.84 us
    ppermute x4, waiting for transfers between devices, on_device(): lax.ppermute(part[j], ('l', 'h'), scatter_pairs(i, j)).astype(wide)  7.08 us
    ppermute x2, starting transfers between devices, on_device(): far_sums = [lax.ppermute(part, 'l', other_core) for part in sums]  6.34 us
  transfers between devices with their start and end apart: 21, of which 8 were waited for; matrix products, arithmetic and copies ran while one was open for 2% of the time, Pallas kernels for 10%

profile of v7, /device:TPU:26, one launch (start us, length us, event | category | flops | bytes accessed | tf_op | source)
XLA Modules:
  0.0 156.6 jit_solution(3712620562498523697)
XLA Ops:
  7.2 0.0 all-gather.5.cloned.1.call-start
  7.2 1.9 %pad_maximum_fusion = bf16[768,384]{1,0:T(8,128)(2,1)} fusion(bf16[384,384]{1,0:T(8,128)(2,1)} %param.8, bf16[384,384]{1,0:T(8,128)(2,1)} %param.7), kind=kLoop, calls=%fused_computation | loop fusion | flops 1179648 | bytes 1179648 | tf_op jit(solution)/shard_map/concatenate | solution.py:287
  9.1 0.0 all-gather.5.cloned.1.call-update
  9.2 0.8 pad_maximum_fusion.4
  10.0 1.0 pad_maximum_fusion.3
  11.0 10.9 %collective-permute-start.2 = (bf16[168,384]{1,0:T(8,128)(2,1)S(1)}, bf16[168,384]{1,0:T(8,128)(2,1)S(1)}, u32[]{:S(2)}, u32[]{:S(2)}) collective-permute-start(bf16[168,384]{1,0:T(8,128)(2,1)S(1)} %pad_maximum_fusion.3), channel_id=1, source_target_pairs={{0,16},{8,24},{16,272},{24,280},{256,0},{264,8},{272,256},{280,264... | collective-permute-start | bytes 387080 | tf_op jit(solution)/shard_map/ppermute | solution.py:292
  21.9 3.4 %collective-permute-start.3 = (bf16[168,384]{1,0:T(8,128)(2,1)S(1)}, bf16[168,384]{1,0:T(8,128)(2,1)S(1)}, u32[]{:S(2)}, u32[]{:S(2)}) collective-permute-start(bf16[168,384]{1,0:T(8,128)(2,1)S(1)} %pad_maximum_fusion.3), channel_id=1, source_target_pairs={{0,24},{8,16},{16,280},{24,272},{256,8},{264,0},{272,264},{280,256... | collective-permute-start | bytes 387080 | tf_op jit(solution)/shard_map/ppermute | solution.py:292
  25.3 0.7 collective-permute-start
  26.0 2.8 %collective-permute-start.1 = (bf16[168,384]{1,0:T(8,128)(2,1)S(1)}, bf16[168,384]{1,0:T(8,128)(2,1)S(1)}, u32[]{:S(2)}, u32[]{:S(2)}) collective-permute-start(bf16[168,384]{1,0:T(8,128)(2,1)S(1)} %pad_maximum_fusion.3), channel_id=1, source_target_pairs={{0,8},{8,0},{16,264},{24,256},{256,24},{264,16},{272,280},{280,272... | collective-permute-start | bytes 387080 | tf_op jit(solution)/shard_map/ppermute | solution.py:292
  28.8 0.0 collective-permute-done.2
  28.8 2.6 %collective-permute-done.3 = bf16[168,384]{1,0:T(8,128)(2,1)S(1)} collective-permute-done((bf16[168,384]{1,0:T(8,128)(2,1)S(1)}, bf16[168,384]{1,0:T(8,128)(2,1)S(1)}, u32[]{:S(2)}, u32[]{:S(2)}) %collective-permute-start.3) | collective-permute-done | bytes 129056 | tf_op jit(solution)/shard_map/ppermute | solution.py:292
  31.5 15.2 %all-gather.1 = bf16[8,168,384]{2,1,0:T(8,128)(2,1)S(1)} all-gather(bf16[2,168,384]{2,1,0:T(8,128)(2,1)S(1)} %pad_maximum_fusion.2), channel_id=3, replica_groups=mesh['l'=2,'y'=8,'h'=4,'x'=4,'k'=2] {'x'}, dimensions={0}, use_global_device_ids=true | all-gather | bytes 1290240 | tf_op jit(solution)/shard_map/all_gather | solution.py:296
  46.7 1.9 %collective-permute-start.5 = (bf16[4,2,168,384]{3,2,1,0:T(8,128)(2,1)S(1)}, bf16[4,2,168,384]{3,2,1,0:T(8,128)(2,1)S(1)}, u32[]{:S(2)}, u32[]{:S(2)}) collective-permute-start(bf16[4,2,168,384]{3,2,1,0:T(8,128)(2,1)S(1)} %bitcast.44), channel_id=1, source_target_pairs={{0,1},{1,0},{2,3},{3,2},{4,5},{5,4},{6,7},{7,6},{8,9},{9,8},{10,11... | collective-permute-start | bytes 3096584 | tf_op jit(solution)/shard_map/ppermute | solution.py:297
  48.6 0.0 collective-permute-done
  48.7 0.0 collective-permute-done.1
  48.7 15.3 %all-gather = bf16[8,168,384]{2,1,0:T(8,128)(2,1)S(1)} all-gather(bf16[2,168,384]{2,1,0:T(8,128)(2,1)S(1)} %pad_maximum_fusion.1), channel_id=2, replica_groups=mesh['l'=2,'y'=8,'h'=4,'x'=4,'k'=2] {'x'}, dimensions={0}, use_global_device_ids=true | all-gather | bytes 1290240 | tf_op jit(solution)/shard_map/all_gather | solution.py:294
  64.0 1.9 %collective-permute-start.4 = (bf16[4,2,168,384]{3,2,1,0:T(8,128)(2,1)S(1)}, bf16[4,2,168,384]{3,2,1,0:T(8,128)(2,1)}, u32[]{:S(2)}, u32[]{:S(2)}) collective-permute-start(bf16[4,2,168,384]{3,2,1,0:T(8,128)(2,1)S(1)} %bitcast.46), channel_id=1, source_target_pairs={{0,1},{1,0},{2,3},{3,2},{4,5},{5,4},{6,7},{7,6},{8,9},{9,8},{10,11... | collective-permute-start | bytes 3096584 | tf_op jit(solution)/shard_map/ppermute | solution.py:295
  66.0 0.1 pad_add_fusion.place_ref
  66.0 0.0 collective-permute-done.5.far1
  66.1 2.6 %collective-permute-done.4.far0 = bf16[4,2,168,384]{3,2,1,0:T(8,128)(2,1)} collective-permute-done((bf16[4,2,168,384]{3,2,1,0:T(8,128)(2,1)S(1)}, bf16[4,2,168,384]{3,2,1,0:T(8,128)(2,1)}, u32[]{:S(2)}, u32[]{:S(2)}) %collective-permute-start.4) | collective-permute-done | bytes 1032224 | tf_op jit(solution)/shard_map/ppermute | solution.py:295
  68.7 5.8 %merge.1 = (bf16[2,160,3072]{2,1,0:T(8,128)(2,1)}, bf16[2,4,160,768]{3,2,1,0:T(8,128)(2,1)}, bf16[2,4,160,768]{3,2,1,0:T(8,128)(2,1)}, f32[8,3072]{1,0:T(8,128)S(1)}, bf16[2,384,128]{2,1,0:T(8,128)(2,1)S(1)}) custom-call(s32[3]{0:T(128)S(1)} %pad_add_fusion.place_ref, bf16[4,2,168,384]{3,2,1,0:T(8,128)(2,1)S(1)} %bitcast.47, ...), custom_call_target="tpu_custom_call" | custom-call | tf_op jit(solution)/shard_map/merge/pallas_call | solution.py:232
  74.5 1.8 %all-gather.5.cloned.1.call-done = bf16[6144,384]{1,0:T(8,128)(2,1)} async-done(((bf16[768,384]{1,0:T(8,128)(2,1)}), bf16[6144,384]{1,0:T(8,128)(2,1)}) %all-gather.5.cloned.1.call-update) | async-done | bytes 4718608 | tf_op jit(solution)/shard_map/all_gather | solution.py:287
  76.4 0.0 copy-start
  76.4 4.9 %first.2.own_ref = bf16[336,384]{1,0:T(8,128)(2,1)S(1)} custom-call(s32[3]{0:T(128)S(1)} %pad_add_fusion.place_ref, f32[8,3072]{1,0:T(8,128)S(1)} %get-tuple-element.11.gain_ref, bf16[2,384,128]{2,1,0:T(8,128)(2,1)S(1)} %get-tuple-element.12.table_ref, bf16[2,4,160,768]{3,2,1,0:T(8,128)(2,1)} %get-tuple-element.13.shift_ref, ...), custom_call_target="tpu_custom_call" | custom-call | tf_op jit(solution)/shard_map/first/pallas_call | solution.py:252
  81.3 0.0 copy-start.1
  81.3 4.4 %collective-permute-start.6 = (bf16[336,384]{1,0:T(8,128)(2,1)S(1)}, bf16[336,384]{1,0:T(8,128)(2,1)S(1)}, u32[]{:S(2)}, u32[]{:S(2)}) collective-permute-start(bf16[336,384]{1,0:T(8,128)(2,1)S(1)} %first.2.own_ref), channel_id=1, source_target_pairs={{0,256},{256,0},{1,257},{257,1},{2,258},{258,2},{3,259},{259,3},{4... | collective-permute-start | bytes 774152 | tf_op jit(solution)/shard_map/ppermute | solution.py:301
  85.7 0.0 copy-done
  85.7 4.0 %first.3.own_ref = bf16[336,384]{1,0:T(8,128)(2,1)S(1)} custom-call(s32[3]{0:T(128)S(1)} %pad_add_fusion.place_ref, f32[8,3072]{1,0:T(8,128)S(1)} %get-tuple-element.11.gain_ref, bf16[2,384,128]{2,1,0:T(8,128)(2,1)S(1)} %get-tuple-element.12.table_ref, bf16[2,4,160,768]{3,2,1,0:T(8,128)(2,1)} %get-tuple-element.13.shift_ref, ...), custom_call_target="tpu_custom_call" | custom-call | tf_op jit(solution)/shard_map/first/pallas_call | solution.py:252
  89.7 1.9 %collective-permute-start.13 = (bf16[336,384]{1,0:T(8,128)(2,1)S(1)}, bf16[336,384]{1,0:T(8,128)(2,1)S(1)}, u32[]{:S(2)}, u32[]{:S(2)}) collective-permute-start(bf16[336,384]{1,0:T(8,128)(2,1)S(1)} %first.3.own_ref), channel_id=1, source_target_pairs={{0,256},{256,0},{1,257},{257,1},{2,258},{258,2},{3,259},{259,3},{4... | collective-permute-start | bytes 774152 | tf_op jit(solution)/shard_map/ppermute | solution.py:301
  91.6 0.6 collective-permute-done.6.far_ref
  92.2 0.0 copy-done.1
  92.2 2.8 %second.2 = (bf16[4,2,160,384]{3,2,1,0:T(8,128)(2,1)S(1)}, bf16[4,2,160,384]{3,2,1,0:T(8,128)(2,1)S(1)}) custom-call(s32[3]{0:T(128)S(1)} %pad_add_fusion.place_ref, bf16[336,384]{1,0:T(8,128)(2,1)S(1)} %first.2.own_ref, bf16[336,384]{1,0:T(8,128)(2,1)S(1)} %collective-permute-done.6.far_ref, bf16[2,160,3072]{2,1,0:T(8,128)(2,1)S(1)} %copy-done.1, ...), custom_call_target="tpu_custom_call" | custom-call | tf_op jit(solution)/shard_map/second/pallas_call | solution.py:270
  95.0 1.9 %collective-permute-start.7 = (bf16[4,2,160,384]{3,2,1,0:T(8,128)(2,1)S(1)}, bf16[4,2,160,384]{3,2,1,0:T(8,128)(2,1)S(1)}, u32[]{:S(2)}, u32[]{:S(2)}) collective-permute-start(bf16[4,2,160,384]{3,2,1,0:T(8,128)(2,1)S(1)} %get-tuple-element.17), channel_id=1, source_target_pairs={{0,1},{1,0},{2,3},{3,2},{4,5},{5,4},{6,7},{7,6},{8,9},{9,8},{10,11... | collective-permute-start | bytes 2949128 | tf_op jit(solution)/shard_map/ppermute | solution.py:306
  96.9 2.6 %collective-permute-done.13.far_ref = bf16[336,384]{1,0:T(8,128)(2,1)S(1)} collective-permute-done((bf16[336,384]{1,0:T(8,128)(2,1)S(1)}, bf16[336,384]{1,0:T(8,128)(2,1)S(1)}, u32[]{:S(2)}, u32[]{:S(2)}) %collective-permute-start.13) | collective-permute-done | bytes 258080 | tf_op jit(solution)/shard_map/ppermute | solution.py:301
  99.5 2.8 %second.3 = (bf16[4,2,160,384]{3,2,1,0:T(8,128)(2,1)S(1)}, bf16[4,2,160,384]{3,2,1,0:T(8,128)(2,1)S(1)}) custom-call(s32[3]{0:T(128)S(1)} %pad_add_fusion.place_ref, bf16[336,384]{1,0:T(8,128)(2,1)S(1)} %first.3.own_ref, bf16[336,384]{1,0:T(8,128)(2,1)S(1)} %collective-permute-done.13.far_ref, bf16[2,160,3072]{2,1,0:T(8,128)(2,1)S(1)} %copy-done.1, ...), custom_call_target="tpu_custom_call" | custom-call | tf_op jit(solution)/shard_map/second/pallas_call | solution.py:270
  102.3 1.9 %collective-permute-start.14 = (bf16[4,2,160,384]{3,2,1,0:T(8,128)(2,1)S(1)}, bf16[4,2,160,384]{3,2,1,0:T(8,128)(2,1)S(1)}, u32[]{:S(2)}, u32[]{:S(2)}) collective-permute-start(bf16[4,2,160,384]{3,2,1,0:T(8,128)(2,1)S(1)} %get-tuple-element.19), channel_id=1, source_target_pairs={{0,1},{1,0},{2,3},{3,2},{4,5},{5,4},{6,7},{7,6},{8,9},{9,8},{10,11... | collective-permute-start | bytes 2949128 | tf_op jit(solution)/shard_map/ppermute | solution.py:306
  104.2 0.0 collective-permute-done.7
  104.3 0.2 fusion.7
  104.5 4.0 %collective-permute-start.10 = (bf16[2,160,384]{2,1,0:T(8,128)(2,1)S(1)}, bf16[2,160,384]{2,1,0:T(8,128)(2,1)S(1)}, u32[]{:S(2)}, u32[]{:S(2)}) collective-permute-start(bf16[2,160,384]{2,1,0:T(8,128)(2,1)S(1)} %get-tuple-element.21), channel_id=1, source_target_pairs={{0,4},{2,6},{4,0},{6,2},{1,5},{3,7},{5,1},{7,3},{8,12},{10,14},{12... | collective-permute-start | bytes 737288 | tf_op jit(solution)/shard_map/ppermute | solution.py:315
  108.5 2.3 %collective-permute-start.8 = (bf16[2,160,384]{2,1,0:T(8,128)(2,1)S(1)}, bf16[2,160,384]{2,1,0:T(8,128)(2,1)S(1)}, u32[]{:S(2)}, u32[]{:S(2)}) collective-permute-start(bf16[2,160,384]{2,1,0:T(8,128)(2,1)S(1)} %get-tuple-element.20), channel_id=1, source_target_pairs={{0,6},{2,0},{4,2},{6,4},{1,7},{3,1},{5,3},{7,5},{8,14},{10,8},{12,... | collective-permute-start | bytes 737288 | tf_op jit(solution)/shard_map/ppermute | solution.py:315
  110.8 3.5 %collective-permute-start.9 = (bf16[2,160,384]{2,1,0:T(8,128)(2,1)S(1)}, bf16[2,160,384]{2,1,0:T(8,128)(2,1)S(1)}, u32[]{:S(2)}, u32[]{:S(2)}) collective-permute-start(bf16[2,160,384]{2,1,0:T(8,128)(2,1)S(1)} %get-tuple-element.22), channel_id=1, source_target_pairs={{0,2},{2,4},{4,6},{6,0},{1,3},{3,5},{5,7},{7,1},{8,10},{10,12},{12... | collective-permute-start | bytes 737288 | tf_op jit(solution)/shard_map/ppermute | solution.py:315
  114.3 0.0 collective-permute-done.14
  114.3 0.2 fusion.11
  114.5 2.5 %collective-permute-start.15 = (bf16[2,160,384]{2,1,0:T(8,128)(2,1)S(1)}, bf16[2,160,384]{2,1,0:T(8,128)(2,1)S(1)}, u32[]{:S(2)}, u32[]{:S(2)}) collective-permute-start(bf16[2,160,384]{2,1,0:T(8,128)(2,1)S(1)} %get-tuple-element.23), channel_id=1, source_target_pairs={{0,6},{2,0},{4,2},{6,4},{1,7},{3,1},{5,3},{7,5},{8,14},{10,8},{12,... | collective-permute-start | bytes 737288 | tf_op jit(solution)/shard_map/ppermute | solution.py:315
  117.0 3.3 %collective-permute-start.16 = (bf16[2,160,384]{2,1,0:T(8,128)(2,1)S(1)}, bf16[2,160,384]{2,1,0:T(8,128)(2,1)S(1)}, u32[]{:S(2)}, u32[]{:S(2)}) collective-permute-start(bf16[2,160,384]{2,1,0:T(8,128)(2,1)S(1)} %get-tuple-element.25), channel_id=1, source_target_pairs={{0,2},{2,4},{4,6},{6,0},{1,3},{3,5},{5,7},{7,1},{8,10},{10,12},{12... | collective-permute-start | bytes 737288 | tf_op jit(solution)/shard_map/ppermute | solution.py:315
  120.4 0.0 collective-permute-done.10
  120.4 5.8 %collective-permute-start.17 = (bf16[2,160,384]{2,1,0:T(8,128)(2,1)S(1)}, bf16[2,160,384]{2,1,0:T(8,128)(2,1)S(1)}, u32[]{:S(2)}, u32[]{:S(2)}) collective-permute-start(bf16[2,160,384]{2,1,0:T(8,128)(2,1)S(1)} %get-tuple-element.24), channel_id=1, source_target_pairs={{0,4},{2,6},{4,0},{6,2},{1,5},{3,7},{5,1},{7,3},{8,12},{10,14},{12... | collective-permute-start | bytes 737288 | tf_op jit(solution)/shard_map/ppermute | solution.py:315
  126.2 0.0 collective-permute-done.8
  126.2 0.0 collective-permute-done.9
  126.2 0.2 fusion.5
  126.4 0.7 collective-permute-start.11
  127.1 3.6 %collective-permute-start.12 = (bf16[160,384]{1,0:T(8,128)(2,1)S(1)}, bf16[160,384]{1,0:T(8,128)(2,1)S(1)}, u32[]{:S(2)}, u32[]{:S(2)}) collective-permute-start(bf16[160,384]{1,0:T(8,128)(2,1)S(1)} %get-tuple-element.27), channel_id=1, source_target_pairs={{0,8},{8,0},{16,264},{24,256},{256,24},{264,16},{272,280},{280,272... | collective-permute-start | bytes 368648 | tf_op jit(solution)/shard_map/ppermute | solution.py:318
  130.7 0.0 collective-permute-done.15
  130.7 0.0 collective-permute-done.16
  130.7 1.4 collective-permute-done.17
  132.1 0.2 fusion.2
  132.3 5.8 %collective-permute-start.18 = (bf16[160,384]{1,0:T(8,128)(2,1)S(1)}, bf16[160,384]{1,0:T(8,128)(2,1)S(1)}, u32[]{:S(2)}, u32[]{:S(2)}) collective-permute-start(bf16[160,384]{1,0:T(8,128)(2,1)S(1)} %get-tuple-element.28), channel_id=1, source_target_pairs={{0,256},{8,264},{16,0},{24,8},{256,272},{264,280},{272,16},{280,24... | collective-permute-start | bytes 368648 | tf_op jit(solution)/shard_map/ppermute | solution.py:318
  138.0 3.9 %collective-permute-start.19 = (bf16[160,384]{1,0:T(8,128)(2,1)S(1)}, bf16[160,384]{1,0:T(8,128)(2,1)S(1)}, u32[]{:S(2)}, u32[]{:S(2)}) collective-permute-start(bf16[160,384]{1,0:T(8,128)(2,1)S(1)} %get-tuple-element.29), channel_id=1, source_target_pairs={{0,264},{8,256},{16,8},{24,0},{256,280},{264,272},{272,24},{280,16... | collective-permute-start | bytes 368648 | tf_op jit(solution)/shard_map/ppermute | solution.py:318
  141.9 0.0 collective-permute-done.11
  141.9 0.0 collective-permute-done.12
  141.9 1.3 collective-permute-done.18
  143.2 5.8 %collective-permute-done.19 = bf16[160,384]{1,0:T(8,128)(2,1)S(1)} collective-permute-done((bf16[160,384]{1,0:T(8,128)(2,1)S(1)}, bf16[160,384]{1,0:T(8,128)(2,1)S(1)}, u32[]{:S(2)}, u32[]{:S(2)}) %collective-permute-start.19) | collective-permute-done | bytes 122912 | tf_op jit(solution)/shard_map/ppermute | solution.py:318
  149.0 0.1 add_convert_fusion.8
  149.1 0.7 fusion.14
  (5 shorter events, 0.1 us)
Async XLA Ops:
  7.2 69.2 %all-gather.5.cloned.1.call-start = ((), (), s32[]{:S(2)}) async-start(), calls=%async_computation | async-start | bytes 5308416 | tf_op jit(solution)/shard_map/all_gather | solution.py:287
  11.0 17.8 %collective-permute-start.2 = (bf16[168,384]{1,0:T(8,128)(2,1)S(1)}, bf16[168,384]{1,0:T(8,128)(2,1)S(1)}, u32[]{:S(2)}, u32[]{:S(2)}) collective-permute-start(bf16[168,384]{1,0:T(8,128)(2,1)S(1)} %pad_maximum_fusion.3), channel_id=1, source_target_pairs={{0,16},{8,24},{16,272},{24,280},{256,0},{264,8},{272,256},{280,264... | collective-permute-start | bytes 387080 | tf_op jit(solution)/shard_map/ppermute | solution.py:292
  21.9 9.5 %collective-permute-start.3 = (bf16[168,384]{1,0:T(8,128)(2,1)S(1)}, bf16[168,384]{1,0:T(8,128)(2,1)S(1)}, u32[]{:S(2)}, u32[]{:S(2)}) collective-permute-start(bf16[168,384]{1,0:T(8,128)(2,1)S(1)} %pad_maximum_fusion.3), channel_id=1, source_target_pairs={{0,24},{8,16},{16,280},{24,272},{256,8},{264,0},{272,264},{280,256... | collective-permute-start | bytes 387080 | tf_op jit(solution)/shard_map/ppermute | solution.py:292
  25.3 23.3 %collective-permute-start = (bf16[168,384]{1,0:T(8,128)(2,1)S(1)}, bf16[168,384]{1,0:T(8,128)(2,1)S(1)}, u32[]{:S(2)}, u32[]{:S(2)}) collective-permute-start(bf16[168,384]{1,0:T(8,128)(2,1)S(1)} %pad_maximum_fusion.3), channel_id=1, source_target_pairs={{0,0},{8,8},{16,256},{24,264},{256,16},{264,24},{272,272},{280,280... | collective-permute-start | bytes 387080 | tf_op jit(solution)/shard_map/ppermute | solution.py:292
  26.0 22.6 %collective-permute-start.1 = (bf16[168,384]{1,0:T(8,128)(2,1)S(1)}, bf16[168,384]{1,0:T(8,128)(2,1)S(1)}, u32[]{:S(2)}, u32[]{:S(2)}) collective-permute-start(bf16[168,384]{1,0:T(8,128)(2,1)S(1)} %pad_maximum_fusion.3), channel_id=1, source_target_pairs={{0,8},{8,0},{16,264},{24,256},{256,24},{264,16},{272,280},{280,272... | collective-permute-start | bytes 387080 | tf_op jit(solution)/shard_map/ppermute | solution.py:292
  46.7 19.3 %collective-permute-start.5 = (bf16[4,2,168,384]{3,2,1,0:T(8,128)(2,1)S(1)}, bf16[4,2,168,384]{3,2,1,0:T(8,128)(2,1)S(1)}, u32[]{:S(2)}, u32[]{:S(2)}) collective-permute-start(bf16[4,2,168,384]{3,2,1,0:T(8,128)(2,1)S(1)} %bitcast.44), channel_id=1, source_target_pairs={{0,1},{1,0},{2,3},{3,2},{4,5},{5,4},{6,7},{7,6},{8,9},{9,8},{10,11... | collective-permute-start | bytes 3096584 | tf_op jit(solution)/shard_map/ppermute | solution.py:297
  64.0 4.7 %collective-permute-start.4 = (bf16[4,2,168,384]{3,2,1,0:T(8,128)(2,1)S(1)}, bf16[4,2,168,384]{3,2,1,0:T(8,128)(2,1)}, u32[]{:S(2)}, u32[]{:S(2)}) collective-permute-start(bf16[4,2,168,384]{3,2,1,0:T(8,128)(2,1)S(1)} %bitcast.46), channel_id=1, source_target_pairs={{0,1},{1,0},{2,3},{3,2},{4,5},{5,4},{6,7},{7,6},{8,9},{9,8},{10,11... | collective-permute-start | bytes 3096584 | tf_op jit(solution)/shard_map/ppermute | solution.py:295
  76.4 9.3 %copy-start = (bf16[6144,384]{1,0:T(8,128)(2,1)S(1)}, bf16[6144,384]{1,0:T(8,128)(2,1)}, u32[]{:S(2)}) copy-start(bf16[6144,384]{1,0:T(8,128)(2,1)} %all-gather.5.cloned.1.call-done) | copy-start | bytes 14155780
  81.3 10.9 %copy-start.1 = (bf16[2,160,3072]{2,1,0:T(8,128)(2,1)S(1)}, bf16[2,160,3072]{2,1,0:T(8,128)(2,1)}, u32[]{:S(2)}) copy-start(bf16[2,160,3072]{2,1,0:T(8,128)(2,1)} %get-tuple-element.15.x_ref) | copy-start | bytes 5898244
  81.3 10.9 %collective-permute-start.6 = (bf16[336,384]{1,0:T(8,128)(2,1)S(1)}, bf16[336,384]{1,0:T(8,128)(2,1)S(1)}, u32[]{:S(2)}, u32[]{:S(2)}) collective-permute-start(bf16[336,384]{1,0:T(8,128)(2,1)S(1)} %first.2.own_ref), channel_id=1, source_target_pairs={{0,256},{256,0},{1,257},{257,1},{2,258},{258,2},{3,259},{259,3},{4... | collective-permute-start | bytes 774152 | tf_op jit(solution)/shard_map/ppermute | solution.py:301
  89.7 9.9 %collective-permute-start.13 = (bf16[336,384]{1,0:T(8,128)(2,1)S(1)}, bf16[336,384]{1,0:T(8,128)(2,1)S(1)}, u32[]{:S(2)}, u32[]{:S(2)}) collective-permute-start(bf16[336,384]{1,0:T(8,128)(2,1)S(1)} %first.3.own_ref), channel_id=1, source_target_pairs={{0,256},{256,0},{1,257},{257,1},{2,258},{258,2},{3,259},{259,3},{4... | collective-permute-start | bytes 774152 | tf_op jit(solution)/shard_map/ppermute | solution.py:301
  95.0 9.3 %collective-permute-start.7 = (bf16[4,2,160,384]{3,2,1,0:T(8,128)(2,1)S(1)}, bf16[4,2,160,384]{3,2,1,0:T(8,128)(2,1)S(1)}, u32[]{:S(2)}, u32[]{:S(2)}) collective-permute-start(bf16[4,2,160,384]{3,2,1,0:T(8,128)(2,1)S(1)} %get-tuple-element.17), channel_id=1, source_target_pairs={{0,1},{1,0},{2,3},{3,2},{4,5},{5,4},{6,7},{7,6},{8,9},{9,8},{10,11... | collective-permute-start | bytes 2949128 | tf_op jit(solution)/shard_map/ppermute | solution.py:306
  102.3 12.0 %collective-permute-start.14 = (bf16[4,2,160,384]{3,2,1,0:T(8,128)(2,1)S(1)}, bf16[4,2,160,384]{3,2,1,0:T(8,128)(2,1)S(1)}, u32[]{:S(2)}, u32[]{:S(2)}) collective-permute-start(bf16[4,2,160,384]{3,2,1,0:T(8,128)(2,1)S(1)} %get-tuple-element.19), channel_id=1, source_target_pairs={{0,1},{1,0},{2,3},{3,2},{4,5},{5,4},{6,7},{7,6},{8,9},{9,8},{10,11... | collective-permute-start | bytes 2949128 | tf_op jit(solution)/shard_map/ppermute | solution.py:306
  104.5 15.9 %collective-permute-start.10 = (bf16[2,160,384]{2,1,0:T(8,128)(2,1)S(1)}, bf16[2,160,384]{2,1,0:T(8,128)(2,1)S(1)}, u32[]{:S(2)}, u32[]{:S(2)}) collective-permute-start(bf16[2,160,384]{2,1,0:T(8,128)(2,1)S(1)} %get-tuple-element.21), channel_id=1, source_target_pairs={{0,4},{2,6},{4,0},{6,2},{1,5},{3,7},{5,1},{7,3},{8,12},{10,14},{12... | collective-permute-start | bytes 737288 | tf_op jit(solution)/shard_map/ppermute | solution.py:315
  108.5 17.7 %collective-permute-start.8 = (bf16[2,160,384]{2,1,0:T(8,128)(2,1)S(1)}, bf16[2,160,384]{2,1,0:T(8,128)(2,1)S(1)}, u32[]{:S(2)}, u32[]{:S(2)}) collective-permute-start(bf16[2,160,384]{2,1,0:T(8,128)(2,1)S(1)} %get-tuple-element.20), channel_id=1, source_target_pairs={{0,6},{2,0},{4,2},{6,4},{1,7},{3,1},{5,3},{7,5},{8,14},{10,8},{12,... | collective-permute-start | bytes 737288 | tf_op jit(solution)/shard_map/ppermute | solution.py:315
  110.8 15.4 %collective-permute-start.9 = (bf16[2,160,384]{2,1,0:T(8,128)(2,1)S(1)}, bf16[2,160,384]{2,1,0:T(8,128)(2,1)S(1)}, u32[]{:S(2)}, u32[]{:S(2)}) collective-permute-start(bf16[2,160,384]{2,1,0:T(8,128)(2,1)S(1)} %get-tuple-element.22), channel_id=1, source_target_pairs={{0,2},{2,4},{4,6},{6,0},{1,3},{3,5},{5,7},{7,1},{8,10},{10,12},{12... | collective-permute-start | bytes 737288 | tf_op jit(solution)/shard_map/ppermute | solution.py:315
  114.5 16.2 %collective-permute-start.15 = (bf16[2,160,384]{2,1,0:T(8,128)(2,1)S(1)}, bf16[2,160,384]{2,1,0:T(8,128)(2,1)S(1)}, u32[]{:S(2)}, u32[]{:S(2)}) collective-permute-start(bf16[2,160,384]{2,1,0:T(8,128)(2,1)S(1)} %get-tuple-element.23), channel_id=1, source_target_pairs={{0,6},{2,0},{4,2},{6,4},{1,7},{3,1},{5,3},{7,5},{8,14},{10,8},{12,... | collective-permute-start | bytes 737288 | tf_op jit(solution)/shard_map/ppermute | solution.py:315
  117.0 13.7 %collective-permute-start.16 = (bf16[2,160,384]{2,1,0:T(8,128)(2,1)S(1)}, bf16[2,160,384]{2,1,0:T(8,128)(2,1)S(1)}, u32[]{:S(2)}, u32[]{:S(2)}) collective-permute-start(bf16[2,160,384]{2,1,0:T(8,128)(2,1)S(1)} %get-tuple-element.25), channel_id=1, source_target_pairs={{0,2},{2,4},{4,6},{6,0},{1,3},{3,5},{5,7},{7,1},{8,10},{10,12},{12... | collective-permute-start | bytes 737288 | tf_op jit(solution)/shard_map/ppermute | solution.py:315
  120.4 11.7 %collective-permute-start.17 = (bf16[2,160,384]{2,1,0:T(8,128)(2,1)S(1)}, bf16[2,160,384]{2,1,0:T(8,128)(2,1)S(1)}, u32[]{:S(2)}, u32[]{:S(2)}) collective-permute-start(bf16[2,160,384]{2,1,0:T(8,128)(2,1)S(1)} %get-tuple-element.24), channel_id=1, source_target_pairs={{0,4},{2,6},{4,0},{6,2},{1,5},{3,7},{5,1},{7,3},{8,12},{10,14},{12... | collective-permute-start | bytes 737288 | tf_op jit(solution)/shard_map/ppermute | solution.py:315
  126.4 15.5 %collective-permute-start.11 = (bf16[160,384]{1,0:T(8,128)(2,1)S(1)}, bf16[160,384]{1,0:T(8,128)(2,1)S(1)}, u32[]{:S(2)}, u32[]{:S(2)}) collective-permute-start(bf16[160,384]{1,0:T(8,128)(2,1)S(1)} %get-tuple-element.26), channel_id=1, source_target_pairs={{0,0},{8,8},{16,256},{24,264},{256,16},{264,24},{272,272},{280,280... | collective-permute-start | bytes 368648 | tf_op jit(solution)/shard_map/ppermute | solution.py:318
  127.1 14.8 %collective-permute-start.12 = (bf16[160,384]{1,0:T(8,128)(2,1)S(1)}, bf16[160,384]{1,0:T(8,128)(2,1)S(1)}, u32[]{:S(2)}, u32[]{:S(2)}) collective-permute-start(bf16[160,384]{1,0:T(8,128)(2,1)S(1)} %get-tuple-element.27), channel_id=1, source_target_pairs={{0,8},{8,0},{16,264},{24,256},{256,24},{264,16},{272,280},{280,272... | collective-permute-start | bytes 368648 | tf_op jit(solution)/shard_map/ppermute | solution.py:318
  132.3 10.9 %collective-permute-start.18 = (bf16[160,384]{1,0:T(8,128)(2,1)S(1)}, bf16[160,384]{1,0:T(8,128)(2,1)S(1)}, u32[]{:S(2)}, u32[]{:S(2)}) collective-permute-start(bf16[160,384]{1,0:T(8,128)(2,1)S(1)} %get-tuple-element.28), channel_id=1, source_target_pairs={{0,256},{8,264},{16,0},{24,8},{256,272},{264,280},{272,16},{280,24... | collective-permute-start | bytes 368648 | tf_op jit(solution)/shard_map/ppermute | solution.py:318
  138.0 11.0 %collective-permute-start.19 = (bf16[160,384]{1,0:T(8,128)(2,1)S(1)}, bf16[160,384]{1,0:T(8,128)(2,1)S(1)}, u32[]{:S(2)}, u32[]{:S(2)}) collective-permute-start(bf16[160,384]{1,0:T(8,128)(2,1)S(1)} %get-tuple-element.29), channel_id=1, source_target_pairs={{0,264},{8,256},{16,8},{24,0},{256,280},{264,272},{272,24},{280,16... | collective-permute-start | bytes 368648 | tf_op jit(solution)/shard_map/ppermute | solution.py:318
Sparse Core Ops, SparseCore 0:
  10.1 66.2 all-gather.4

commit v8 on v7

--- a/solution.py
+++ b/solution.py
@@ -315,7 +315,7 @@
             lax.ppermute(parts[d], "x", [(x, (x + d) % 4) for x in range(4)]) for d in (3, 1, 2)
         ]
         part = sum(part.astype(wide) for part in parts).astype(narrow)
-        shares += [lax.ppermute(part[j], ("l", "h"), scatter_pairs(i, j)).astype(wide) for j in range(2)]
+        shares += [lax.ppermute(part[j], ("l", "h"), scatter_pairs(i, j)).astype(wide) for j in (1, 0)]
     total = (shares[0] + shares[1] + shares[2] + shares[3]).astype(narrow)
     return (total[:, :piece], total[:, piece:])
 

time: 157 us -> 158 us (level)
  the two profiles are of different devices: /device:TPU:26 before, /device:TPU:24 now
where the time goes in v8:
time: 158 us; the launch traced here: 157 us
  starting transfers between devices  64.2 us (41%)
  blocking collectives  30.3 us (19%)
  waiting for transfers between devices  22.6 us (14%)
  Pallas kernels  20.2 us (13%)
  between operations  14.4 us (9%)
  other arithmetic  4.69 us (3%)
    ppermute x6, starting transfers between devices, on_device(): lax.ppermute(parts[d], 'x', [(x, (x + d) % 4) for x in range(4)])  20.5 us
    ppermute x4, starting transfers between devices, on_device(): lax.ppermute(pack, ('l', 'h'), gather_pairs(i, j))  17.8 us
    all_gather x1, blocking collectives, on_device(): own0 = lax.all_gather(jnp.stack(near[0]), 'x', axis=0)  15.9 us
    all_gather x1, blocking collectives, on_device(): own1 = lax.all_gather(jnp.stack(near[1]), 'x', axis=0)  14.4 us
    ppermute x4, starting transfers between devices, on_device(): lax.ppermute(part[j], ('l', 'h'), scatter_pairs(i, j)).astype(wide)  12.1 us
    pallas_call x2, Pallas kernels, first_call(): call(functools.partial(first_kernel, part), ['scalar', 'here', 'here', 'a...  8.84 us
    ppermute x4, waiting for transfers between devices, on_device(): lax.ppermute(part[j], ('l', 'h'), scatter_pairs(i, j)).astype(wide)  6.24 us
    ppermute x2, starting transfers between devices, on_device(): far_sums = [lax.ppermute(part, 'l', other_core) for part in sums]  6.1 us
  transfers between devices with their start and end apart: 21, of which 8 were waited for; matrix products, arithmetic and copies ran while one was open for 2% of the time, Pallas kernels for 10%

profile of v8, /device:TPU:24, one launch (start us, length us, event | category | flops | bytes accessed | tf_op | source)
XLA Modules:
  0.0 157.3 jit_solution(1781956729363957217)
XLA Ops:
  7.2 0.0 all-gather.5.cloned.1.call-start
  7.2 1.9 %pad_maximum_fusion = bf16[768,384]{1,0:T(8,128)(2,1)} fusion(bf16[384,384]{1,0:T(8,128)(2,1)} %param.8, bf16[384,384]{1,0:T(8,128)(2,1)} %param.7), kind=kLoop, calls=%fused_computation | loop fusion | flops 1179648 | bytes 1179648 | tf_op jit(solution)/shard_map/concatenate | solution.py:287
  9.1 0.0 all-gather.5.cloned.1.call-update
  9.2 0.8 pad_maximum_fusion.4
  10.0 1.0 pad_maximum_fusion.3
  11.0 10.9 %collective-permute-start.2 = (bf16[168,384]{1,0:T(8,128)(2,1)S(1)}, bf16[168,384]{1,0:T(8,128)(2,1)S(1)}, u32[]{:S(2)}, u32[]{:S(2)}) collective-permute-start(bf16[168,384]{1,0:T(8,128)(2,1)S(1)} %pad_maximum_fusion.3), channel_id=1, source_target_pairs={{0,16},{8,24},{16,272},{24,280},{256,0},{264,8},{272,256},{280,264... | collective-permute-start | bytes 387080 | tf_op jit(solution)/shard_map/ppermute | solution.py:292
  21.9 3.4 %collective-permute-start.3 = (bf16[168,384]{1,0:T(8,128)(2,1)S(1)}, bf16[168,384]{1,0:T(8,128)(2,1)S(1)}, u32[]{:S(2)}, u32[]{:S(2)}) collective-permute-start(bf16[168,384]{1,0:T(8,128)(2,1)S(1)} %pad_maximum_fusion.3), channel_id=1, source_target_pairs={{0,24},{8,16},{16,280},{24,272},{256,8},{264,0},{272,264},{280,256... | collective-permute-start | bytes 387080 | tf_op jit(solution)/shard_map/ppermute | solution.py:292
  25.3 0.7 collective-permute-start
  26.0 2.8 %collective-permute-start.1 = (bf16[168,384]{1,0:T(8,128)(2,1)S(1)}, bf16[168,384]{1,0:T(8,128)(2,1)S(1)}, u32[]{:S(2)}, u32[]{:S(2)}) collective-permute-start(bf16[168,384]{1,0:T(8,128)(2,1)S(1)} %pad_maximum_fusion.3), channel_id=1, source_target_pairs={{0,8},{8,0},{16,264},{24,256},{256,24},{264,16},{272,280},{280,272... | collective-permute-start | bytes 387080 | tf_op jit(solution)/shard_map/ppermute | solution.py:292
  28.8 0.0 collective-permute-done.2
  28.8 2.6 %collective-permute-done.3 = bf16[168,384]{1,0:T(8,128)(2,1)S(1)} collective-permute-done((bf16[168,384]{1,0:T(8,128)(2,1)S(1)}, bf16[168,384]{1,0:T(8,128)(2,1)S(1)}, u32[]{:S(2)}, u32[]{:S(2)}) %collective-permute-start.3) | collective-permute-done | bytes 129056 | tf_op jit(solution)/shard_map/ppermute | solution.py:292
  31.5 14.4 %all-gather.1 = bf16[8,168,384]{2,1,0:T(8,128)(2,1)S(1)} all-gather(bf16[2,168,384]{2,1,0:T(8,128)(2,1)S(1)} %pad_maximum_fusion.2), channel_id=3, replica_groups=mesh['l'=2,'y'=8,'h'=4,'x'=4,'k'=2] {'x'}, dimensions={0}, use_global_device_ids=true | all-gather | bytes 1290240 | tf_op jit(solution)/shard_map/all_gather | solution.py:296
  45.9 1.9 %collective-permute-start.5 = (bf16[4,2,168,384]{3,2,1,0:T(8,128)(2,1)S(1)}, bf16[4,2,168,384]{3,2,1,0:T(8,128)(2,1)S(1)}, u32[]{:S(2)}, u32[]{:S(2)}) collective-permute-start(bf16[4,2,168,384]{3,2,1,0:T(8,128)(2,1)S(1)} %bitcast.44), channel_id=1, source_target_pairs={{0,1},{1,0},{2,3},{3,2},{4,5},{5,4},{6,7},{7,6},{8,9},{9,8},{10,11... | collective-permute-start | bytes 3096584 | tf_op jit(solution)/shard_map/ppermute | solution.py:297
  47.8 0.0 collective-permute-done
  47.8 0.0 collective-permute-done.1
  47.9 15.9 %all-gather = bf16[8,168,384]{2,1,0:T(8,128)(2,1)S(1)} all-gather(bf16[2,168,384]{2,1,0:T(8,128)(2,1)S(1)} %pad_maximum_fusion.1), channel_id=2, replica_groups=mesh['l'=2,'y'=8,'h'=4,'x'=4,'k'=2] {'x'}, dimensions={0}, use_global_device_ids=true | all-gather | bytes 1290240 | tf_op jit(solution)/shard_map/all_gather | solution.py:294
  63.8 1.9 %collective-permute-start.4 = (bf16[4,2,168,384]{3,2,1,0:T(8,128)(2,1)S(1)}, bf16[4,2,168,384]{3,2,1,0:T(8,128)(2,1)}, u32[]{:S(2)}, u32[]{:S(2)}) collective-permute-start(bf16[4,2,168,384]{3,2,1,0:T(8,128)(2,1)S(1)} %bitcast.46), channel_id=1, source_target_pairs={{0,1},{1,0},{2,3},{3,2},{4,5},{5,4},{6,7},{7,6},{8,9},{9,8},{10,11... | collective-permute-start | bytes 3096584 | tf_op jit(solution)/shard_map/ppermute | solution.py:295
  65.7 0.1 pad_add_fusion.place_ref
  65.8 0.0 collective-permute-done.5.far1
  65.8 2.6 %collective-permute-done.4.far0 = bf16[4,2,168,384]{3,2,1,0:T(8,128)(2,1)} collective-permute-done((bf16[4,2,168,384]{3,2,1,0:T(8,128)(2,1)S(1)}, bf16[4,2,168,384]{3,2,1,0:T(8,128)(2,1)}, u32[]{:S(2)}, u32[]{:S(2)}) %collective-permute-start.4) | collective-permute-done | bytes 1032224 | tf_op jit(solution)/shard_map/ppermute | solution.py:295
  68.5 5.8 %merge.1 = (bf16[2,160,3072]{2,1,0:T(8,128)(2,1)}, bf16[2,4,160,768]{3,2,1,0:T(8,128)(2,1)}, bf16[2,4,160,768]{3,2,1,0:T(8,128)(2,1)}, f32[8,3072]{1,0:T(8,128)S(1)}, bf16[2,384,128]{2,1,0:T(8,128)(2,1)S(1)}) custom-call(s32[3]{0:T(128)S(1)} %pad_add_fusion.place_ref, bf16[4,2,168,384]{3,2,1,0:T(8,128)(2,1)S(1)} %bitcast.47, ...), custom_call_target="tpu_custom_call" | custom-call | tf_op jit(solution)/shard_map/merge/pallas_call | solution.py:232
  74.3 2.1 %all-gather.5.cloned.1.call-done = bf16[6144,384]{1,0:T(8,128)(2,1)} async-done(((bf16[768,384]{1,0:T(8,128)(2,1)}), bf16[6144,384]{1,0:T(8,128)(2,1)}) %all-gather.5.cloned.1.call-update) | async-done | bytes 4718608 | tf_op jit(solution)/shard_map/all_gather | solution.py:287
  76.4 0.0 copy-start
  76.4 4.9 %first.2.own_ref = bf16[336,384]{1,0:T(8,128)(2,1)S(1)} custom-call(s32[3]{0:T(128)S(1)} %pad_add_fusion.place_ref, f32[8,3072]{1,0:T(8,128)S(1)} %get-tuple-element.11.gain_ref, bf16[2,384,128]{2,1,0:T(8,128)(2,1)S(1)} %get-tuple-element.12.table_ref, bf16[2,4,160,768]{3,2,1,0:T(8,128)(2,1)} %get-tuple-element.13.shift_ref, ...), custom_call_target="tpu_custom_call" | custom-call | tf_op jit(solution)/shard_map/first/pallas_call | solution.py:252
  81.3 0.0 copy-start.1
  81.3 4.2 %collective-permute-start.6 = (bf16[336,384]{1,0:T(8,128)(2,1)S(1)}, bf16[336,384]{1,0:T(8,128)(2,1)S(1)}, u32[]{:S(2)}, u32[]{:S(2)}) collective-permute-start(bf16[336,384]{1,0:T(8,128)(2,1)S(1)} %first.2.own_ref), channel_id=1, source_target_pairs={{0,256},{256,0},{1,257},{257,1},{2,258},{258,2},{3,259},{259,3},{4... | collective-permute-start | bytes 774152 | tf_op jit(solution)/shard_map/ppermute | solution.py:301
  85.5 0.0 copy-done
  85.5 4.0 %first.3.own_ref = bf16[336,384]{1,0:T(8,128)(2,1)S(1)} custom-call(s32[3]{0:T(128)S(1)} %pad_add_fusion.place_ref, f32[8,3072]{1,0:T(8,128)S(1)} %get-tuple-element.11.gain_ref, bf16[2,384,128]{2,1,0:T(8,128)(2,1)S(1)} %get-tuple-element.12.table_ref, bf16[2,4,160,768]{3,2,1,0:T(8,128)(2,1)} %get-tuple-element.13.shift_ref, ...), custom_call_target="tpu_custom_call" | custom-call | tf_op jit(solution)/shard_map/first/pallas_call | solution.py:252
  89.4 1.9 %collective-permute-start.13 = (bf16[336,384]{1,0:T(8,128)(2,1)S(1)}, bf16[336,384]{1,0:T(8,128)(2,1)S(1)}, u32[]{:S(2)}, u32[]{:S(2)}) collective-permute-start(bf16[336,384]{1,0:T(8,128)(2,1)S(1)} %first.3.own_ref), channel_id=1, source_target_pairs={{0,256},{256,0},{1,257},{257,1},{2,258},{258,2},{3,259},{259,3},{4... | collective-permute-start | bytes 774152 | tf_op jit(solution)/shard_map/ppermute | solution.py:301
  91.4 0.6 collective-permute-done.6.far_ref
  92.0 0.0 copy-done.1
  92.0 2.8 %second.2 = (bf16[4,2,160,384]{3,2,1,0:T(8,128)(2,1)S(1)}, bf16[4,2,160,384]{3,2,1,0:T(8,128)(2,1)S(1)}) custom-call(s32[3]{0:T(128)S(1)} %pad_add_fusion.place_ref, bf16[336,384]{1,0:T(8,128)(2,1)S(1)} %first.2.own_ref, bf16[336,384]{1,0:T(8,128)(2,1)S(1)} %collective-permute-done.6.far_ref, bf16[2,160,3072]{2,1,0:T(8,128)(2,1)S(1)} %copy-done.1, ...), custom_call_target="tpu_custom_call" | custom-call | tf_op jit(solution)/shard_map/second/pallas_call | solution.py:270
  94.8 1.9 %collective-permute-start.7 = (bf16[4,2,160,384]{3,2,1,0:T(8,128)(2,1)S(1)}, bf16[4,2,160,384]{3,2,1,0:T(8,128)(2,1)S(1)}, u32[]{:S(2)}, u32[]{:S(2)}) collective-permute-start(bf16[4,2,160,384]{3,2,1,0:T(8,128)(2,1)S(1)} %get-tuple-element.17), channel_id=1, source_target_pairs={{0,1},{1,0},{2,3},{3,2},{4,5},{5,4},{6,7},{7,6},{8,9},{9,8},{10,11... | collective-permute-start | bytes 2949128 | tf_op jit(solution)/shard_map/ppermute | solution.py:306
  96.7 2.6 %collective-permute-done.13.far_ref = bf16[336,384]{1,0:T(8,128)(2,1)S(1)} collective-permute-done((bf16[336,384]{1,0:T(8,128)(2,1)S(1)}, bf16[336,384]{1,0:T(8,128)(2,1)S(1)}, u32[]{:S(2)}, u32[]{:S(2)}) %collective-permute-start.13) | collective-permute-done | bytes 258080 | tf_op jit(solution)/shard_map/ppermute | solution.py:301
  99.3 2.8 %second.3 = (bf16[4,2,160,384]{3,2,1,0:T(8,128)(2,1)S(1)}, bf16[4,2,160,384]{3,2,1,0:T(8,128)(2,1)S(1)}) custom-call(s32[3]{0:T(128)S(1)} %pad_add_fusion.place_ref, bf16[336,384]{1,0:T(8,128)(2,1)S(1)} %first.3.own_ref, bf16[336,384]{1,0:T(8,128)(2,1)S(1)} %collective-permute-done.13.far_ref, bf16[2,160,3072]{2,1,0:T(8,128)(2,1)S(1)} %copy-done.1, ...), custom_call_target="tpu_custom_call" | custom-call | tf_op jit(solution)/shard_map/second/pallas_call | solution.py:270
  102.1 1.9 %collective-permute-start.14 = (bf16[4,2,160,384]{3,2,1,0:T(8,128)(2,1)S(1)}, bf16[4,2,160,384]{3,2,1,0:T(8,128)(2,1)S(1)}, u32[]{:S(2)}, u32[]{:S(2)}) collective-permute-start(bf16[4,2,160,384]{3,2,1,0:T(8,128)(2,1)S(1)} %get-tuple-element.19), channel_id=1, source_target_pairs={{0,1},{1,0},{2,3},{3,2},{4,5},{5,4},{6,7},{7,6},{8,9},{9,8},{10,11... | collective-permute-start | bytes 2949128 | tf_op jit(solution)/shard_map/ppermute | solution.py:306
  104.0 0.0 collective-permute-done.7
  104.0 0.2 fusion.7
  104.2 4.1 %collective-permute-start.10 = (bf16[2,160,384]{2,1,0:T(8,128)(2,1)S(1)}, bf16[2,160,384]{2,1,0:T(8,128)(2,1)S(1)}, u32[]{:S(2)}, u32[]{:S(2)}) collective-permute-start(bf16[2,160,384]{2,1,0:T(8,128)(2,1)S(1)} %get-tuple-element.21), channel_id=1, source_target_pairs={{0,4},{2,6},{4,0},{6,2},{1,5},{3,7},{5,1},{7,3},{8,12},{10,14},{12... | collective-permute-start | bytes 737288 | tf_op jit(solution)/shard_map/ppermute | solution.py:315
  108.3 4.1 %collective-permute-start.8 = (bf16[2,160,384]{2,1,0:T(8,128)(2,1)S(1)}, bf16[2,160,384]{2,1,0:T(8,128)(2,1)S(1)}, u32[]{:S(2)}, u32[]{:S(2)}) collective-permute-start(bf16[2,160,384]{2,1,0:T(8,128)(2,1)S(1)} %get-tuple-element.20), channel_id=1, source_target_pairs={{0,6},{2,0},{4,2},{6,4},{1,7},{3,1},{5,3},{7,5},{8,14},{10,8},{12,... | collective-permute-start | bytes 737288 | tf_op jit(solution)/shard_map/ppermute | solution.py:315
  112.5 1.9 %collective-permute-start.9 = (bf16[2,160,384]{2,1,0:T(8,128)(2,1)S(1)}, bf16[2,160,384]{2,1,0:T(8,128)(2,1)S(1)}, u32[]{:S(2)}, u32[]{:S(2)}) collective-permute-start(bf16[2,160,384]{2,1,0:T(8,128)(2,1)S(1)} %get-tuple-element.22), channel_id=1, source_target_pairs={{0,2},{2,4},{4,6},{6,0},{1,3},{3,5},{5,7},{7,1},{8,10},{10,12},{12... | collective-permute-start | bytes 737288 | tf_op jit(solution)/shard_map/ppermute | solution.py:315
  114.4 0.0 collective-permute-done.14
  114.4 0.2 fusion.11
  114.6 5.1 %collective-permute-start.15 = (bf16[2,160,384]{2,1,0:T(8,128)(2,1)S(1)}, bf16[2,160,384]{2,1,0:T(8,128)(2,1)S(1)}, u32[]{:S(2)}, u32[]{:S(2)}) collective-permute-start(bf16[2,160,384]{2,1,0:T(8,128)(2,1)S(1)} %get-tuple-element.23), channel_id=1, source_target_pairs={{0,6},{2,0},{4,2},{6,4},{1,7},{3,1},{5,3},{7,5},{8,14},{10,8},{12,... | collective-permute-start | bytes 737288 | tf_op jit(solution)/shard_map/ppermute | solution.py:315
  119.7 1.9 %collective-permute-start.16 = (bf16[2,160,384]{2,1,0:T(8,128)(2,1)S(1)}, bf16[2,160,384]{2,1,0:T(8,128)(2,1)S(1)}, u32[]{:S(2)}, u32[]{:S(2)}) collective-permute-start(bf16[2,160,384]{2,1,0:T(8,128)(2,1)S(1)} %get-tuple-element.25), channel_id=1, source_target_pairs={{0,2},{2,4},{4,6},{6,0},{1,3},{3,5},{5,7},{7,1},{8,10},{10,12},{12... | collective-permute-start | bytes 737288 | tf_op jit(solution)/shard_map/ppermute | solution.py:315
  121.7 0.0 collective-permute-done.10
  121.7 3.4 %collective-permute-start.17 = (bf16[2,160,384]{2,1,0:T(8,128)(2,1)S(1)}, bf16[2,160,384]{2,1,0:T(8,128)(2,1)S(1)}, u32[]{:S(2)}, u32[]{:S(2)}) collective-permute-start(bf16[2,160,384]{2,1,0:T(8,128)(2,1)S(1)} %get-tuple-element.24), channel_id=1, source_target_pairs={{0,4},{2,6},{4,0},{6,2},{1,5},{3,7},{5,1},{7,3},{8,12},{10,14},{12... | collective-permute-start | bytes 737288 | tf_op jit(solution)/shard_map/ppermute | solution.py:315
  125.1 0.0 collective-permute-done.8
  125.1 0.0 collective-permute-done.9
  125.1 0.2 fusion.5
  125.3 3.6 %collective-permute-start.11 = (bf16[160,384]{1,0:T(8,128)(2,1)S(1)}, bf16[160,384]{1,0:T(8,128)(2,1)S(1)}, u32[]{:S(2)}, u32[]{:S(2)}) collective-permute-start(bf16[160,384]{1,0:T(8,128)(2,1)S(1)} %get-tuple-element.26), channel_id=1, source_target_pairs={{0,8},{8,0},{16,264},{24,256},{256,24},{264,16},{272,280},{280,272... | collective-permute-start | bytes 368648 | tf_op jit(solution)/shard_map/ppermute | solution.py:318
  128.9 0.7 collective-permute-start.12
  129.6 0.0 collective-permute-done.15
  129.6 5.8 %collective-permute-done.16 = bf16[2,160,384]{2,1,0:T(8,128)(2,1)S(1)} collective-permute-done((bf16[2,160,384]{2,1,0:T(8,128)(2,1)S(1)}, bf16[2,160,384]{2,1,0:T(8,128)(2,1)S(1)}, u32[]{:S(2)}, u32[]{:S(2)}) %collective-permute-start.16) | collective-permute-done | bytes 245792 | tf_op jit(solution)/shard_map/ppermute | solution.py:315
  135.3 0.0 collective-permute-done.17
  135.3 0.2 fusion.2
  135.5 3.4 %collective-permute-start.18 = (bf16[160,384]{1,0:T(8,128)(2,1)S(1)}, bf16[160,384]{1,0:T(8,128)(2,1)S(1)}, u32[]{:S(2)}, u32[]{:S(2)}) collective-permute-start(bf16[160,384]{1,0:T(8,128)(2,1)S(1)} %get-tuple-element.28), channel_id=1, source_target_pairs={{0,264},{8,256},{16,8},{24,0},{256,280},{264,272},{272,24},{280,16... | collective-permute-start | bytes 368648 | tf_op jit(solution)/shard_map/ppermute | solution.py:318
  139.0 4.4 %collective-permute-start.19 = (bf16[160,384]{1,0:T(8,128)(2,1)S(1)}, bf16[160,384]{1,0:T(8,128)(2,1)S(1)}, u32[]{:S(2)}, u32[]{:S(2)}) collective-permute-start(bf16[160,384]{1,0:T(8,128)(2,1)S(1)} %get-tuple-element.29), channel_id=1, source_target_pairs={{0,256},{8,264},{16,0},{24,8},{256,272},{264,280},{272,16},{280,24... | collective-permute-start | bytes 368648 | tf_op jit(solution)/shard_map/ppermute | solution.py:318
  143.4 0.0 collective-permute-done.11
  143.4 0.0 collective-permute-done.12
  143.4 3.0 %collective-permute-done.18 = bf16[160,384]{1,0:T(8,128)(2,1)S(1)} collective-permute-done((bf16[160,384]{1,0:T(8,128)(2,1)S(1)}, bf16[160,384]{1,0:T(8,128)(2,1)S(1)}, u32[]{:S(2)}, u32[]{:S(2)}) %collective-permute-start.18) | collective-permute-done | bytes 122912 | tf_op jit(solution)/shard_map/ppermute | solution.py:318
  146.5 3.2 %collective-permute-done.19 = bf16[160,384]{1,0:T(8,128)(2,1)S(1)} collective-permute-done((bf16[160,384]{1,0:T(8,128)(2,1)S(1)}, bf16[160,384]{1,0:T(8,128)(2,1)S(1)}, u32[]{:S(2)}, u32[]{:S(2)}) %collective-permute-start.19) | collective-permute-done | bytes 122912 | tf_op jit(solution)/shard_map/ppermute | solution.py:318
  149.7 0.1 add_convert_fusion.8
  149.7 0.7 fusion.14
  (5 shorter events, 0.1 us)
Async XLA Ops:
  7.2 69.2 %all-gather.5.cloned.1.call-start = ((), (), s32[]{:S(2)}) async-start(), calls=%async_computation | async-start | bytes 5308416 | tf_op jit(solution)/shard_map/all_gather | solution.py:287
  11.0 17.8 %collective-permute-start.2 = (bf16[168,384]{1,0:T(8,128)(2,1)S(1)}, bf16[168,384]{1,0:T(8,128)(2,1)S(1)}, u32[]{:S(2)}, u32[]{:S(2)}) collective-permute-start(bf16[168,384]{1,0:T(8,128)(2,1)S(1)} %pad_maximum_fusion.3), channel_id=1, source_target_pairs={{0,16},{8,24},{16,272},{24,280},{256,0},{264,8},{272,256},{280,264... | collective-permute-start | bytes 387080 | tf_op jit(solution)/shard_map/ppermute | solution.py:292
  21.9 9.5 %collective-permute-start.3 = (bf16[168,384]{1,0:T(8,128)(2,1)S(1)}, bf16[168,384]{1,0:T(8,128)(2,1)S(1)}, u32[]{:S(2)}, u32[]{:S(2)}) collective-permute-start(bf16[168,384]{1,0:T(8,128)(2,1)S(1)} %pad_maximum_fusion.3), channel_id=1, source_target_pairs={{0,24},{8,16},{16,280},{24,272},{256,8},{264,0},{272,264},{280,256... | collective-permute-start | bytes 387080 | tf_op jit(solution)/shard_map/ppermute | solution.py:292
  25.3 22.5 %collective-permute-start = (bf16[168,384]{1,0:T(8,128)(2,1)S(1)}, bf16[168,384]{1,0:T(8,128)(2,1)S(1)}, u32[]{:S(2)}, u32[]{:S(2)}) collective-permute-start(bf16[168,384]{1,0:T(8,128)(2,1)S(1)} %pad_maximum_fusion.3), channel_id=1, source_target_pairs={{0,0},{8,8},{16,256},{24,264},{256,16},{264,24},{272,272},{280,280... | collective-permute-start | bytes 387080 | tf_op jit(solution)/shard_map/ppermute | solution.py:292
  26.0 21.8 %collective-permute-start.1 = (bf16[168,384]{1,0:T(8,128)(2,1)S(1)}, bf16[168,384]{1,0:T(8,128)(2,1)S(1)}, u32[]{:S(2)}, u32[]{:S(2)}) collective-permute-start(bf16[168,384]{1,0:T(8,128)(2,1)S(1)} %pad_maximum_fusion.3), channel_id=1, source_target_pairs={{0,8},{8,0},{16,264},{24,256},{256,24},{264,16},{272,280},{280,272... | collective-permute-start | bytes 387080 | tf_op jit(solution)/shard_map/ppermute | solution.py:292
  45.9 19.9 %collective-permute-start.5 = (bf16[4,2,168,384]{3,2,1,0:T(8,128)(2,1)S(1)}, bf16[4,2,168,384]{3,2,1,0:T(8,128)(2,1)S(1)}, u32[]{:S(2)}, u32[]{:S(2)}) collective-permute-start(bf16[4,2,168,384]{3,2,1,0:T(8,128)(2,1)S(1)} %bitcast.44), channel_id=1, source_target_pairs={{0,1},{1,0},{2,3},{3,2},{4,5},{5,4},{6,7},{7,6},{8,9},{9,8},{10,11... | collective-permute-start | bytes 3096584 | tf_op jit(solution)/shard_map/ppermute | solution.py:297
  63.8 4.7 %collective-permute-start.4 = (bf16[4,2,168,384]{3,2,1,0:T(8,128)(2,1)S(1)}, bf16[4,2,168,384]{3,2,1,0:T(8,128)(2,1)}, u32[]{:S(2)}, u32[]{:S(2)}) collective-permute-start(bf16[4,2,168,384]{3,2,1,0:T(8,128)(2,1)S(1)} %bitcast.46), channel_id=1, source_target_pairs={{0,1},{1,0},{2,3},{3,2},{4,5},{5,4},{6,7},{7,6},{8,9},{9,8},{10,11... | collective-permute-start | bytes 3096584 | tf_op jit(solution)/shard_map/ppermute | solution.py:295
  76.4 9.1 %copy-start = (bf16[6144,384]{1,0:T(8,128)(2,1)S(1)}, bf16[6144,384]{1,0:T(8,128)(2,1)}, u32[]{:S(2)}) copy-start(bf16[6144,384]{1,0:T(8,128)(2,1)} %all-gather.5.cloned.1.call-done) | copy-start | bytes 14155780
  81.3 10.7 %copy-start.1 = (bf16[2,160,3072]{2,1,0:T(8,128)(2,1)S(1)}, bf16[2,160,3072]{2,1,0:T(8,128)(2,1)}, u32[]{:S(2)}) copy-start(bf16[2,160,3072]{2,1,0:T(8,128)(2,1)} %get-tuple-element.15.x_ref) | copy-start | bytes 5898244
  81.3 10.7 %collective-permute-start.6 = (bf16[336,384]{1,0:T(8,128)(2,1)S(1)}, bf16[336,384]{1,0:T(8,128)(2,1)S(1)}, u32[]{:S(2)}, u32[]{:S(2)}) collective-permute-start(bf16[336,384]{1,0:T(8,128)(2,1)S(1)} %first.2.own_ref), channel_id=1, source_target_pairs={{0,256},{256,0},{1,257},{257,1},{2,258},{258,2},{3,259},{259,3},{4... | collective-permute-start | bytes 774152 | tf_op jit(solution)/shard_map/ppermute | solution.py:301
  89.4 9.9 %collective-permute-start.13 = (bf16[336,384]{1,0:T(8,128)(2,1)S(1)}, bf16[336,384]{1,0:T(8,128)(2,1)S(1)}, u32[]{:S(2)}, u32[]{:S(2)}) collective-permute-start(bf16[336,384]{1,0:T(8,128)(2,1)S(1)} %first.3.own_ref), channel_id=1, source_target_pairs={{0,256},{256,0},{1,257},{257,1},{2,258},{258,2},{3,259},{259,3},{4... | collective-permute-start | bytes 774152 | tf_op jit(solution)/shard_map/ppermute | solution.py:301
  94.8 9.3 %collective-permute-start.7 = (bf16[4,2,160,384]{3,2,1,0:T(8,128)(2,1)S(1)}, bf16[4,2,160,384]{3,2,1,0:T(8,128)(2,1)S(1)}, u32[]{:S(2)}, u32[]{:S(2)}) collective-permute-start(bf16[4,2,160,384]{3,2,1,0:T(8,128)(2,1)S(1)} %get-tuple-element.17), channel_id=1, source_target_pairs={{0,1},{1,0},{2,3},{3,2},{4,5},{5,4},{6,7},{7,6},{8,9},{9,8},{10,11... | collective-permute-start | bytes 2949128 | tf_op jit(solution)/shard_map/ppermute | solution.py:306
  102.1 12.3 %collective-permute-start.14 = (bf16[4,2,160,384]{3,2,1,0:T(8,128)(2,1)S(1)}, bf16[4,2,160,384]{3,2,1,0:T(8,128)(2,1)S(1)}, u32[]{:S(2)}, u32[]{:S(2)}) collective-permute-start(bf16[4,2,160,384]{3,2,1,0:T(8,128)(2,1)S(1)} %get-tuple-element.19), channel_id=1, source_target_pairs={{0,1},{1,0},{2,3},{3,2},{4,5},{5,4},{6,7},{7,6},{8,9},{9,8},{10,11... | collective-permute-start | bytes 2949128 | tf_op jit(solution)/shard_map/ppermute | solution.py:306
  104.2 17.4 %collective-permute-start.10 = (bf16[2,160,384]{2,1,0:T(8,128)(2,1)S(1)}, bf16[2,160,384]{2,1,0:T(8,128)(2,1)S(1)}, u32[]{:S(2)}, u32[]{:S(2)}) collective-permute-start(bf16[2,160,384]{2,1,0:T(8,128)(2,1)S(1)} %get-tuple-element.21), channel_id=1, source_target_pairs={{0,4},{2,6},{4,0},{6,2},{1,5},{3,7},{5,1},{7,3},{8,12},{10,14},{12... | collective-permute-start | bytes 737288 | tf_op jit(solution)/shard_map/ppermute | solution.py:315
  108.3 16.7 %collective-permute-start.8 = (bf16[2,160,384]{2,1,0:T(8,128)(2,1)S(1)}, bf16[2,160,384]{2,1,0:T(8,128)(2,1)S(1)}, u32[]{:S(2)}, u32[]{:S(2)}) collective-permute-start(bf16[2,160,384]{2,1,0:T(8,128)(2,1)S(1)} %get-tuple-element.20), channel_id=1, source_target_pairs={{0,6},{2,0},{4,2},{6,4},{1,7},{3,1},{5,3},{7,5},{8,14},{10,8},{12,... | collective-permute-start | bytes 737288 | tf_op jit(solution)/shard_map/ppermute | solution.py:315
  112.5 12.6 %collective-permute-start.9 = (bf16[2,160,384]{2,1,0:T(8,128)(2,1)S(1)}, bf16[2,160,384]{2,1,0:T(8,128)(2,1)S(1)}, u32[]{:S(2)}, u32[]{:S(2)}) collective-permute-start(bf16[2,160,384]{2,1,0:T(8,128)(2,1)S(1)} %get-tuple-element.22), channel_id=1, source_target_pairs={{0,2},{2,4},{4,6},{6,0},{1,3},{3,5},{5,7},{7,1},{8,10},{10,12},{12... | collective-permute-start | bytes 737288 | tf_op jit(solution)/shard_map/ppermute | solution.py:315
  114.6 15.0 %collective-permute-start.15 = (bf16[2,160,384]{2,1,0:T(8,128)(2,1)S(1)}, bf16[2,160,384]{2,1,0:T(8,128)(2,1)S(1)}, u32[]{:S(2)}, u32[]{:S(2)}) collective-permute-start(bf16[2,160,384]{2,1,0:T(8,128)(2,1)S(1)} %get-tuple-element.23), channel_id=1, source_target_pairs={{0,6},{2,0},{4,2},{6,4},{1,7},{3,1},{5,3},{7,5},{8,14},{10,8},{12,... | collective-permute-start | bytes 737288 | tf_op jit(solution)/shard_map/ppermute | solution.py:315
  119.7 15.6 %collective-permute-start.16 = (bf16[2,160,384]{2,1,0:T(8,128)(2,1)S(1)}, bf16[2,160,384]{2,1,0:T(8,128)(2,1)S(1)}, u32[]{:S(2)}, u32[]{:S(2)}) collective-permute-start(bf16[2,160,384]{2,1,0:T(8,128)(2,1)S(1)} %get-tuple-element.25), channel_id=1, source_target_pairs={{0,2},{2,4},{4,6},{6,0},{1,3},{3,5},{5,7},{7,1},{8,10},{10,12},{12... | collective-permute-start | bytes 737288 | tf_op jit(solution)/shard_map/ppermute | solution.py:315
  121.7 13.7 %collective-permute-start.17 = (bf16[2,160,384]{2,1,0:T(8,128)(2,1)S(1)}, bf16[2,160,384]{2,1,0:T(8,128)(2,1)S(1)}, u32[]{:S(2)}, u32[]{:S(2)}) collective-permute-start(bf16[2,160,384]{2,1,0:T(8,128)(2,1)S(1)} %get-tuple-element.24), channel_id=1, source_target_pairs={{0,4},{2,6},{4,0},{6,2},{1,5},{3,7},{5,1},{7,3},{8,12},{10,14},{12... | collective-permute-start | bytes 737288 | tf_op jit(solution)/shard_map/ppermute | solution.py:315
  125.3 18.1 %collective-permute-start.11 = (bf16[160,384]{1,0:T(8,128)(2,1)S(1)}, bf16[160,384]{1,0:T(8,128)(2,1)S(1)}, u32[]{:S(2)}, u32[]{:S(2)}) collective-permute-start(bf16[160,384]{1,0:T(8,128)(2,1)S(1)} %get-tuple-element.26), channel_id=1, source_target_pairs={{0,8},{8,0},{16,264},{24,256},{256,24},{264,16},{272,280},{280,272... | collective-permute-start | bytes 368648 | tf_op jit(solution)/shard_map/ppermute | solution.py:318
  128.9 14.5 %collective-permute-start.12 = (bf16[160,384]{1,0:T(8,128)(2,1)S(1)}, bf16[160,384]{1,0:T(8,128)(2,1)S(1)}, u32[]{:S(2)}, u32[]{:S(2)}) collective-permute-start(bf16[160,384]{1,0:T(8,128)(2,1)S(1)} %get-tuple-element.27), channel_id=1, source_target_pairs={{0,0},{8,8},{16,256},{24,264},{256,16},{264,24},{272,272},{280,280... | collective-permute-start | bytes 368648 | tf_op jit(solution)/shard_map/ppermute | solution.py:318
  135.5 10.9 %collective-permute-start.18 = (bf16[160,384]{1,0:T(8,128)(2,1)S(1)}, bf16[160,384]{1,0:T(8,128)(2,1)S(1)}, u32[]{:S(2)}, u32[]{:S(2)}) collective-permute-start(bf16[160,384]{1,0:T(8,128)(2,1)S(1)} %get-tuple-element.28), channel_id=1, source_target_pairs={{0,264},{8,256},{16,8},{24,0},{256,280},{264,272},{272,24},{280,16... | collective-permute-start | bytes 368648 | tf_op jit(solution)/shard_map/ppermute | solution.py:318
  139.0 10.7 %collective-permute-start.19 = (bf16[160,384]{1,0:T(8,128)(2,1)S(1)}, bf16[160,384]{1,0:T(8,128)(2,1)S(1)}, u32[]{:S(2)}, u32[]{:S(2)}) collective-permute-start(bf16[160,384]{1,0:T(8,128)(2,1)S(1)} %get-tuple-element.29), channel_id=1, source_target_pairs={{0,256},{8,264},{16,0},{24,8},{256,272},{264,280},{272,16},{280,24... | collective-permute-start | bytes 368648 | tf_op jit(solution)/shard_map/ppermute | solution.py:318
Sparse Core Ops, SparseCore 0:
  10.1 66.2 all-gather.4
